TPU v7x, 128 devices: a whole 4x4x4 slice. The times are simulated.
128 devices in a mesh: fsdp: 32 (over x, y_lo, z), tp: 4 (over y_hi, core).
Axes of the slice: x: 4, y: 4 (y_hi: 2, y_lo: 2; y = y_hi * 2 + y_lo), z: 4, core: 2. Of those that a mesh axis runs over, the one named last changes fastest.
Arguments:
- tokens: bfloat16 [16384, 2048], P(('fsdp', 'tp')), may hold values from -6 to 6
- seq_lengths: int32 [32, 4], P('fsdp'), may hold values from 0 to 512, as said below
- norms: float32 [4, 2048], P(None, ('fsdp', 'tp')), may hold values from -1.2 to 2.72, as said below
- w_qkv: bfloat16 [3, 2048, 2048], P(None, 'fsdp', 'tp'), may hold values from -0.125 to 0.125
- qkv_bias: bfloat16 [3, 32, 64], P(None, 'tp', 'fsdp'), may hold values from -2.5 to 2.5
- w_out: bfloat16 [2048, 2048], P('tp', 'fsdp'), may hold values from -0.75 to 0.75
- w_gate_up: bfloat16 [2, 2048, 5632], P(None, 'fsdp', 'tp'), may hold values from -0.125 to 0.125
- w_down: bfloat16 [5632, 2048], P('tp', 'fsdp'), may hold values from -0.078125 to 0.078125
- out_grad: bfloat16 [16384, 2048], P(('fsdp', 'tp')), may hold values from -24 to 24
Outputs:
- layer_out: bfloat16 [16384, 2048], P(('fsdp', 'tp'))
- grad_tokens: bfloat16 [16384, 2048], P(('fsdp', 'tp'))
- grad_norms: float32 [4, 2048], P(None, ('fsdp', 'tp'))
- grad_qkv: float32 [3, 2048, 2048], P(None, 'fsdp', 'tp')
- grad_bias: float32 [3, 32, 64], P(None, 'tp', 'fsdp')
- grad_out_proj: float32 [2048, 2048], P('tp', 'fsdp')
- grad_gate_up: float32 [2, 2048, 5632], P(None, 'fsdp', 'tp')
- grad_down: float32 [5632, 2048], P('tp', 'fsdp')
Inputs may be any that keep to these rules, and one draw needn't show every extreme that they name: `seq_lengths`: in each group the 4 lengths sum to 512; zeros are empty slots. The second sequence of every group starts within the group's first 65 tokens and ends within its last 128; in one group it fills all 512 tokens. `norms`: rows 0 and 2 are positive gains, rows 1 and 3 biases.
All inputs are finite; a program needn't handle non-finite values.
Results may differ from a plain program's by a relative error of at most 0.035.
Values may be sent and summed in bfloat16 or wider, within the bound.
No kernel may reach another device: no remote copies, remote signals or barrier semaphores. Data moves between devices by JAX's collectives and lax.ppermute only.
A program may use at most 192 MiB of HBM per device.

v0:
```python
import math

import jax
import jax.numpy as jnp
from jax import lax
from jax.sharding import PartitionSpec as P

HD = 64
ROT = 16


epsilon = 1e-05


def layer_norm(values, gain, shift):
    centre = jnp.mean(values, axis=-1, keepdims=True)
    centred = values - centre
    spread = jnp.mean(centred * centred, axis=-1, keepdims=True)
    return centred * lax.rsqrt(spread + epsilon) * gain + shift


def rotate(values, cosine, sine):
    half = cosine.shape[-1]
    lower = values[..., :half]
    upper = values[..., half : 2 * half]
    remain = values[..., 2 * half :]
    return jnp.concatenate(
        [lower * cosine - upper * sine, upper * cosine + lower * sine, remain], axis=-1
    )


def sequence_marks(lengths, group):
    ends = jnp.cumsum(lengths)
    places = jnp.arange(group, dtype=jnp.int32)
    segment = jnp.sum((places[:, None] >= ends[None, :]).astype(jnp.int32), axis=1)
    starts = ends - lengths
    slot_ids = jnp.arange(lengths.shape[0], dtype=jnp.int32)
    begin = jnp.sum(jnp.where(slot_ids[None, :] == segment[:, None], starts[None, :], 0), axis=1)
    return (segment, places - begin)


def rotary_tables(position, width):
    steps = jnp.arange(width // 2, dtype=jnp.float32)
    rates = jnp.exp(steps * (-2.0 * math.log(10000.0) / width))
    angles = position.astype(jnp.float32)[:, None] * rates[None, :]
    return (jnp.cos(angles), jnp.sin(angles))


def spread_rows(piece):
    return lax.all_gather(piece, "tp", axis=0, tiled=True)


def branch_rows(term, row_count):
    return lax.psum_scatter(
        term(jnp.int32(0), row_count * lax.axis_size("tp")).astype(jnp.bfloat16),
        "tp",
        scatter_dimension=0,
        tiled=True,
    ).astype(jnp.float32)


def spread_grads(piece):
    return lax.all_gather(piece, "tp", axis=0, tiled=True)


def input_rows(term, row_count):
    return lax.psum_scatter(
        term(jnp.int32(0), row_count * lax.axis_size("tp")).astype(jnp.bfloat16),
        "tp",
        scatter_dimension=0,
        tiled=True,
    ).astype(jnp.float32)


def block_size():
    return 512


def allowed_block(seg_block, place_block, segment, places):
    return (seg_block[:, None] == segment[None, :]) & (places[None, :] <= place_block[:, None])


def attend(query, keys, values, segment, places, scale):
    group, heads, depth = query.shape
    size = block_size()
    count = group // size

    def one_block(items):
        query_block, seg_block, place_block = items
        allowed = allowed_block(seg_block, place_block, segment, places)
        scores = (
            jnp.einsum("qhe,khe->hqk", query_block, keys, preferred_element_type=jnp.float32)
            * scale
        )
        scores = jnp.where(allowed[None], scores, -1e30)
        top_score = jnp.max(scores, axis=2, keepdims=True)
        shifted = jnp.exp(scores - top_score)
        total = jnp.sum(shifted, axis=2, keepdims=True)
        probs = (shifted / total).astype(jnp.bfloat16)
        mixed = jnp.einsum("hqk,khe->qhe", probs, values, preferred_element_type=jnp.float32)
        return (mixed.astype(jnp.bfloat16), top_score + jnp.log(total))

    mixed, log_total = lax.map(
        one_block,
        (
            query.reshape(count, size, heads, depth),
            segment.reshape(count, size),
            places.reshape(count, size),
        ),
    )
    return (mixed.reshape(group, heads * depth), log_total)


def attend_back(query, keys, values, grad_mixed, log_total, segment, places, scale):
    group, heads, depth = query.shape
    size = block_size()
    count = group // size

    def one_block(carry, items):
        grad_keys, grad_values = carry
        query_block, grad_block, total_block, seg_block, place_block = items
        allowed = allowed_block(seg_block, place_block, segment, places)
        scores = (
            jnp.einsum("qhe,khe->hqk", query_block, keys, preferred_element_type=jnp.float32)
            * scale
        )
        scores = jnp.where(allowed[None], scores, -1e30)
        probs = jnp.exp(scores - total_block)
        grad_probs = jnp.einsum(
            "qhe,khe->hqk", grad_block, values, preferred_element_type=jnp.float32
        )
        inner = jnp.sum(grad_probs * probs, axis=2, keepdims=True)
        grad_scores = (probs * (grad_probs - inner)).astype(jnp.bfloat16)
        grad_query = (
            jnp.einsum("hqk,khe->qhe", grad_scores, keys, preferred_element_type=jnp.float32)
            * scale
        )
        grad_keys = (
            grad_keys
            + jnp.einsum(
                "hqk,qhe->khe", grad_scores, query_block, preferred_element_type=jnp.float32
            )
            * scale
        )
        grad_values = grad_values + jnp.einsum(
            "hqk,qhe->khe",
            probs.astype(jnp.bfloat16),
            grad_block,
            preferred_element_type=jnp.float32,
        )
        return ((grad_keys, grad_values), grad_query)

    zeros = jnp.zeros(keys.shape, jnp.float32)
    (grad_keys, grad_values), grad_query = lax.scan(
        one_block,
        (zeros, zeros),
        (
            query.reshape(count, size, heads, depth),
            grad_mixed.reshape(count, size, heads, depth),
            log_total,
            segment.reshape(count, size),
            places.reshape(count, size),
        ),
    )
    return (grad_query.reshape(group, heads, depth), grad_keys, grad_values)


def body(tokens, seq_lengths, norms, w_qkv, qkv_bias, w_out, w_gate_up, w_down, out_grad):
    row_count = tokens.shape[0]
    norm_all = lax.all_gather(norms, ("fsdp", "tp"), axis=1, tiled=True)
    qkv_full, bias_full, out_full = (
        lax.all_gather(w_qkv, "fsdp", axis=1, tiled=True),
        lax.all_gather(qkv_bias, "fsdp", axis=2, tiled=True),
        lax.all_gather(w_out, "fsdp", axis=1, tiled=True),
    )
    gate_full, down_full = (
        lax.all_gather(w_gate_up, "fsdp", axis=1, tiled=True),
        lax.all_gather(w_down, "fsdp", axis=1, tiled=True),
    )
    width = qkv_full.shape[2]
    heads = width // HD
    scale = 1.0 / math.sqrt(HD)
    inputs = tokens.astype(jnp.float32)
    first = spread_rows(layer_norm(inputs, norm_all[0], norm_all[1]).astype(jnp.bfloat16))
    group = first.shape[0]
    segment, position = sequence_marks(seq_lengths[0], group)
    places = jnp.arange(group, dtype=jnp.int32)
    cosine, sine = rotary_tables(position, ROT)
    cosine = cosine[:, None, :]
    sine = sine[:, None, :]
    proj = jnp.einsum("rd,cde->cre", first, qkv_full, preferred_element_type=jnp.float32)
    proj = (proj + bias_full.reshape(3, 1, width).astype(jnp.float32)).reshape(3, group, heads, HD)
    query = rotate(proj[0], cosine, sine).astype(jnp.bfloat16)
    keys = rotate(proj[1], cosine, sine).astype(jnp.bfloat16)
    values = proj[2].astype(jnp.bfloat16)
    mixed, log_total = attend(query, keys, values, segment, places, scale)

    def attn_term(start, count):
        return jnp.dot(mixed, out_full, preferred_element_type=jnp.float32)

    middle = inputs + branch_rows(attn_term, row_count)
    second = spread_rows(layer_norm(middle, norm_all[2], norm_all[3]).astype(jnp.bfloat16))
    gate_up = jnp.einsum("rd,cdf->crf", second, gate_full, preferred_element_type=jnp.float32)
    hidden = (jax.nn.silu(gate_up[0]) * gate_up[1]).astype(jnp.bfloat16)

    def mlp_term(start, count):
        return jnp.dot(hidden, down_full, preferred_element_type=jnp.float32)

    layer_out = (middle + branch_rows(mlp_term, row_count)).astype(jnp.bfloat16)
    qkv_back, out_back = (
        lax.all_gather(w_qkv, "fsdp", axis=1, tiled=True),
        lax.all_gather(w_out, "fsdp", axis=1, tiled=True),
    )
    gate_back, down_back = (
        lax.all_gather(w_gate_up, "fsdp", axis=1, tiled=True),
        lax.all_gather(w_down, "fsdp", axis=1, tiled=True),
    )
    grad_out = out_grad.astype(jnp.float32)
    grad_mlp = spread_grads(out_grad)
    grad_down = jnp.einsum("rf,rd->fd", hidden, grad_mlp, preferred_element_type=jnp.float32)
    grad_hidden = jnp.einsum("rd,fd->rf", grad_mlp, down_back, preferred_element_type=jnp.float32)
    _, pull_gate = jax.vjp(
        lambda gate_in, up_in: jax.nn.silu(gate_in) * up_in, gate_up[0], gate_up[1]
    )
    grad_gate, grad_up = pull_gate(grad_hidden)
    grad_pair = jnp.stack([grad_gate, grad_up]).astype(jnp.bfloat16)
    grad_gate_up = jnp.einsum("rd,crf->cdf", second, grad_pair, preferred_element_type=jnp.float32)

    def mlp_back(start, count):
        return jnp.einsum("crf,cdf->rd", grad_pair, gate_back, preferred_element_type=jnp.float32)

    grad_second = input_rows(mlp_back, row_count)
    _, pull_second = jax.vjp(layer_norm, middle, norm_all[2], norm_all[3])
    grad_mid_part, gain_two, shift_two = pull_second(grad_second)
    grad_middle = grad_out + grad_mid_part
    grad_attn = spread_grads(grad_middle.astype(jnp.bfloat16))
    grad_out_proj = jnp.einsum("rk,rd->kd", mixed, grad_attn, preferred_element_type=jnp.float32)
    grad_mixed = jnp.einsum("rd,kd->rk", grad_attn, out_back, preferred_element_type=jnp.float32)
    grad_mixed = grad_mixed.astype(jnp.bfloat16).reshape(group, heads, HD)
    grad_query, grad_keys, grad_values = attend_back(
        query, keys, values, grad_mixed, log_total, segment, places, scale
    )
    _, pull_rotate = jax.vjp(
        lambda query_in, keys_in: (rotate(query_in, cosine, sine), rotate(keys_in, cosine, sine)),
        proj[0],
        proj[1],
    )
    back_query, back_keys = pull_rotate((grad_query, grad_keys))
    grad_proj = (
        jnp.stack([back_query, back_keys, grad_values])
        .astype(jnp.bfloat16)
        .reshape(3, group, width)
    )
    grad_bias = jnp.sum(grad_proj, axis=1, dtype=jnp.float32).reshape(3, heads, HD)
    grad_qkv = jnp.einsum("rd,cre->cde", first, grad_proj, preferred_element_type=jnp.float32)

    def attn_back(start, count):
        return jnp.einsum("cre,cde->rd", grad_proj, qkv_back, preferred_element_type=jnp.float32)

    grad_first = input_rows(attn_back, row_count)
    _, pull_first = jax.vjp(layer_norm, inputs, norm_all[0], norm_all[1])
    grad_in_part, gain_one, shift_one = pull_first(grad_first)
    grad_tokens = (grad_middle + grad_in_part).astype(jnp.bfloat16)
    summed_qkv, summed_bias, summed_out = (
        lax.psum_scatter(
            grad_qkv.astype(jnp.bfloat16), "fsdp", scatter_dimension=1, tiled=True
        ).astype(jnp.float32),
        lax.psum_scatter(
            grad_bias.astype(jnp.bfloat16), "fsdp", scatter_dimension=2, tiled=True
        ).astype(jnp.float32),
        lax.psum_scatter(
            grad_out_proj.astype(jnp.bfloat16), "fsdp", scatter_dimension=1, tiled=True
        ).astype(jnp.float32),
    )
    summed_gate_up, summed_down = (
        lax.psum_scatter(
            grad_gate_up.astype(jnp.bfloat16), "fsdp", scatter_dimension=1, tiled=True
        ).astype(jnp.float32),
        lax.psum_scatter(
            grad_down.astype(jnp.bfloat16), "fsdp", scatter_dimension=1, tiled=True
        ).astype(jnp.float32),
    )
    summed_norms = lax.psum_scatter(
        jnp.stack([gain_one, shift_one, gain_two, shift_two]),
        ("fsdp", "tp"),
        scatter_dimension=1,
        tiled=True,
    )
    return (
        layer_out,
        grad_tokens,
        summed_norms,
        summed_qkv,
        summed_bias,
        summed_out,
        summed_gate_up,
        summed_down,
    )


def solution(mesh):
    return jax.shard_map(
        body,
        mesh=mesh,
        in_specs=(
            P(("fsdp", "tp"), None),
            P("fsdp", None),
            P(None, ("fsdp", "tp")),
            P(None, "fsdp", "tp"),
            P(None, "tp", "fsdp"),
            P("tp", "fsdp"),
            P(None, "fsdp", "tp"),
            P("tp", "fsdp"),
            P(("fsdp", "tp"), None),
        ),
        out_specs=(
            P(("fsdp", "tp"), None),
            P(("fsdp", "tp"), None),
            P(None, ("fsdp", "tp")),
            P(None, "fsdp", "tp"),
            P(None, "tp", "fsdp"),
            P("tp", "fsdp"),
            P(None, "fsdp", "tp"),
            P("tp", "fsdp"),
        ),
        check_vma=False,
    )
```

profile of v0, /device:TPU:0, one launch (start us, length us, event | category | flops | bytes accessed | tf_op | source)
XLA Modules:
  0.0 2599.3 jit_solution(3153684073367257753)
XLA Ops:
  9.8 179.8 %all-gather = f32[128,16,4]{1,2,0:T(4,128)S(1)} all-gather(f32[1,16,4]{1,2,0:T(4,128)} %bitcast.140), channel_id=1, replica_groups=mesh['fsdp'=32,'tp'=4] {'fsdp','tp'}, dimensions={0}, use_global_device_ids=true | all-gather | bytes 33024 | tf_op jit(solution)/shard_map/all_gather | solution.py:170
  189.9 2.2 fusion.34
  194.1 75.8 %all_gather.37 = bf16[3,8,64]{1,0,2:T(4,128)(2,1)S(1)} all-gather(bf16[3,8,2]{1,0,2:T(4,128)(2,1)S(1)} %copy.79), channel_id=1, replica_groups=mesh['fsdp'=32,'tp'=4] {'fsdp'}, dimensions={2}, use_global_device_ids=true | all-gather | bytes 3168 | tf_op jit(solution)/shard_map/all_gather | solution.py:173
  270.5 106.2 %all-gather.12.cloned.1.call-done = bf16[3,2048,512]{2,1,0:T(8,128)(2,1)} async-done(((bf16[3,64,512]{2,1,0:T(8,128)(2,1)}), bf16[3,2048,512]{2,1,0:T(8,128)(2,1)}) %all-gather.12.cloned.1.call-update) | async-done | bytes 6291472 | tf_op jit(solution)/shard_map/all_gather | solution.py:172
  376.7 6.3 add_bitcast_fusion
  383.5 1.5 fusion.57
  386.3 2.1 copy-done
  388.4 1.6 fusion.25
  390.0 142.1 %all-gather.14.cloned.1.call-done = bf16[512,2048]{0,1:T(8,128)(2,1)} async-done(((bf16[512,64]{0,1:T(8,128)(2,1)}), bf16[512,2048]{0,1:T(8,128)(2,1)}) %all-gather.14.cloned.1.call-update) | async-done | bytes 2097168 | tf_op jit(solution)/shard_map/all_gather | solution.py:174
  532.1 4.3 convolution_convert_fusion.2
  536.5 38.5 %reduce-scatter.10.cloned.1.call-done = bf16[128,2048]{1,0:T(8,128)(2,1)} async-done(((bf16[512,2048]{1,0:T(8,128)(2,1)}), bf16[128,2048]{1,0:T(8,128)(2,1)}) %reduce-scatter.10.cloned.1.call-update) | async-done | bytes 524304 | tf_op jit(solution)/shard_map/reduce_scatter | solution.py:54
  577.6 2.1 add_convert_fusion.4
  582.3 23.6 all-gather.16.cloned.1.call-done
  605.9 175.5 %all-gather.18.cloned.1.call-done = bf16[2,2048,1408]{2,1,0:T(8,128)(2,1)} async-done(((bf16[2,64,1408]{2,1,0:T(8,128)(2,1)}), bf16[2,2048,1408]{2,1,0:T(8,128)(2,1)}) %all-gather.18.cloned.1.call-update) | async-done | bytes 11534352 | tf_op jit(solution)/shard_map/all_gather | solution.py:177
  781.5 12.6 convolution_bitcast_fusion
  794.0 14.2 all-gather.22.cloned.1.call-done
  808.2 163.1 %all-gather.20.cloned.1.call-done = bf16[1408,2048]{0,1:T(8,128)(2,1)} async-done(((bf16[1408,64]{0,1:T(8,128)(2,1)}), bf16[1408,2048]{0,1:T(8,128)(2,1)}) %all-gather.20.cloned.1.call-update) | async-done | bytes 5767184 | tf_op jit(solution)/shard_map/all_gather | solution.py:178
  971.4 10.5 fusion.22
  982.9 7.4 bitcast_convert_fusion.1
  990.4 7.9 convolution_convert_fusion.3
  998.4 30.3 %reduce-scatter.14.cloned.1.call-done = bf16[128,2048]{1,0:T(8,128)(2,1)} async-done(((bf16[512,2048]{1,0:T(8,128)(2,1)}), bf16[128,2048]{1,0:T(8,128)(2,1)}) %reduce-scatter.14.cloned.1.call-update) | async-done | bytes 524304 | tf_op jit(solution)/shard_map/reduce_scatter | solution.py:67
  1028.8 2.2 fusion.38
  1031.5 37.6 %reduce-scatter.12.cloned.1.call-done = bf16[128,2048]{1,0:T(8,128)(2,1)} async-done(((bf16[512,2048]{1,0:T(8,128)(2,1)}), bf16[128,2048]{1,0:T(8,128)(2,1)}) %reduce-scatter.12.cloned.1.call-update) | async-done | bytes 524304 | tf_op jit(solution)/shard_map/reduce_scatter | solution.py:54
  1069.0 2.5 fusion.54
  1073.5 25.2 all-gather.24.cloned.1.call-done
  1098.7 3.5 convolution_convert_fusion.4
  1102.2 5.7 fusion.26
  1108.0 5.4 multiply_reduce_fusion
  1113.5 2.6 multiply_convert_fusion
  1116.1 1.4 fusion.23
  1121.5 2.6 add_convert_fusion.1
  1125.4 2.2 copy.85
  1127.6 7.7 bitcast_convert_fusion
  1135.4 4.4 convolution_convert_fusion.1
  1140.1 7.9 convolution_convert_fusion
  1148.1 11.1 convert_bitcast_fusion
  1159.2 29.0 %copy.92 = bf16[2,2048,1408]{2,0,1:T(2,128)(2,1)} copy(bf16[2,2048,1408]{1,2,0:T(8,128)(2,1)} %convert_bitcast_fusion) | data formatting | bytes 23068672 | tf_op jit(solution)/shard_map/convert_element_type | solution.py:277
  1188.2 1.4 fusion.37
  1189.6 1.6 fusion.39
  1193.0 7.9 convert_bitcast_fusion.1
  1200.9 14.1 copy.89
  1217.6 1.5 fusion.53
  1219.3 157.3 %all-reduce.7 = bf16[3,8,64]{1,0,2:T(4,128)(2,1)S(1)} all-reduce(bf16[3,8,64]{1,0,2:T(4,128)(2,1)S(1)} %copy.90), channel_id=8, replica_groups=mesh['fsdp'=32,'tp'=4] {'fsdp'}, use_global_device_ids=true, to_apply=%region_25.26.clone | all-reduce | flops 1536 | bytes 6144
  1377.2 1.5 convert_element_type.171
  1378.8 131.3 %reduce-scatter.20.cloned.1.call-done = bf16[1408,64]{0,1:T(8,128)(2,1)} async-done(((bf16[1408,2048]{0,1:T(8,128)(2,1)}), bf16[1408,64]{0,1:T(8,128)(2,1)}) %reduce-scatter.20.cloned.1.call-update) | async-done | bytes 180240 | tf_op jit(solution)/shard_map/reduce_scatter | solution.py:279
  1510.0 1.7 convert_element_type.176
  1513.1 633.9 %reduce-scatter.22.cloned.1.call-done = f32[16,4]{1,0:T(8,128)} async-done(((f32[2048,4]{1,0:T(8,128)}), f32[16,4]{1,0:T(8,128)}) %reduce-scatter.22.cloned.1.call-update) | async-done | bytes 272
  2148.3 440.0 %all-reduce.12.cloned.1.call-done = (bf16[3,2048,512]{2,0,1:T(4,128)(2,1)}, bf16[2,2048,1408]{2,0,1:T(2,128)(2,1)}) async-done(((bf16[3,2048,512]{2,0,1:T(4,128)(2,1)}, bf16[2,2048,1408]{2,0,1:T(2,128)(2,1)}), (bf16[3,2048,512]{2,0,1:T(4,128)(2,1)}, bf16[2,2048,1408]{2,0,1:T(2,128)(2,1)})) %all-reduce.12.cloned.1.call-update) | async-done | bytes 17825808
  (181 shorter events, 31.9 us)
Async XLA Ops:
  7.2 186.5 %copy-start.39 = (s32[1,4]{1,0:T(1,128)S(1)}, s32[1,4]{1,0:T(1,128)}, u32[]{:S(2)}) copy-start(s32[1,4]{1,0:T(1,128)} %param.10) | copy-start | bytes 52
  7.2 186.9 %copy-start.35 = (bf16[3,8,2]{1,2,0:T(2,128)(2,1)S(1)}, bf16[3,8,2]{1,2,0:T(2,128)(2,1)}, u32[]{:S(2)}) copy-start(bf16[3,8,2]{1,2,0:T(2,128)(2,1)} %param.13) | copy-start | bytes 292
  7.2 263.3 %all-gather.10.cloned.1.call-start = ((), (), s32[]{:S(2)}) async-start(), calls=%async_computation.7 | async-start | bytes 2621440 | tf_op jit(solution)/shard_map/all_gather | solution.py:50
  8.4 185.6 %copy-start.29 = (f32[128]{0:T(128)}, f32[128]{0:T(128)S(1)}, u32[]{:S(2)}) copy-start(f32[128]{0:T(128)S(1)} %broadcast_multiply_fusion.1) | copy-start | bytes 1540
  9.8 183.9 %copy-start.36 = (f32[128]{0:T(128)}, f32[128]{0:T(128)S(1)}, u32[]{:S(2)}) copy-start(f32[128]{0:T(128)S(1)} %fusion.36) | copy-start | bytes 1540
  9.8 184.1 %copy-start.31 = (f32[128]{0:T(128)}, f32[128]{0:T(128)S(1)}, u32[]{:S(2)}) copy-start(f32[128]{0:T(128)S(1)} %fusion.46) | copy-start | bytes 1540
  189.8 4.2 copy-start.19
  192.1 184.6 %all-gather.12.cloned.1.call-start = ((), (), s32[]{:S(2)}) async-start(), calls=%async_computation.8 | async-start | bytes 6488064 | tf_op jit(solution)/shard_map/all_gather | solution.py:172
  192.9 339.3 %all-gather.14.cloned.1.call-start = ((), (), s32[]{:S(2)}) async-start(), calls=%async_computation.9 | async-start | bytes 2162688 | tf_op jit(solution)/shard_map/all_gather | solution.py:174
  193.6 381.4 %reduce-scatter.10.cloned.1.call-start = ((), (), s32[]{:S(2)}) async-start(), calls=%async_computation.10 | async-start | bytes 2621440 | tf_op jit(solution)/shard_map/reduce_scatter | solution.py:54
  270.2 113.1 %copy-start.21 = (f32[512,8]{0,1:T(8,128)}, f32[512,8]{0,1:T(8,128)S(1)}, u32[]{:S(2)}) copy-start(f32[512,8]{0,1:T(8,128)S(1)} %get-tuple-element.149) | copy-start | bytes 49156
  270.2 113.1 %copy-start.23 = (f32[512,8]{0,1:T(8,128)}, f32[512,8]{0,1:T(8,128)S(1)}, u32[]{:S(2)}) copy-start(f32[512,8]{0,1:T(8,128)S(1)} %get-tuple-element.150) | copy-start | bytes 49156
  385.1 3.3 copy-start
  385.1 3.3 copy-start.25
  386.3 3.6 copy-start.26
  390.0 146.5 %copy-start.40 = (bf16[8,64,512]{2,1,0:T(8,128)(2,1)}, bf16[8,64,512]{2,1,0:T(8,128)(2,1)S(1)}, u32[]{:S(2)}) copy-start(bf16[8,64,512]{2,1,0:T(8,128)(2,1)S(1)} %fusion.25) | copy-start | bytes 1572868
  532.1 42.9 %copy-start.1 = (bf16[128,2048]{1,0:T(8,128)(2,1)S(1)}, bf16[128,2048]{1,0:T(8,128)(2,1)}, u32[]{:S(2)}) copy-start(bf16[128,2048]{1,0:T(8,128)(2,1)} %param.9) | copy-start | bytes 1572868
  536.5 69.5 %all-gather.16.cloned.1.call-start = ((), (), s32[]{:S(2)}) async-start(), calls=%async_computation.11 | async-start | bytes 2621440 | tf_op jit(solution)/shard_map/all_gather | solution.py:50
  579.8 201.7 %all-gather.18.cloned.1.call-start = ((), (), s32[]{:S(2)}) async-start(), calls=%async_computation.12 | async-start | bytes 11894784 | tf_op jit(solution)/shard_map/all_gather | solution.py:177
  580.3 227.9 %all-gather.22.cloned.1.call-start = ((), (), s32[]{:S(2)}) async-start(), calls=%async_computation.15 | async-start | bytes 2621440 | tf_op jit(solution)/shard_map/all_gather | solution.py:63
  581.1 390.3 %all-gather.20.cloned.1.call-start = ((), (), s32[]{:S(2)}) async-start(), calls=%async_computation.13 | async-start | bytes 5947392 | tf_op jit(solution)/shard_map/all_gather | solution.py:178
  581.8 446.9 %reduce-scatter.14.cloned.1.call-start = ((), (), s32[]{:S(2)}) async-start(), calls=%async_computation.16 | async-start | bytes 2621440 | tf_op jit(solution)/shard_map/reduce_scatter | solution.py:67
  971.4 11.6 copy-start.38
  981.8 8.5 copy-start.42
  990.4 78.7 %reduce-scatter.12.cloned.1.call-start = ((), (), s32[]{:S(2)}) async-start(), calls=%async_computation.14 | async-start | bytes 2621440 | tf_op jit(solution)/shard_map/reduce_scatter | solution.py:54
  990.4 38.4 %copy-start.2 = (bf16[128,2048]{1,0:T(8,128)(2,1)S(1)}, bf16[128,2048]{1,0:T(8,128)(2,1)}, u32[]{:S(2)}) copy-start(bf16[128,2048]{1,0:T(8,128)(2,1)} %reduce-scatter.10.cloned.1.call-done) | copy-start | bytes 1572868
  998.4 73.2 %copy-start.3 = (bf16[128,2048]{1,0:T(8,128)(2,1)S(1)}, bf16[128,2048]{1,0:T(8,128)(2,1)}, u32[]{:S(2)}) copy-start(bf16[128,2048]{1,0:T(8,128)(2,1)} %param.17) | copy-start | bytes 1572868
  998.4 100.3 %all-gather.24.cloned.1.call-start = ((), (), s32[]{:S(2)}) async-start(), calls=%async_computation.17 | async-start | bytes 2621440 | tf_op jit(solution)/shard_map/all_gather | solution.py:63
  1072.5 115.6 %reduce-scatter.16.cloned.1.call-start = ((), (), s32[]{:S(2)}) async-start(), calls=%async_computation.18 | async-start | bytes 2621440 | tf_op jit(solution)/shard_map/reduce_scatter | solution.py:67
  1102.2 11.2 slice-start
  1108.0 5.4 slice-start.1
  1113.4 2.6 copy-start.10
  1113.5 2.6 copy-start.16
  1113.5 2.6 copy-start.18
  1121.5 71.5 %copy-start.6 = (bf16[1,512,512]{2,1,0:T(8,128)(2,1)}, bf16[1,512,512]{2,1,0:T(8,128)(2,1)S(1)}, u32[]{:S(2)}) copy-start(bf16[1,512,512]{2,1,0:T(8,128)(2,1)S(1)} %copy.87) | copy-start | bytes 1572868
  1125.3 67.6 %copy-start.8 = (bf16[1,512,512]{2,1,0:T(8,128)(2,1)}, bf16[1,512,512]{2,1,0:T(8,128)(2,1)S(1)}, u32[]{:S(2)}) copy-start(bf16[1,512,512]{2,1,0:T(8,128)(2,1)S(1)} %copy.86) | copy-start | bytes 1572868
  1135.3 241.9 %reduce-scatter.18.cloned.1.call-start = ((), (), s32[]{:S(2)}) async-start(), calls=%async_computation.19 | async-start | bytes 2162688 | tf_op jit(solution)/shard_map/reduce_scatter | solution.py:271
  1139.8 370.3 %reduce-scatter.20.cloned.1.call-start = ((), (), s32[]{:S(2)}) async-start(), calls=%async_computation.20 | async-start | bytes 5947392 | tf_op jit(solution)/shard_map/reduce_scatter | solution.py:279
  1148.0 998.9 %reduce-scatter.22.cloned.1.call-start = ((), (), s32[]{:S(2)}) async-start(), calls=%async_computation.21 | async-start | bytes 1056768
  1159.2 29.0 %copy-start.20 = (f32[1,2048]{1,0:T(1,128)S(1)}, f32[1,2048]{1,0:T(1,128)}, u32[]{:S(2)}) copy-start(f32[1,2048]{1,0:T(1,128)} %copy-done.19) | copy-start | bytes 24580
  1159.2 29.0 %copy-start.30 = (f32[128]{0:T(128)S(1)}, f32[128]{0:T(128)}, u32[]{:S(2)}) copy-start(f32[128]{0:T(128)} %copy-done.29) | copy-start | bytes 1540
  1159.2 30.4 %copy-start.37 = (f32[128]{0:T(128)S(1)}, f32[128]{0:T(128)}, u32[]{:S(2)}) copy-start(f32[128]{0:T(128)} %copy-done.36) | copy-start | bytes 1540
  1159.2 30.4 %copy-start.32 = (f32[128]{0:T(128)S(1)}, f32[128]{0:T(128)}, u32[]{:S(2)}) copy-start(f32[128]{0:T(128)} %copy-done.31) | copy-start | bytes 1540
  1159.2 32.0 %copy-start.27 = (f32[2048]{0:T(1024)S(1)}, f32[2048]{0:T(1024)}, u32[]{:S(2)}) copy-start(f32[2048]{0:T(1024)} %get-tuple-element.117) | copy-start | bytes 24580
  1159.2 32.0 %copy-start.28 = (f32[2048]{0:T(1024)S(1)}, f32[2048]{0:T(1024)}, u32[]{:S(2)}) copy-start(f32[2048]{0:T(1024)} %get-tuple-element.122) | copy-start | bytes 24580
  1192.6 1395.7 %all-reduce.12.cloned.1.call-start = ((), (), s32[]{:S(2)}) async-start(), calls=%async_computation.22 | async-start | bytes 39845888
  1215.0 296.7 %copy-start.34 = (f32[128]{0:T(128)S(1)}, f32[128]{0:T(128)}, u32[]{:S(2)}) copy-start(f32[128]{0:T(128)} %copy-done.33) | copy-start | bytes 1540
  1215.1 296.7 %copy-start.4 = (bf16[128,2048]{1,0:T(8,128)(2,1)S(1)}, bf16[128,2048]{1,0:T(8,128)(2,1)}, u32[]{:S(2)}) copy-start(bf16[128,2048]{1,0:T(8,128)(2,1)} %reduce-scatter.16.cloned.1.call-done) | copy-start | bytes 1572868
  (15 other events, 22.3 us)
Sparse Core Ops, SparseCore 0:
  192.2 20.3 all-gather.9
  214.2 162.4 all-gather.11
  378.4 153.7 all-gather.13
  536.6 38.3 reduce-scatter.9
  579.9 26.0 all-gather.15
  607.5 173.8 all-gather.17
  783.2 24.9 all-gather.21
  810.0 161.3 all-gather.19
  990.5 38.2 reduce-scatter.13
  1031.3 37.7 reduce-scatter.11
  1072.7 26.0 all-gather.23
  1135.5 37.7 reduce-scatter.15
  1175.6 162.9 reduce-scatter.17
  1340.9 169.0 reduce-scatter.19
  1512.4 634.5 reduce-scatter.21
  2149.4 438.8 all-reduce.11
where the time goes:
time: 2610 us; the launch traced here: 2600 us
  waiting for transfers between devices  1970 us (75%)
  blocking collectives  413 us (16%)
  matrix products  108 us (4%)
  local copies, waits for them, and re-layouts  59.4 us (2%)
  other arithmetic  35.7 us (1%)
    unnamed x18, waiting for transfers between devices  1080 us
    all_gather x1, blocking collectives, body(): norm_all = lax.all_gather(norms, ('fsdp', 'tp'), axis=1, tiled=True)  180 us
    all_gather x1, waiting for transfers between devices, body(): lax.all_gather(w_gate_up, 'fsdp', axis=1, tiled=True)  176 us
    all_gather x1, waiting for transfers between devices, body(): lax.all_gather(w_down, 'fsdp', axis=1, tiled=True)  163 us
    unnamed x1, blocking collectives  157 us
    all_gather x1, waiting for transfers between devices, body(): lax.all_gather(w_out, 'fsdp', axis=1, tiled=True)  142 us
    reduce_scatter x1, waiting for transfers between devices, body(): lax.psum_scatter(grad_down.astype(jnp.bfloat16), 'fsdp', scatter_dimensio...  131 us
    all_gather x1, waiting for transfers between devices, body(): lax.all_gather(w_qkv, 'fsdp', axis=1, tiled=True)  106 us
  transfers between devices with their start and end apart: 16, of which 13 were waited for; matrix products, arithmetic and copies ran while one was open for 5% of the time, Pallas kernels for 0%

commit v1 on v0

v1 whole, which is shorter than its diff:
```python
import math

import jax
import jax.numpy as jnp
from jax import lax
from jax.experimental import pallas as pl
from jax.experimental.pallas import tpu as pltpu
from jax.sharding import Mesh, PartitionSpec as P

HD = 64
ROT = 16
EPS = 1e-05
ROWS = 128
FSDP = ("x", "core", "z")
ALL = ("x", "yl", "z", "yh", "core")
BF = jnp.bfloat16
F32 = jnp.float32


def swap(v):
    return lax.ppermute(v, ("yl", "core"), [(0, 0), (1, 2), (2, 1), (3, 3)])


def ring_index(y):
    return (y % 2) * 2 + (y // 2) % 2


def shift(v, k):
    return lax.ppermute(v, ("yl", "yh"), [(ring_index(y), ring_index((y + k) % 4)) for y in range(4)])


def spread_pairs(k):
    pairs = []
    for g in range(2):
        for yh in range(2):
            for c in range(2):
                y = (2 * yh + c + k) % 4
                pairs.append((g * 4 + yh * 2 + c, (y % 2) * 4 + (y // 2) * 2 + g))
    return pairs


def spread(v, k):
    return lax.ppermute(v, ("yl", "yh", "core"), spread_pairs(k))


def collect(v, k):
    return lax.ppermute(v, ("yl", "yh", "core"), [(b, a) for a, b in spread_pairs(k)])


def gather_rows(piece, name):
    with jax.named_scope(name):
        return [piece] + [shift(piece, k) for k in (1, 2, 3)]


def spread_rows(piece, name):
    with jax.named_scope(name):
        return [spread(piece, k) for k in range(4)]


def scatter_rows(blocks, name):
    with jax.named_scope(name):
        return [blocks[0]] + [shift(blocks[k], -k) for k in (2, 1, 3)]


def collect_rows(blocks, name):
    with jax.named_scope(name):
        return [collect(blocks[k], k) for k in (2, 1, 3, 0)]


def call(kernel, args, outs, deps=(), limit=60, grid=None, specs=None, out_specs=None, scratch=()):
    n, m = len(args), len(deps)
    whole = pl.BlockSpec(memory_space=pltpu.VMEM)
    return pl.pallas_call(
        lambda *refs: kernel(*refs[:n], *refs[n + m :]),
        name=kernel.__name__,
        **({} if grid is None else {"grid": grid}),
        in_specs=list(specs or [whole] * n) + [pl.BlockSpec(memory_space=pl.ANY)] * m,
        out_specs=list(out_specs or [whole] * len(outs)),
        out_shape=[jax.ShapeDtypeStruct(s, t) for s, t in outs],
        scratch_shapes=list(scratch),
        compiler_params=pltpu.CompilerParams(vmem_limit_bytes=limit << 20),
    )(*args, *deps)


def hold(arrays, deps):
    n, m = len(arrays), len(deps)
    return pl.pallas_call(
        lambda *refs: None,
        name="hold",
        in_specs=[pl.BlockSpec(memory_space=pl.ANY)] * (n + m),
        out_specs=[pl.BlockSpec(memory_space=pl.ANY)] * n,
        out_shape=[jax.ShapeDtypeStruct(v.shape, v.dtype) for v in arrays],
        input_output_aliases={i: i for i in range(n)},
    )(*arrays, *deps)


MM = (((1,), (0,)), ((), ()))
MT = (((1,), (1,)), ((), ()))
TM = (((0,), (0,)), ((), ()))


def mul(a, b, dims):
    return lax.dot_general(a, b, dims, preferred_element_type=F32)


def total(refs):
    value = refs[0][...].astype(F32)
    for ref in refs[1:]:
        value = value + ref[...].astype(F32)
    return value


def normal_kernel(tokens, n):
    n[...] = normal(tokens[...].astype(F32))[0].astype(BF)


def middle_kernel(tokens, norms, *refs):
    middle = tokens[...].astype(F32) + total(refs[:4])
    refs[4][...] = middle
    refs[6][...] = middle.astype(BF)
    refs[5][...] = (normal(middle)[0] * norms[2:3] + norms[3:4]).astype(BF)


def back_kernel(middle, norms, grad, *refs):
    n, r = normal(middle[...])
    part = total(refs[:4])
    value = grad[...].astype(F32) + normal_back(n, r, part * norms[2:3])
    refs[4][...] = value.astype(BF)
    refs[5][0:1] = jnp.sum(part * n, axis=0, keepdims=True)
    refs[5][1:2] = jnp.sum(part, axis=0, keepdims=True)


def tokens_kernel(tokens, norms, grad, *refs):
    n, r = normal(tokens[...].astype(F32))
    refs[4][...] = (grad[...].astype(F32) + normal_back(n, r, total(refs[:4]) * norms[0:1])).astype(BF)


def last_kernel(middle, *refs):
    refs[4][...] = (middle[...].astype(F32) + total(refs[:4])).astype(BF)


def block_shapes(own=F32):
    return [((ROWS, 2048), own)] + [((ROWS, 2048), BF)] * 3


def store_blocks(value, refs, columns):
    for j in range(4):
        refs[j][:, columns] = value[j * ROWS : (j + 1) * ROWS].astype(refs[j].dtype)


def mask_of(begin, place, row):
    return jnp.where((row[...] >= begin[...]) & (row[...] <= place[...]), 0.0, -1e30).astype(F32)


def lane_of(width):
    return lax.broadcasted_iota(jnp.int32, (1, width), 1)


def turn(v, tables, sign):
    straight, ahead, behind = tables
    return v * straight[...] + sign * (pltpu.roll(v, 120, 1) * ahead[...] + pltpu.roll(v, 8, 1) * behind[...])


def attend_kernel(n0, n1, n2, n3, norms, wq, wk, wv, wo, bias, straight, ahead, behind, begin, place, row, *refs):
    first, query, keys, values, logs, mixed, t0, t1, t2, t3, mask = refs
    step = pl.program_id(0)

    @pl.when(step == 0)
    def _():
        for j, n in enumerate((n0, n1, n2, n3)):
            first[j * ROWS : (j + 1) * ROWS] = (n[...].astype(F32) * norms[0:1] + norms[1:2]).astype(BF)
        mask[...] = mask_of(begin, place, row)
        logs[...] = jnp.zeros_like(logs)

    tables = (straight, ahead, behind)
    q4 = mul(first[...], wq[...], MM) + bias[0, pl.ds(step, 1)]
    k4 = mul(first[...], wk[...], MM) + bias[1, pl.ds(step, 1)]
    v4 = (mul(first[...], wv[...], MM) + bias[2, pl.ds(step, 1)]).astype(BF)
    lane = lane_of(128)
    for pair in range(2):
        at = slice(pair * 128, (pair + 1) * 128)
        columns = pl.ds(pl.multiple_of(step * 256 + pair * 128, 128), 128)
        q = (turn(q4[:, at], tables, 1.0).astype(BF) * BF(1.0 / math.sqrt(HD))).astype(BF)
        k = turn(k4[:, at], tables, 1.0).astype(BF)
        v = v4[:, at]
        query[:, columns] = q
        keys[:, columns] = k
        values[:, columns] = v
        result = None
        for head in range(2):
            own = (lane >= 64) if head else (lane < 64)
            scores = mul(jnp.where(own, q, BF(0)), k, MT) + mask[...]
            top = jnp.max(scores, axis=1, keepdims=True)
            shifted = jnp.exp(scores - top)
            whole = jnp.sum(shifted, axis=1, keepdims=True)
            probs = (shifted * (1.0 / whole)).astype(BF)
            out = mul(probs, v, MM)
            result = out if result is None else jnp.where(own, out, result)
            logs[...] = jnp.where(lane == step * 4 + pair * 2 + head, top + jnp.log(whole), logs[...])
        mixed[:, columns] = result.astype(BF)

    @pl.when(step == 1)
    def _():
        for i in range(4):
            columns = slice(i * 512, (i + 1) * 512)
            store_blocks(mul(mixed[...], wo[columns], MT), (t0, t1, t2, t3), columns)


def attend_back_kernel(g0, g1, g2, g3, wo, query, keys, values, logs, straight, ahead, behind, begin, place, row, *refs):
    grad_proj, grad_bias, mask, grad_mixed = refs
    step = pl.program_id(0)

    @pl.when(step == 0)
    def _():
        for j, g in enumerate((g0, g1, g2, g3)):
            grad_mixed[j * ROWS : (j + 1) * ROWS] = mul(g[...], wo[...], MM).astype(BF)
        mask[...] = mask_of(begin, place, row)

    tables = (straight, ahead, behind)
    lane = lane_of(128)
    columns = pl.ds(pl.multiple_of(step * 128, 128), 128)
    q, k, v, g = query[...], keys[...], values[...], grad_mixed[:, columns]
    grad_q = grad_k = grad_v = 0.0
    for head in range(2):
        own = (lane >= 64) if head else (lane < 64)
        q1, k1, g1 = (jnp.where(own, w, BF(0)) for w in (q, k, g))
        log = jnp.sum(jnp.where(lane == step * 2 + head, logs[...], 0.0), axis=1, keepdims=True)
        probs = jnp.exp(mul(q1, k, MT) + mask[...] - log)
        grad_probs = mul(g1, v, MT)
        inner = jnp.sum(grad_probs * probs, axis=1, keepdims=True)
        grad_scores = (probs * (grad_probs - inner)).astype(BF)
        grad_q = grad_q + mul(grad_scores, k1, MM)
        grad_k = grad_k + mul(grad_scores, q1, TM)
        grad_v = grad_v + mul(probs.astype(BF), g1, TM)
    for c, value in enumerate(
        (turn(grad_q * (1.0 / math.sqrt(HD)), tables, -1.0), turn(grad_k, tables, -1.0), grad_v)
    ):
        low = value.astype(BF)
        at = pl.ds(pl.multiple_of(c * 512 + step * 128, 128), 128)
        grad_proj[:, at] = low
        sums = jnp.sum(low.astype(F32), axis=0, keepdims=True)
        grad_bias[pl.ds(c * 8 + 2 * step, 1)] = sums[:, :HD]
        grad_bias[pl.ds(c * 8 + 2 * step + 1, 1)] = sums[:, HD:]


def feed_kernel(*refs):
    second, grads, w, (hidden, pair, t0, t1, t2, t3, held, sems) = refs[:4], refs[4:8], refs[8], refs[9:]
    cuts = [(i * 256, 256) for i in range(5)] + [(1280, 128)]
    copies = []
    for i, (f, width) in enumerate(cuts):
        for c, at, size in ((0, 2 * f, 2 * width), (1, 2816 + f, width)):
            copy = pltpu.make_async_copy(w.at[:, at : at + size], held.at[:, at : at + size], sems.at[i, c])
            copy.start()
            copies.append(copy)
    for i, (f, width) in enumerate(cuts):
        copies[2 * i].wait()
        copies[2 * i + 1].wait()
        for j in range(2):
            rows = slice(j * 256, (j + 1) * 256)
            lhs = jnp.concatenate([second[2 * j][...], second[2 * j + 1][...]], axis=0)
            both = mul(lhs, held[:, 2 * f : 2 * (f + width)], MM)
            lhs = jnp.concatenate([grads[2 * j][...], grads[2 * j + 1][...]], axis=0)
            back = mul(lhs, held[:, 2816 + f : 2816 + f + width], MM)
            for b in range(width // 128):
                gate, up = both[:, b * 256 : b * 256 + 128], both[:, b * 256 + 128 : b * 256 + 256]
                grad = back[:, b * 128 : (b + 1) * 128]
                sig = jax.nn.sigmoid(gate)
                silu = gate * sig
                at = f + b * 128
                hidden[rows, at : at + 128] = (silu * up).astype(BF)
                pair[rows, 2 * at : 2 * at + 128] = (grad * up * (sig + silu * (1.0 - sig))).astype(BF)
                pair[rows, 2 * at + 128 : 2 * at + 256] = (grad * silu).astype(BF)
    for i in range(4):
        columns = slice(i * 512, (i + 1) * 512)
        store_blocks(mul(pair[...], held[columns, :2816], MT), (t0, t1, t2, t3), columns)


def outer_kernel(a0, a1, a2, a3, b, c0, c1, c2, c3, d, out):
    n, m = b.shape[1], d.shape[1]
    a = jnp.concatenate([a0[...], a1[...], a2[...], a3[...]], axis=0)
    c = jnp.concatenate([c0[...], c1[...], c2[...], c3[...]], axis=0)
    out[:, :n] = mul(a, b[...], TM).astype(BF)
    out[:, n : n + m] = mul(c, d[...], TM).astype(BF)


def outer(a, b, c, d, deps=(), tile=256):
    n, m = b.shape[1], d.shape[1]
    left = [pl.BlockSpec((ROWS, tile), lambda i: (0, i))] * 4
    whole = lambda w: pl.BlockSpec((512, w), lambda i: (0, 0))
    return call(
        outer_kernel,
        (*a, b, *c, d),
        [((2048, n + m), BF)],
        deps,
        grid=(2048 // tile,),
        specs=left + [whole(n)] + left + [whole(m)],
        out_specs=[pl.BlockSpec((tile, n + m), lambda i: (i, 0))],
    )[0]


def half_columns(a, b, c, d, extra):
    n, m = b.shape[1], d.shape[1]
    rows = jnp.concatenate([ref[...] for ref in c], axis=0)
    return ((0, n, mul(a[...], b[...], TM)), (n, m, mul(rows, d[...], TM)), (n + m, extra.shape[1], extra[...].astype(F32)))


def their_half_kernel(place, a, b, c0, c1, c2, c3, d, extra, out):
    for begin, width, value in half_columns(a, b, (c0, c1, c2, c3), d, extra):
        out[:, begin : begin + width] = value.astype(BF)


def own_half_kernel(place, a, b, c0, c1, c2, c3, d, extra, theirs, one, two):
    split = one.shape[-1]
    for begin, width, value in half_columns(a, b, (c0, c1, c2, c3), d, extra):
        value = (value + theirs[:, begin : begin + width].astype(F32)).astype(BF)
        for z in range(4):
            at = lax.rem(z - place[2] + 4, 4)
            rows = value[z * 64 : (z + 1) * 64]
            if begin < split:
                one[0, at] = rows[:, :split]
                two[at, 0, :, : width - split] = rows[:, split:]
            else:
                two[at, 0, :, begin - split : begin - split + width] = rows


def outer_half(place, a, b, c, d, extra, split, deps, theirs=None):
    rows = a.shape[0]
    n, m, e = b.shape[1], d.shape[1], extra.shape[1]
    wide = n + m + e
    pick = lambda i, p: 2 * lax.rem(p[1] + i, 4) + p[0]
    left = pl.BlockSpec((rows, 256), lambda i, p: (0, pick(i, p)))
    quarter = [pl.BlockSpec((ROWS, 256), lambda i, p: (0, pick(i, p)))] * 4
    whole = lambda w: pl.BlockSpec((rows, w), lambda i, p: (0, 0))
    flat = pl.BlockSpec((256, wide), lambda i, p: (i, 0))
    specs = [left, whole(n), *quarter, whole(m), pl.BlockSpec((256, e), lambda i, p: (pick(i, p), 0))]
    if theirs is None:
        kernel, args, outs, shapes = their_half_kernel, [], [flat], [(1024, wide)]
    else:
        kernel, args, specs = own_half_kernel, [theirs], specs + [flat]
        outs = [
            pl.BlockSpec((1, 4, 64, split), lambda i, p: (i, 0, 0, 0)),
            pl.BlockSpec((4, 1, 64, wide - split), lambda i, p: (0, i, 0, 0)),
        ]
        shapes = [(4, 4, 64, split), (4, 4, 64, wide - split)]
    count = 1 + len(specs)
    return pl.pallas_call(
        lambda *refs: kernel(*refs[:count], *refs[count + len(deps) :]),
        name=kernel.__name__,
        grid_spec=pltpu.PrefetchScalarGridSpec(
            num_scalar_prefetch=1,
            grid=(4,),
            in_specs=specs + [pl.BlockSpec(memory_space=pl.ANY)] * len(deps),
            out_specs=outs,
        ),
        out_shape=[jax.ShapeDtypeStruct(shape, BF) for shape in shapes],
        compiler_params=pltpu.CompilerParams(vmem_limit_bytes=60 << 20),
    )(place, a, b, *c, d, extra, *args, *deps)


def term_kernel(a, w, *refs):
    value = mul(a[...], w[...], MT)
    if len(refs) > 4:
        *n, norm_two, grad_bias, t0, t1, t2, t3, tail = refs
        refs = (t0, t1, t2, t3)
        gain = jnp.zeros((1, value.shape[1]), F32)
        for j in range(4):
            gain = gain + jnp.sum(value[j * ROWS : (j + 1) * ROWS] * n[j][...].astype(F32), axis=0, keepdims=True)
        rows = jnp.concatenate([gain, jnp.sum(value, axis=0, keepdims=True), norm_two[...], jnp.zeros_like(norm_two), jnp.zeros_like(norm_two)], axis=0)
        step = pl.program_id(0)
        bias = jnp.zeros((24, 128), F32)
        lane = lane_of(HD)
        for f in range(8):
            ones = [jnp.sum(jnp.where(lane == 2 * (step * 8 + f) + j, grad_bias[...], 0.0), axis=1, keepdims=True) for j in (0, 1)]
            bias = jnp.concatenate(ones + [jnp.zeros((24, 126), F32)], axis=1)
            tail[f * 64 : (f + 1) * 64] = jnp.concatenate(
                [
                    jnp.concatenate([rows[:, f * 64 : (f + 1) * 64], jnp.zeros((8, 64), F32)], axis=1),
                    bias,
                    jnp.zeros((32, 128), F32),
                ],
                axis=0,
            ).astype(BF)
    for j in range(4):
        refs[j][...] = value[j * ROWS : (j + 1) * ROWS].astype(refs[j].dtype)


def row_term(a, w, at, n=None, norm_two=None, grad_bias=None, deps=(), own=BF, tile=512):
    rows, depth = a.shape
    block = pl.BlockSpec((ROWS, tile), lambda i: (0, i))
    args = [a, w]
    specs = [pl.BlockSpec((rows, depth), lambda i: (0, 0)), pl.BlockSpec((tile, depth), lambda i: (i, at))]
    shapes, outs = block_shapes(own), [block] * 4
    if n is not None:
        args += [*n, norm_two, grad_bias]
        specs += [block] * 4 + [pl.BlockSpec((2, tile), lambda i: (0, i)), pl.BlockSpec((24, HD), lambda i: (0, 0))]
        shapes = shapes + [((2048, 128), BF)]
        outs = outs + [pl.BlockSpec((tile, 128), lambda i: (i, 0))]
    return call(term_kernel, args, shapes, deps, grid=(2048 // tile,), specs=specs, out_specs=outs)


def along(v, axis, k):
    return lax.ppermute(v, axis, [(i, (i + k) % 4) for i in range(4)])


def sum_along(blocks, axis, name):
    with jax.named_scope(name):
        got = [along(blocks[k], axis, k) for k in (2, 1, 3)]
    return blocks[0].astype(F32) + got[0].astype(F32) + got[1].astype(F32) + got[2].astype(F32)


def normal(v):
    centred = v - jnp.mean(v, axis=-1, keepdims=True)
    r = lax.rsqrt(jnp.mean(centred * centred, axis=-1, keepdims=True) + EPS)
    return centred * r, r


def normal_back(n, r, t):
    return r * (t - jnp.mean(t, axis=-1, keepdims=True) - n * jnp.mean(t * n, axis=-1, keepdims=True))


def across(v):
    return lax.ppermute(v, "core", [(0, 1), (1, 0)])


def body(tokens, seq_lengths, norms, w_qkv, qkv_bias, w_out, w_gate_up, w_down, out_grad):
    me = 2 * lax.axis_index("yh") + lax.axis_index("yl")
    small = jnp.concatenate(
        [
            norms,
            qkv_bias.astype(F32).reshape(3, 16),
            jnp.pad(seq_lengths.astype(F32), ((0, 0), (0, 12))),
        ],
        axis=0,
    )
    row_shape = [((ROWS, 2048), BF)]
    w_attn = swap(jnp.concatenate([w_qkv[0], w_qkv[1], w_qkv[2], w_out.T], axis=1))
    n_own = call(normal_kernel, (tokens,), row_shape)[0]
    pieces = [spread(small, k) for k in range(4)]
    lengths = pieces[0][7, :4].astype(jnp.int32)
    bias_row = pieces[0][4:7].reshape(1, 48)
    turned = jnp.stack([p[:4] for p in pieces[::-1]] * 2)
    ordered = lax.dynamic_slice_in_dim(turned, 3 - me, 4, axis=0)
    norm_part = ordered.transpose(1, 0, 2).reshape(4, 64)
    high = norm_part.astype(BF)
    rest = norm_part - high.astype(F32)
    middle_part = rest.astype(BF)
    low = (rest - middle_part.astype(F32)).astype(BF)
    extra = jnp.concatenate([high, middle_part, low, jnp.pad(bias_row.astype(BF), ((0, 0), (0, 16)))], axis=0)
    extra = jnp.pad(extra, ((0, 64 - 13), (0, 64)))
    (extra,) = hold([extra], (n_own,))
    attn_full = lax.all_gather(jnp.concatenate([w_attn, extra], axis=1), FSDP, axis=0, tiled=True)

    n_rows = spread_rows(n_own, "n_rows")
    w_ffn = swap(
        jnp.concatenate([w_gate_up.reshape(2, 64, 11, 128).transpose(1, 2, 0, 3).reshape(64, 2816), w_down.T], axis=1)
    )
    inputs = swap(tokens)
    mlp_rows = spread_rows(out_grad, "grad_rows")
    ffn_full = lax.all_gather(w_ffn, FSDP, axis=0, tiled=True)

    extras = attn_full[:, 2048:].reshape(32, 64, 128)
    norm_all = extras[:, :12, :64].astype(F32).reshape(32, 3, 4, 64).sum(axis=1)
    norm_all = norm_all.transpose(1, 0, 2).reshape(4, 2048)
    bias = extras[:, 12, :48].astype(F32).reshape(32, 3, 8, 2).transpose(1, 2, 0, 3).reshape(3, 2, 256)

    places = (((me - jnp.arange(4, dtype=jnp.int32)) % 4) * ROWS)[:, None] + jnp.arange(ROWS, dtype=jnp.int32)
    places = places.reshape(512)
    ends = jnp.cumsum(lengths)
    segment = jnp.sum((places[:, None] >= ends[None, :]).astype(jnp.int32), axis=1)
    begin = jnp.sum(
        jnp.where(jnp.arange(4, dtype=jnp.int32)[None, :] == segment[:, None], (ends - lengths)[None, :], 0), axis=1
    )
    position = places - begin
    rates = jnp.exp(jnp.arange(ROT // 2, dtype=F32) * (-2.0 * math.log(10000.0) / ROT))
    angles = position.astype(F32)[:, None] * rates[None, :]
    cosine, sine = jnp.cos(angles), jnp.sin(angles)
    zero, one = jnp.zeros((512, 8), F32), jnp.ones((512, 48), F32)
    still = jnp.zeros((512, 48), F32)
    tables = (
        jnp.concatenate([cosine, cosine, one] * 2, axis=1),
        jnp.concatenate([-sine, zero, still] * 2, axis=1),
        jnp.concatenate([zero, sine, still] * 2, axis=1),
    )
    marks = (begin[:, None], places[:, None], places[None, :])

    sticky = lambda *shape: pl.BlockSpec(shape, lambda i: (0,) * len(shape))
    part = lambda first: pl.BlockSpec((2048, 256), lambda i: (0, first + i))
    table_specs = [sticky(512, 128)] * 3 + [sticky(512, 1)] * 2 + [sticky(1, 512)]
    first, query, keys, values, logs, mixed, *term = call(
        attend_kernel,
        (*n_rows, norm_all, *[attn_full] * 4, bias, *tables, *marks),
        [((512, 2048), BF)] + [((512, 512), BF)] * 3 + [((512, 128), F32), ((512, 512), BF)] + block_shapes(),
        (w_ffn, inputs),
        grid=(2,),
        specs=[sticky(ROWS, 2048)] * 4
        + [sticky(4, 2048), part(0), part(2), part(4), pl.BlockSpec((2048, 512), lambda i: (0, 3)), sticky(3, 2, 256)]
        + table_specs,
        out_specs=[sticky(512, 2048)]
        + [sticky(512, 512)] * 3
        + [sticky(512, 128), sticky(512, 512)]
        + [sticky(ROWS, 2048)] * 4,
        scratch=[pltpu.VMEM((512, 512), F32)],
    )
    term = hold(term, mlp_rows)
    middle, second, middle_low = call(
        middle_kernel, (inputs, norm_all, *scatter_rows(term, "attn_sum")), [((ROWS, 2048), F32)] + row_shape * 2
    )
    second = gather_rows(second, "second_rows")
    middle_low = swap(hold([middle_low], second)[0])
    hidden, grad_pair, *term = call(
        feed_kernel,
        (*second, *mlp_rows, ffn_full),
        [((512, 1408), BF), ((512, 2816), BF)] + block_shapes(),
        specs=[pl.BlockSpec(memory_space=pltpu.VMEM)] * 8 + [pl.BlockSpec(memory_space=pl.ANY)],
        scratch=[pltpu.VMEM((2048, 4224), BF), pltpu.SemaphoreType.DMA((6, 2))],
    )
    term = scatter_rows(term, "second_sum")
    grad_ffn = outer(second, grad_pair, mlp_rows, hidden)
    last_term = row_term(hidden, ffn_full, 2, deps=(grad_ffn,))
    grad_rows, norm_two = call(
        back_kernel,
        (middle, norm_all, mlp_rows[0], *term),
        row_shape + [((2, 2048), F32)],
        (last_term[0],),
    )
    (grad_ffn,) = hold([grad_ffn], (grad_rows,))
    ffn_sum = swap(lax.psum_scatter(grad_ffn, FSDP, scatter_dimension=0, tiled=True)).astype(F32)
    attn_rows = gather_rows(grad_rows, "middle_rows")
    *last_term, grad_middle = hold([*last_term, grad_rows], attn_rows[1:])
    last_term = collect_rows(last_term, "out_sum")
    grad_middle = swap(grad_middle)
    column = pl.BlockSpec((512, 128), lambda i: (0, i))
    grad_proj, grad_bias = call(
        attend_back_kernel,
        (*attn_rows, attn_full, query, keys, values, logs, *tables, *marks),
        [((512, 1536), BF), ((24, HD), F32)],
        grid=(4,),
        specs=[sticky(ROWS, 2048)] * 4
        + [pl.BlockSpec((2048, 512), lambda i: (0, 3)), column, column, column, sticky(512, 128)]
        + table_specs,
        out_specs=[sticky(512, 1536), sticky(24, HD)],
        scratch=[pltpu.VMEM((512, 512), F32), pltpu.VMEM((512, 512), BF)],
    )

    place = jnp.stack([lax.axis_index("core"), lax.axis_index("x"), lax.axis_index("z")]).astype(jnp.int32)
    *term, tail = row_term(grad_proj, attn_full, 0, n_rows, norm_two, grad_bias)
    first_term = collect_rows(hold(term, last_term), "first_sum")
    place_other = place * jnp.array([-1, 1, 1]) + jnp.array([1, 0, 0])
    theirs = across(outer_half(place_other, first, grad_proj, attn_rows, mixed, tail, 1024, last_term)[0])
    one, two = outer_half(place, first, grad_proj, attn_rows, mixed, tail, 1024, first_term, theirs)
    layer_out = call(last_kernel, (middle_low, *last_term), row_shape)[0]
    one = sum_along(one, "x", "one_x").astype(BF)
    two = sum_along(two, "z", "two_z").astype(BF)
    grad_tokens = call(tokens_kernel, (tokens, norm_all, grad_middle, *first_term), row_shape, (one, two))[0]
    one = sum_along(one, "z", "one_z").astype(BF)
    two = sum_along(two, "x", "two_x")
    small = two[:32, 1024:].astype(F32)
    (attn_grads,) = hold([jnp.concatenate([one, two[:, :1024].astype(BF)], axis=1)], (layer_out, grad_tokens))
    attn_grads = swap(attn_grads).astype(F32)

    norm_parts = small[:4, :64].reshape(4, 4, 16).transpose(1, 0, 2)
    pick = lambda k: lax.dynamic_index_in_dim(norm_parts, (me - k) % 4, 0, keepdims=False)
    with jax.named_scope("norm_sum"):
        got = collect(jnp.concatenate([pick(0), small[8:, :2].reshape(3, 16)], axis=0), 0)
        grad_norms = got[:4] + collect(pick(1), 1) + collect(pick(2), 2) + collect(pick(3), 3)
    return (
        layer_out,
        grad_tokens,
        grad_norms,
        attn_grads[:, :1536].reshape(64, 3, 512).transpose(1, 0, 2),
        got[4:].reshape(3, 8, 2),
        attn_grads[:, 1536:2048].T,
        ffn_sum[:, :2816].reshape(64, 11, 2, 128).transpose(2, 0, 1, 3).reshape(2, 64, 1408),
        ffn_sum[:, 2816:].T,
    )


def solution(mesh):
    ring = Mesh(mesh.devices.reshape(4, 2, 4, 2, 2), ALL)
    fsdp, tp = ("x", "yl", "z"), ("yh", "core")
    return jax.shard_map(
        body,
        mesh=ring,
        in_specs=(
            P(ALL, None),
            P(fsdp, None),
            P(None, ALL),
            P(None, fsdp, tp),
            P(None, tp, fsdp),
            P(tp, fsdp),
            P(None, fsdp, tp),
            P(tp, fsdp),
            P(ALL, None),
        ),
        out_specs=(
            P(ALL, None),
            P(ALL, None),
            P(None, ALL),
            P(None, fsdp, tp),
            P(None, tp, fsdp),
            P(tp, fsdp),
            P(None, fsdp, tp),
            P(tp, fsdp),
        ),
        check_vma=False,
    )
```

time: 2610 us -> 423 us (0.16)
  waiting for transfers between devices: 1970 us -> 123 us
  blocking collectives: 413 us -> 0 us
  Pallas kernels: 0 us -> 120 us
  starting transfers between devices: 1.75 us -> 110 us
  matrix products: 108 us -> 0 us
  local copies, waits for them, and re-layouts: 59.4 us -> 33.1 us
    unnamed x18 -> x3, waiting for transfers between devices: 1080 us -> 0.05 us
    all_gather x8 -> x2, waiting for transfers between devices: 650 us -> 4.04 us  [the longest x1 4.02 us: body(): lax.all_gather(jnp.concatenate([w_attn, extra], axis=1), FSDP, axis=0, ti...]
    all_gather x2 -> x0, blocking collectives: 256 us -> none  [the longest x1 180 us: body(): norm_all = lax.all_gather(norms, ('fsdp', 'tp'), axis=1, tiled=True)]
    reduce_scatter x6 -> x1, waiting for transfers between devices: 238 us -> 0.02 us  [body(): lax.psum_scatter(grad_ffn, FSDP, scatter_dimension=0, tiled=True)]
    unnamed x1 -> x0, blocking collectives: 157 us -> none
    pallas_call x0 -> x20, Pallas kernels: none -> 120 us  [the longest x11 105 us: call(): pl.pallas_call(lambda *refs: kernel(*refs[:n], *refs[n + m:]), name=kerne...]
    ppermute x0 -> x56, waiting for transfers between devices: none -> 119 us  [the longest x12 65.3 us: shift(): lax.ppermute(v, ('yl', 'yh'), [(ring_index(y), ring_index((y + k) % 4)) f...]
    ppermute x0 -> x56, starting transfers between devices: none -> 110 us  [the longest x12 35.9 us: spread(): return lax.ppermute(v, ('yl', 'yh', 'core'), spread_pairs(k))]
  transfers between devices with their start and end apart: 16 -> 59, of which waited for: 13 -> 19; matrix products, arithmetic and copies ran while one was open for 5% -> 7% of each run, Pallas kernels for 0% -> 23%
where the time goes in v1:
time: 423 us; the launch traced here: 414 us
  waiting for transfers between devices  123 us (29%)
  Pallas kernels  120 us (28%)
  starting transfers between devices  110 us (26%)
  local copies, waits for them, and re-layouts  33.1 us (8%)
  between operations  14.7 us (3%)
  other arithmetic  12.9 us (3%)
    pallas_call x11, Pallas kernels, call(): pl.pallas_call(lambda *refs: kernel(*refs[:n], *refs[n + m:]), name=kerne...  105 us
    ppermute x12, waiting for transfers between devices, shift(): lax.ppermute(v, ('yl', 'yh'), [(ring_index(y), ring_index((y + k) % 4)) f...  65.3 us
    ppermute x12, starting transfers between devices, spread(): return lax.ppermute(v, ('yl', 'yh', 'core'), spread_pairs(k))  35.9 us
    ppermute x12, waiting for transfers between devices, collect(): lax.ppermute(v, ('yl', 'yh', 'core'), [(b, a) for a, b in spread_pairs(k)])  23 us
    ppermute x12, starting transfers between devices, collect(): lax.ppermute(v, ('yl', 'yh', 'core'), [(b, a) for a, b in spread_pairs(k)])  20.1 us
    ppermute x12, starting transfers between devices, along(): return lax.ppermute(v, axis, [(i, (i + k) % 4) for i in range(4)])  19.9 us
    ppermute x12, starting transfers between devices, shift(): lax.ppermute(v, ('yl', 'yh'), [(ring_index(y), ring_index((y + k) % 4)) f...  19.1 us
    ppermute x12, waiting for transfers between devices, along(): return lax.ppermute(v, axis, [(i, (i + k) % 4) for i in range(4)])  17.5 us
  transfers between devices with their start and end apart: 59, of which 19 were waited for; matrix products, arithmetic and copies ran while one was open for 7% of the time, Pallas kernels for 23%

profile of v1, /device:TPU:0, one launch (start us, length us, event | category | flops | bytes accessed | tf_op | source)
XLA Modules:
  0.0 414.4 jit_solution(7216862767456493273)
XLA Ops:
  9.5 3.1 collective-permute-start.2
  16.3 2.2 normal_kernel.1.refs_1_
  25.0 20.2 %collective-permute-start.7 = (bf16[128,2048]{1,0:T(8,128)(2,1)S(1)}, bf16[128,2048]{1,0:T(8,128)(2,1)}, u32[]{:S(2)}, u32[]{:S(2)}) collective-permute-start(bf16[128,2048]{1,0:T(8,128)(2,1)S(1)} %copy-done.19), channel_id=1, source_target_pairs={{0,16},{1,2},{2,18},{3,0},{16,17},{17,3},{18,19},{19,1},{4,20},{5,... | collective-permute-start | bytes 1572872 | tf_op jit(solution)/shard_map/n_rows/ppermute | solution.py:43
  45.8 2.4 collective-permute-start.9
  48.2 5.3 %collective-permute-start = (bf16[128,2048]{1,0:T(8,128)(2,1)}, bf16[128,2048]{1,0:T(8,128)(2,1)}, u32[]{:S(2)}, u32[]{:S(2)}) collective-permute-start(bf16[128,2048]{1,0:T(8,128)(2,1)} %refs_0_.3), channel_id=1, source_target_pairs={{0,0},{1,16},{16,1},{17,17},{2,2},{3,18},{18,3},{19,19},{4,4},{5,2... | collective-permute-start | bytes 1572872 | tf_op jit(solution)/shard_map/ppermute | solution.py:21
  56.7 12.0 %collective-permute-done.7.refs_1_.refs_3_ = bf16[128,2048]{1,0:T(8,128)(2,1)} collective-permute-done((bf16[128,2048]{1,0:T(8,128)(2,1)S(1)}, bf16[128,2048]{1,0:T(8,128)(2,1)}, u32[]{:S(2)}, u32[]{:S(2)}) %collective-permute-start.7) | collective-permute-done | bytes 524320 | tf_op jit(solution)/shard_map/n_rows/ppermute | solution.py:43
  69.9 2.9 collective-permute-start.13
  72.8 2.3 collective-permute-start.14
  80.3 4.0 all-gather.3.cloned.1.call-done.refs_5_.refs_6_.refs_7_.refs_8_.refs_4_.refs_1_
  87.4 17.8 %attend_kernel.1 = (bf16[512,2048]{1,0:T(8,128)(2,1)}, bf16[512,512]{1,0:T(8,128)(2,1)}, bf16[512,512]{1,0:T(8,128)(2,1)}, bf16[512,512]{1,0:T(8,128)(2,1)}, f32...) custom-call(bf16[128,2048]{1,0:T(8,128)(2,1)} %collective-permute-do, ...), custom_call_target="tpu_custom_call" | custom-call | tf_op jit(solution)/shard_map/attend_kernel/pallas_call | solution.py:73
  106.6 3.0 collective-permute-start.15
  111.7 11.5 %collective-permute-done.15.refs_3_ = bf16[128,2048]{1,0:T(8,128)(2,1)S(1)} collective-permute-done((bf16[128,2048]{1,0:T(8,128)(2,1)}, bf16[128,2048]{1,0:T(8,128)(2,1)S(1)}, u32[]{:S(2)}, u32[]{:S(2)}) %collective-permute-start.15) | collective-permute-done | bytes 524320 | tf_op jit(solution)/shard_map/attn_sum/ppermute | solution.py:29
  123.1 10.6 %collective-permute-done.16.refs_4_ = bf16[128,2048]{1,0:T(8,128)(2,1)S(1)} collective-permute-done((bf16[128,2048]{1,0:T(8,128)(2,1)}, bf16[128,2048]{1,0:T(8,128)(2,1)S(1)}, u32[]{:S(2)}, u32[]{:S(2)}) %collective-permute-start.16) | collective-permute-done | bytes 524320 | tf_op jit(solution)/shard_map/attn_sum/ppermute | solution.py:29
  134.8 3.6 middle_kernel.1
  139.8 2.7 collective-permute-start.19
  143.9 9.8 %collective-permute-done.18.refs_2_.refs_1_ = bf16[128,2048]{1,0:T(8,128)(2,1)S(1)} collective-permute-done((bf16[128,2048]{1,0:T(8,128)(2,1)}, bf16[128,2048]{1,0:T(8,128)(2,1)S(1)}, u32[]{:S(2)}, u32[]{:S(2)}) %collective-permute-start.18) | collective-permute-done | bytes 524320 | tf_op jit(solution)/shard_map/second_rows/ppermute | solution.py:29
  153.7 12.4 %collective-permute-done.19.refs_3_.refs_2_ = bf16[128,2048]{1,0:T(8,128)(2,1)S(1)} collective-permute-done((bf16[128,2048]{1,0:T(8,128)(2,1)}, bf16[128,2048]{1,0:T(8,128)(2,1)S(1)}, u32[]{:S(2)}, u32[]{:S(2)}) %collective-permute-start.19) | collective-permute-done | bytes 524320 | tf_op jit(solution)/shard_map/second_rows/ppermute | solution.py:29
  167.1 22.5 %feed_kernel.1 = (bf16[512,1408]{1,0:T(8,128)(2,1)}, bf16[512,2816]{1,0:T(8,128)(2,1)}, f32[128,2048]{1,0:T(8,128)}, bf16[128,2048]{1,0:T(8,128)(2,1)}, bf16[128...) custom-call(bf16[128,2048]{1,0:T(8,128)(2,1)} %get-tuple-element.64.refs_1_.refs_0_, bf16[128,2048]{1,0:T(8,128)(2,1)} %copy-done.14, ...), custom_call_target="tpu_custom_call" | custom-call | tf_op jit(solution)/shard_map/feed_kernel/pallas_call | solution.py:73
  189.6 2.2 collective-permute-start.22
  193.8 15.9 %outer_kernel.1.refs_2_.refs_0_ = bf16[2048,4224]{1,0:T(8,128)(2,1)} custom-call(bf16[128,2048]{1,0:T(8,128)(2,1)} %get-tuple-element.64.refs_1_.refs_0_, bf16[128,2048]{1,0:T(8,128)(2,1)} %copy-done.14, bf16[128,2048]{1,0:T(8,128)(2,1)} %copy-done.15, bf16[128,2048]{1,0:T(8,128)(2,1)} %copy-done.16, bf16[512,2816]{1,0:T(8,128)(2,1)} %get-tuple-element.66.refs_4_, ...), custom_call_target="tpu_custom_call" | custom-call | tf_op jit(solution)/shard_map/outer_kernel/pallas_call | solution.py:73
  209.7 7.2 %term_kernel.2 = (bf16[128,2048]{1,0:T(8,128)(2,1)}, bf16[128,2048]{1,0:T(8,128)(2,1)}, bf16[128,2048]{1,0:T(8,128)(2,1)}, bf16[128,2048]{1,0:T(8,128)(2,1)}) custom-call(bf16[512,1408]{1,0:T(8,128)(2,1)} %get-tuple-element.65.refs_9_.refs_0_, bf16[2048,4224]{1,0:T(8,128)(2,1)} %all-gather.5.cloned.1.call-done.refs_8_.refs_1_, ...), custom_call_target="tpu_custom_call" | custom-call | tf_op jit(solution)/shard_map/term_kernel/pallas_call | solution.py:73
  218.0 4.0 back_kernel.1
  223.7 3.7 collective-permute-start.26
  228.2 10.0 %collective-permute-done.25.refs_5_.refs_1_.refs_4_ = bf16[128,2048]{1,0:T(8,128)(2,1)S(1)} collective-permute-done((bf16[128,2048]{1,0:T(8,128)(2,1)S(1)}, bf16[128,2048]{1,0:T(8,128)(2,1)S(1)}, u32[]{:S(2)}, u32[]{:S(2)}) %collective-permute-start.25) | collective-permute-done | bytes 524320 | tf_op jit(solution)/shard_map/middle_rows/ppermute | solution.py:29
  238.2 11.0 %collective-permute-done.26.refs_6_.refs_2_.refs_5_ = bf16[128,2048]{1,0:T(8,128)(2,1)S(1)} collective-permute-done((bf16[128,2048]{1,0:T(8,128)(2,1)S(1)}, bf16[128,2048]{1,0:T(8,128)(2,1)S(1)}, u32[]{:S(2)}, u32[]{:S(2)}) %collective-permute-start.26) | collective-permute-done | bytes 524320 | tf_op jit(solution)/shard_map/middle_rows/ppermute | solution.py:29
  252.8 1.7 collective-permute-start.31
  255.2 16.4 %attend_back_kernel.1 = (bf16[512,1536]{1,0:T(8,128)(2,1)}, f32[24,64]{1,0:T(8,128)}) custom-call(bf16[128,2048]{1,0:T(8,128)(2,1)} %get-tuple-element.76.refs_0_.refs_3_.refs_1_, bf16[128,2048]{1,0:T(8,128)(2,1)} %copy-done.2, bf16[128,2048]{1,0:T(8,128)(2,1)} %copy-done.3, bf16[128,2048]{1,0:T(8,128)(2,1)} %copy-done.4, ...), custom_call_target="tpu_custom_call" | custom-call | tf_op jit(solution)/shard_map/attend_back_kernel/pallas_call | solution.py:73
  271.6 8.6 %term_kernel.3 = (bf16[128,2048]{1,0:T(8,128)(2,1)}, bf16[128,2048]{1,0:T(8,128)(2,1)}, bf16[128,2048]{1,0:T(8,128)(2,1)}, bf16[128,2048]{1,0:T(8,128)(2,1)}, bf16[2048,128]{1,0:T(8,128)(2,1)}) custom-call(bf16[512,1536]{1,0:T(8,128)(2,1)} %get-tuple-element.86.refs_0_.refs_2_, ...), custom_call_target="tpu_custom_call" | custom-call | tf_op jit(solution)/shard_map/term_kernel/pallas_call | solution.py:73
  281.6 7.4 %their_half_kernel.1 = bf16[1024,2176]{1,0:T(8,128)(2,1)} custom-call(s32[3]{0:T(128)} %get-tuple-element.134.refs_0_, bf16[512,2048]{1,0:T(8,128)(2,1)} %get-tuple-element.97.refs_1_, bf16[512,1536]{1,0:T(8,128)(2,1)} %get-tuple-element.86.refs_0_.refs_2_, bf16[128,2048]{1,0:T(8,128)(2,1)} %get-tuple-element.76.refs_0_.refs_3_.refs_1_, ...), custom_call_target="tpu_custom_call" | custom-call | tf_op jit(solution)/shard_map/their_half_kernel/pallas_call | solution.py:346
  288.9 2.7 collective-permute-start.37
  291.6 1.8 collective-permute-start.33
  296.1 11.7 %collective-permute-done.33.refs_10_.refs_3_ = bf16[128,2048]{1,0:T(8,128)(2,1)S(1)} collective-permute-done((bf16[128,2048]{1,0:T(8,128)(2,1)}, bf16[128,2048]{1,0:T(8,128)(2,1)S(1)}, u32[]{:S(2)}, u32[]{:S(2)}) %collective-permute-start.33) | collective-permute-done | bytes 524320 | tf_op jit(solution)/shard_map/first_sum/ppermute | solution.py:47
  309.5 7.5 %collective-permute-done.34.refs_11_.refs_4_ = bf16[128,2048]{1,0:T(8,128)(2,1)S(1)} collective-permute-done((bf16[128,2048]{1,0:T(8,128)(2,1)}, bf16[128,2048]{1,0:T(8,128)(2,1)S(1)}, u32[]{:S(2)}, u32[]{:S(2)}) %collective-permute-start.34) | collective-permute-done | bytes 524320 | tf_op jit(solution)/shard_map/first_sum/ppermute | solution.py:47
  319.5 8.3 %own_half_kernel.1 = (bf16[4,4,64,1024]{3,2,1,0:T(8,128)(2,1)}, bf16[4,4,64,1152]{3,2,1,0:T(8,128)(2,1)}) custom-call(s32[3]{0:T(128)} %get-tuple-element.135.refs_0_, bf16[512,2048]{1,0:T(8,128)(2,1)} %get-tuple-element.97.refs_1_, bf16[512,1536]{1,0:T(8,128)(2,1)} %get-tuple-element.86.refs_0_.refs_2_, ...), custom_call_target="tpu_custom_call" | custom-call | tf_op jit(solution)/shard_map/own_half_kernel/pallas_call | solution.py:346
  327.8 2.6 slice_bitcast_fusion.5
  330.5 3.0 collective-permute-start.38
  334.0 2.7 collective-permute-start.40
  337.8 1.7 collective-permute-start.41
  340.2 9.0 %collective-permute-done.38 = bf16[4,64,1024]{2,1,0:T(8,128)(2,1)S(1)} collective-permute-done((bf16[4,64,1024]{2,1,0:T(8,128)(2,1)S(1)}, bf16[4,64,1024]{2,1,0:T(8,128)(2,1)S(1)}, u32[]{:S(2)}, u32[]{:S(2)}) %collective-permute-start.38) | collective-permute-done | bytes 524320 | tf_op jit(solution)/shard_map/one_x/ppermute | solution.py:402
  350.0 2.1 collective-permute-start.43
  352.1 2.8 last_kernel.1.refs_1_
  355.0 5.1 %collective-permute-done.39 = bf16[4,64,1024]{2,1,0:T(8,128)(2,1)} collective-permute-done((bf16[4,64,1024]{2,1,0:T(8,128)(2,1)}, bf16[4,64,1024]{2,1,0:T(8,128)(2,1)}, u32[]{:S(2)}, u32[]{:S(2)}) %collective-permute-start.39) | collective-permute-done | bytes 524320 | tf_op jit(solution)/shard_map/one_x/ppermute | solution.py:402
  363.4 2.4 collective-permute-start.51
  367.1 1.9 collective-permute-start.53
  373.4 3.6 tokens_kernel.1.refs_2_
  377.0 2.6 collective-permute-start.46
  389.2 7.3 %collective-permute-start.48 = (f32[4,16]{1,0:T(4,128)S(1)}, f32[4,16]{1,0:T(4,128)S(1)}, u32[]{:S(2)}, u32[]{:S(2)}) collective-permute-start(f32[4,16]{1,0:T(4,128)S(1)} %bitcast.129), channel_id=1, source_target_pairs={{16,0},{2,1},{18,2},{0,3},{17,16},{3,17},{19,18},{1,19},{20,4},{6,... | collective-permute-start | bytes 776 | tf_op jit(solution)/shard_map/norm_sum/ppermute | solution.py:47
  397.7 2.1 collective-permute-start.50
  (262 shorter events, 82.4 us)
Async XLA Ops:
  7.2 77.2 %all-gather.3.cloned.1.call-start = ((), (), s32[]{:S(2)}) async-start(), calls=%async_computation.1 | async-start | bytes 9191424 | tf_op jit(solution)/shard_map/all_gather | solution.py:451
  21.0 145.1 %all-gather.5.cloned.1.call-start = ((), (), s32[]{:S(2)}) async-start(), calls=%async_computation.2 | async-start | bytes 17842176 | tf_op jit(solution)/shard_map/all_gather | solution.py:459
  23.4 363.4 %reduce-scatter.2.cloned.1.call-start = ((), (), s32[]{:S(2)}) async-start(), calls=%async_computation.3 | async-start | bytes 17842176 | tf_op jit(solution)/shard_map/reduce_scatter | solution.py:527
  23.5 31.5 %collective-permute-start.6 = (bf16[128,2048]{1,0:T(8,128)(2,1)S(1)}, bf16[128,2048]{1,0:T(8,128)(2,1)}, u32[]{:S(2)}, u32[]{:S(2)}) collective-permute-start(bf16[128,2048]{1,0:T(8,128)(2,1)S(1)} %copy-done.19), channel_id=1, source_target_pairs={{0,0},{1,16},{2,2},{3,18},{16,1},{17,17},{18,3},{19,19},{4,4},{5,2... | collective-permute-start | bytes 1572872 | tf_op jit(solution)/shard_map/n_rows/ppermute | solution.py:43
  25.0 43.7 %collective-permute-start.7 = (bf16[128,2048]{1,0:T(8,128)(2,1)S(1)}, bf16[128,2048]{1,0:T(8,128)(2,1)}, u32[]{:S(2)}, u32[]{:S(2)}) collective-permute-start(bf16[128,2048]{1,0:T(8,128)(2,1)S(1)} %copy-done.19), channel_id=1, source_target_pairs={{0,16},{1,2},{2,18},{3,0},{16,17},{17,3},{18,19},{19,1},{4,20},{5,... | collective-permute-start | bytes 1572872 | tf_op jit(solution)/shard_map/n_rows/ppermute | solution.py:43
  45.2 24.7 %collective-permute-start.8 = (bf16[128,2048]{1,0:T(8,128)(2,1)S(1)}, bf16[128,2048]{1,0:T(8,128)(2,1)}, u32[]{:S(2)}, u32[]{:S(2)}) collective-permute-start(bf16[128,2048]{1,0:T(8,128)(2,1)S(1)} %copy-done.19), channel_id=1, source_target_pairs={{0,2},{1,18},{2,0},{3,16},{16,3},{17,19},{18,1},{19,17},{4,6},{5,2... | collective-permute-start | bytes 1572872 | tf_op jit(solution)/shard_map/n_rows/ppermute | solution.py:43
  45.8 27.0 %collective-permute-start.9 = (bf16[128,2048]{1,0:T(8,128)(2,1)S(1)}, bf16[128,2048]{1,0:T(8,128)(2,1)}, u32[]{:S(2)}, u32[]{:S(2)}) collective-permute-start(bf16[128,2048]{1,0:T(8,128)(2,1)S(1)} %copy-done.19), channel_id=1, source_target_pairs={{0,18},{1,0},{2,16},{3,2},{16,19},{17,1},{18,17},{19,3},{4,22},{5,... | collective-permute-start | bytes 1572872 | tf_op jit(solution)/shard_map/n_rows/ppermute | solution.py:43
  48.2 39.2 %collective-permute-start = (bf16[128,2048]{1,0:T(8,128)(2,1)}, bf16[128,2048]{1,0:T(8,128)(2,1)}, u32[]{:S(2)}, u32[]{:S(2)}) collective-permute-start(bf16[128,2048]{1,0:T(8,128)(2,1)} %refs_0_.3), channel_id=1, source_target_pairs={{0,0},{1,16},{16,1},{17,17},{2,2},{3,18},{18,3},{19,19},{4,4},{5,2... | collective-permute-start | bytes 1572872 | tf_op jit(solution)/shard_map/ppermute | solution.py:21
  55.0 50.3 %collective-permute-start.11 = (bf16[128,2048]{1,0:T(8,128)(2,1)}, bf16[128,2048]{1,0:T(8,128)(2,1)S(1)}, u32[]{:S(2)}, u32[]{:S(2)}) collective-permute-start(bf16[128,2048]{1,0:T(8,128)(2,1)} %param.19), channel_id=1, source_target_pairs={{0,0},{1,16},{2,2},{3,18},{16,1},{17,17},{18,3},{19,19},{4,4},{5,2... | collective-permute-start | bytes 1572872 | tf_op jit(solution)/shard_map/grad_rows/ppermute | solution.py:43
  68.7 36.6 %collective-permute-start.12 = (bf16[128,2048]{1,0:T(8,128)(2,1)}, bf16[128,2048]{1,0:T(8,128)(2,1)S(1)}, u32[]{:S(2)}, u32[]{:S(2)}) collective-permute-start(bf16[128,2048]{1,0:T(8,128)(2,1)} %param.19), channel_id=1, source_target_pairs={{0,16},{1,2},{2,18},{3,0},{16,17},{17,3},{18,19},{19,1},{4,20},{5,... | collective-permute-start | bytes 1572872 | tf_op jit(solution)/shard_map/grad_rows/ppermute | solution.py:43
  69.9 35.4 %collective-permute-start.13 = (bf16[128,2048]{1,0:T(8,128)(2,1)}, bf16[128,2048]{1,0:T(8,128)(2,1)S(1)}, u32[]{:S(2)}, u32[]{:S(2)}) collective-permute-start(bf16[128,2048]{1,0:T(8,128)(2,1)} %param.19), channel_id=1, source_target_pairs={{0,2},{1,18},{2,0},{3,16},{16,3},{17,19},{18,1},{19,17},{4,6},{5,2... | collective-permute-start | bytes 1572872 | tf_op jit(solution)/shard_map/grad_rows/ppermute | solution.py:43
  72.8 32.5 %collective-permute-start.14 = (bf16[128,2048]{1,0:T(8,128)(2,1)}, bf16[128,2048]{1,0:T(8,128)(2,1)S(1)}, u32[]{:S(2)}, u32[]{:S(2)}) collective-permute-start(bf16[128,2048]{1,0:T(8,128)(2,1)} %param.19), channel_id=1, source_target_pairs={{0,18},{1,0},{2,16},{3,2},{16,19},{17,1},{18,17},{19,3},{4,22},{5,... | collective-permute-start | bytes 1572872 | tf_op jit(solution)/shard_map/grad_rows/ppermute | solution.py:43
  106.6 16.5 %collective-permute-start.15 = (bf16[128,2048]{1,0:T(8,128)(2,1)}, bf16[128,2048]{1,0:T(8,128)(2,1)S(1)}, u32[]{:S(2)}, u32[]{:S(2)}) collective-permute-start(bf16[128,2048]{1,0:T(8,128)(2,1)} %get-tuple-element.60), channel_id=1, source_target_pairs={{0,2},{16,18},{2,0},{18,16},{1,3},{17,19},{3,1},{19,17},{4,6},{20,... | collective-permute-start | bytes 1572872 | tf_op jit(solution)/shard_map/attn_sum/ppermute | solution.py:29
  109.6 24.1 %collective-permute-start.16 = (bf16[128,2048]{1,0:T(8,128)(2,1)}, bf16[128,2048]{1,0:T(8,128)(2,1)S(1)}, u32[]{:S(2)}, u32[]{:S(2)}) collective-permute-start(bf16[128,2048]{1,0:T(8,128)(2,1)} %get-tuple-element.61), channel_id=1, source_target_pairs={{0,18},{16,0},{2,16},{18,2},{1,19},{17,1},{3,17},{19,3},{4,22},{20... | collective-permute-start | bytes 1572872 | tf_op jit(solution)/shard_map/attn_sum/ppermute | solution.py:29
  110.8 23.0 %collective-permute-start.17 = (bf16[128,2048]{1,0:T(8,128)(2,1)}, bf16[128,2048]{1,0:T(8,128)(2,1)S(1)}, u32[]{:S(2)}, u32[]{:S(2)}) collective-permute-start(bf16[128,2048]{1,0:T(8,128)(2,1)} %get-tuple-element.62), channel_id=1, source_target_pairs={{0,16},{16,2},{2,18},{18,0},{1,17},{17,3},{3,19},{19,1},{4,20},{20... | collective-permute-start | bytes 1572872 | tf_op jit(solution)/shard_map/attn_sum/ppermute | solution.py:29
  138.4 15.3 %collective-permute-start.18 = (bf16[128,2048]{1,0:T(8,128)(2,1)}, bf16[128,2048]{1,0:T(8,128)(2,1)S(1)}, u32[]{:S(2)}, u32[]{:S(2)}) collective-permute-start(bf16[128,2048]{1,0:T(8,128)(2,1)} %get-tuple-element.64.refs_1_.refs_0_), channel_id=1, source_target_pairs={{0,16},{16,2},{2,18},{18,0},{1,17},{17,3},{3,19},{19,1},{4,20},{20... | collective-permute-start | bytes 1572872 | tf_op jit(solution)/shard_map/second_rows/ppermute | solution.py:29
  139.8 26.3 %collective-permute-start.19 = (bf16[128,2048]{1,0:T(8,128)(2,1)}, bf16[128,2048]{1,0:T(8,128)(2,1)S(1)}, u32[]{:S(2)}, u32[]{:S(2)}) collective-permute-start(bf16[128,2048]{1,0:T(8,128)(2,1)} %get-tuple-element.64.refs_1_.refs_0_), channel_id=1, source_target_pairs={{0,2},{16,18},{2,0},{18,16},{1,3},{17,19},{3,1},{19,17},{4,6},{20,... | collective-permute-start | bytes 1572872 | tf_op jit(solution)/shard_map/second_rows/ppermute | solution.py:29
  142.5 23.6 %collective-permute-start.20 = (bf16[128,2048]{1,0:T(8,128)(2,1)}, bf16[128,2048]{1,0:T(8,128)(2,1)S(1)}, u32[]{:S(2)}, u32[]{:S(2)}) collective-permute-start(bf16[128,2048]{1,0:T(8,128)(2,1)} %get-tuple-element.64.refs_1_.refs_0_), channel_id=1, source_target_pairs={{0,18},{16,0},{2,16},{18,2},{1,19},{17,1},{3,17},{19,3},{4,22},{20... | collective-permute-start | bytes 1572872 | tf_op jit(solution)/shard_map/second_rows/ppermute | solution.py:29
  189.6 27.3 %collective-permute-start.22 = (bf16[128,2048]{1,0:T(8,128)(2,1)}, bf16[128,2048]{1,0:T(8,128)(2,1)S(1)}, u32[]{:S(2)}, u32[]{:S(2)}) collective-permute-start(bf16[128,2048]{1,0:T(8,128)(2,1)} %get-tuple-element.73), channel_id=1, source_target_pairs={{0,2},{16,18},{2,0},{18,16},{1,3},{17,19},{3,1},{19,17},{4,6},{20,... | collective-permute-start | bytes 1572872 | tf_op jit(solution)/shard_map/second_sum/ppermute | solution.py:29
  191.8 25.1 %collective-permute-start.23 = (bf16[128,2048]{1,0:T(8,128)(2,1)}, bf16[128,2048]{1,0:T(8,128)(2,1)S(1)}, u32[]{:S(2)}, u32[]{:S(2)}) collective-permute-start(bf16[128,2048]{1,0:T(8,128)(2,1)} %get-tuple-element.74), channel_id=1, source_target_pairs={{0,18},{16,0},{2,16},{18,2},{1,19},{17,1},{3,17},{19,3},{4,22},{20... | collective-permute-start | bytes 1572872 | tf_op jit(solution)/shard_map/second_sum/ppermute | solution.py:29
  193.4 23.5 %collective-permute-start.24 = (bf16[128,2048]{1,0:T(8,128)(2,1)}, bf16[128,2048]{1,0:T(8,128)(2,1)S(1)}, u32[]{:S(2)}, u32[]{:S(2)}) collective-permute-start(bf16[128,2048]{1,0:T(8,128)(2,1)} %get-tuple-element.75), channel_id=1, source_target_pairs={{0,16},{16,2},{2,18},{18,0},{1,17},{17,3},{3,19},{19,1},{4,20},{20... | collective-permute-start | bytes 1572872 | tf_op jit(solution)/shard_map/second_sum/ppermute | solution.py:29
  223.1 15.1 %collective-permute-start.25 = (bf16[128,2048]{1,0:T(8,128)(2,1)S(1)}, bf16[128,2048]{1,0:T(8,128)(2,1)S(1)}, u32[]{:S(2)}, u32[]{:S(2)}) collective-permute-start(bf16[128,2048]{1,0:T(8,128)(2,1)S(1)} %copy-done), channel_id=1, source_target_pairs={{0,16},{16,2},{2,18},{18,0},{1,17},{17,3},{3,19},{19,1},{4,20},{20... | collective-permute-start | bytes 1572872 | tf_op jit(solution)/shard_map/middle_rows/ppermute | solution.py:29
  223.7 25.5 %collective-permute-start.26 = (bf16[128,2048]{1,0:T(8,128)(2,1)S(1)}, bf16[128,2048]{1,0:T(8,128)(2,1)S(1)}, u32[]{:S(2)}, u32[]{:S(2)}) collective-permute-start(bf16[128,2048]{1,0:T(8,128)(2,1)S(1)} %copy-done), channel_id=1, source_target_pairs={{0,2},{16,18},{2,0},{18,16},{1,3},{17,19},{3,1},{19,17},{4,6},{20,... | collective-permute-start | bytes 1572872 | tf_op jit(solution)/shard_map/middle_rows/ppermute | solution.py:29
  227.4 21.8 %collective-permute-start.27 = (bf16[128,2048]{1,0:T(8,128)(2,1)S(1)}, bf16[128,2048]{1,0:T(8,128)(2,1)S(1)}, u32[]{:S(2)}, u32[]{:S(2)}) collective-permute-start(bf16[128,2048]{1,0:T(8,128)(2,1)S(1)} %copy-done), channel_id=1, source_target_pairs={{0,18},{16,0},{2,16},{18,2},{1,19},{17,1},{3,17},{19,3},{4,22},{20... | collective-permute-start | bytes 1572872 | tf_op jit(solution)/shard_map/middle_rows/ppermute | solution.py:29
  250.2 30.0 %collective-permute-start.28 = (bf16[128,2048]{1,0:T(8,128)(2,1)}, bf16[128,2048]{1,0:T(8,128)(2,1)S(1)}, u32[]{:S(2)}, u32[]{:S(2)}) collective-permute-start(bf16[128,2048]{1,0:T(8,128)(2,1)} %get-tuple-element.77), channel_id=1, source_target_pairs={{2,0},{18,1},{0,2},{16,3},{3,16},{19,17},{1,18},{17,19},{6,4},{22,... | collective-permute-start | bytes 1572872 | tf_op jit(solution)/shard_map/out_sum/ppermute | solution.py:47
  251.3 28.9 %collective-permute-start.29 = (bf16[128,2048]{1,0:T(8,128)(2,1)}, bf16[128,2048]{1,0:T(8,128)(2,1)S(1)}, u32[]{:S(2)}, u32[]{:S(2)}) collective-permute-start(bf16[128,2048]{1,0:T(8,128)(2,1)} %get-tuple-element.78), channel_id=1, source_target_pairs={{16,0},{2,1},{18,2},{0,3},{17,16},{3,17},{19,18},{1,19},{20,4},{6,... | collective-permute-start | bytes 1572872 | tf_op jit(solution)/shard_map/out_sum/ppermute | solution.py:47
  252.5 27.8 %collective-permute-start.30 = (bf16[128,2048]{1,0:T(8,128)(2,1)}, bf16[128,2048]{1,0:T(8,128)(2,1)S(1)}, u32[]{:S(2)}, u32[]{:S(2)}) collective-permute-start(bf16[128,2048]{1,0:T(8,128)(2,1)} %get-tuple-element.79), channel_id=1, source_target_pairs={{18,0},{0,1},{16,2},{2,3},{19,16},{1,17},{17,18},{3,19},{22,4},{4,... | collective-permute-start | bytes 1572872 | tf_op jit(solution)/shard_map/out_sum/ppermute | solution.py:47
  252.8 27.4 %collective-permute-start.31 = (bf16[128,2048]{1,0:T(8,128)(2,1)}, bf16[128,2048]{1,0:T(8,128)(2,1)S(1)}, u32[]{:S(2)}, u32[]{:S(2)}) collective-permute-start(bf16[128,2048]{1,0:T(8,128)(2,1)} %get-tuple-element.80), channel_id=1, source_target_pairs={{0,0},{16,1},{2,2},{18,3},{1,16},{17,17},{3,18},{19,19},{4,4},{20,... | collective-permute-start | bytes 1572872 | tf_op jit(solution)/shard_map/out_sum/ppermute | solution.py:47
  288.9 29.6 %collective-permute-start.37 = (bf16[1024,2176]{1,0:T(8,128)(2,1)}, bf16[1024,2176]{1,0:T(8,128)(2,1)}, u32[]{:S(2)}, u32[]{:S(2)}) collective-permute-start(bf16[1024,2176]{1,0:T(8,128)(2,1)} %their_half_kernel.1), channel_id=1, source_target_pairs={{0,1},{1,0},{2,3},{3,2},{4,5},{5,4},{6,7},{7,6},{8,9},{9,8},{10,11... | collective-permute-start | bytes 13369352 | tf_op jit(solution)/shard_map/ppermute | solution.py:422
  291.6 16.2 %collective-permute-start.33 = (bf16[128,2048]{1,0:T(8,128)(2,1)}, bf16[128,2048]{1,0:T(8,128)(2,1)S(1)}, u32[]{:S(2)}, u32[]{:S(2)}) collective-permute-start(bf16[128,2048]{1,0:T(8,128)(2,1)} %get-tuple-element.93), channel_id=1, source_target_pairs={{2,0},{18,1},{0,2},{16,3},{3,16},{19,17},{1,18},{17,19},{6,4},{22,... | collective-permute-start | bytes 1572872 | tf_op jit(solution)/shard_map/first_sum/ppermute | solution.py:47
  293.4 23.5 %collective-permute-start.34 = (bf16[128,2048]{1,0:T(8,128)(2,1)}, bf16[128,2048]{1,0:T(8,128)(2,1)S(1)}, u32[]{:S(2)}, u32[]{:S(2)}) collective-permute-start(bf16[128,2048]{1,0:T(8,128)(2,1)} %get-tuple-element.94), channel_id=1, source_target_pairs={{16,0},{2,1},{18,2},{0,3},{17,16},{3,17},{19,18},{1,19},{20,4},{6,... | collective-permute-start | bytes 1572872 | tf_op jit(solution)/shard_map/first_sum/ppermute | solution.py:47
  293.7 24.8 %collective-permute-start.35 = (bf16[128,2048]{1,0:T(8,128)(2,1)}, bf16[128,2048]{1,0:T(8,128)(2,1)S(1)}, u32[]{:S(2)}, u32[]{:S(2)}) collective-permute-start(bf16[128,2048]{1,0:T(8,128)(2,1)} %get-tuple-element.95), channel_id=1, source_target_pairs={{18,0},{0,1},{16,2},{2,3},{19,16},{1,17},{17,18},{3,19},{22,4},{4,... | collective-permute-start | bytes 1572872 | tf_op jit(solution)/shard_map/first_sum/ppermute | solution.py:47
  294.4 24.1 %collective-permute-start.36 = (bf16[128,2048]{1,0:T(8,128)(2,1)}, bf16[128,2048]{1,0:T(8,128)(2,1)S(1)}, u32[]{:S(2)}, u32[]{:S(2)}) collective-permute-start(bf16[128,2048]{1,0:T(8,128)(2,1)} %get-tuple-element.96), channel_id=1, source_target_pairs={{0,0},{16,1},{2,2},{18,3},{1,16},{17,17},{3,18},{19,19},{4,4},{20,... | collective-permute-start | bytes 1572872 | tf_op jit(solution)/shard_map/first_sum/ppermute | solution.py:47
  307.8 31.8 %collective-permute-start.21 = (bf16[128,2048]{1,0:T(8,128)(2,1)}, bf16[128,2048]{1,0:T(8,128)(2,1)S(1)}, u32[]{:S(2)}, u32[]{:S(2)}) collective-permute-start(bf16[128,2048]{1,0:T(8,128)(2,1)} %hold.9), channel_id=1, source_target_pairs={{0,0},{1,16},{16,1},{17,17},{2,2},{3,18},{18,3},{19,19},{4,4},{5,2... | collective-permute-start | bytes 1572872 | tf_op jit(solution)/shard_map/ppermute | solution.py:21
  330.5 18.8 %collective-permute-start.38 = (bf16[4,64,1024]{2,1,0:T(8,128)(2,1)S(1)}, bf16[4,64,1024]{2,1,0:T(8,128)(2,1)S(1)}, u32[]{:S(2)}, u32[]{:S(2)}) collective-permute-start(bf16[4,64,1024]{2,1,0:T(8,128)(2,1)S(1)} %get-tuple-element.139), channel_id=1, source_target_pairs={{0,64},{32,96},{64,0},{96,32},{1,65},{33,97},{65,1},{97,33},{2,66}... | collective-permute-start | bytes 1572872 | tf_op jit(solution)/shard_map/one_x/ppermute | solution.py:402
  333.4 26.7 %collective-permute-start.39 = (bf16[4,64,1024]{2,1,0:T(8,128)(2,1)}, bf16[4,64,1024]{2,1,0:T(8,128)(2,1)}, u32[]{:S(2)}, u32[]{:S(2)}) collective-permute-start(bf16[4,64,1024]{2,1,0:T(8,128)(2,1)} %get-tuple-element.141), channel_id=1, source_target_pairs={{0,32},{32,64},{64,96},{96,0},{1,33},{33,65},{65,97},{97,1},{2,34}... | collective-permute-start | bytes 1572872 | tf_op jit(solution)/shard_map/one_x/ppermute | solution.py:402
  334.0 26.8 %collective-permute-start.40 = (bf16[4,64,1024]{2,1,0:T(8,128)(2,1)}, bf16[4,64,1024]{2,1,0:T(8,128)(2,1)}, u32[]{:S(2)}, u32[]{:S(2)}) collective-permute-start(bf16[4,64,1024]{2,1,0:T(8,128)(2,1)} %get-tuple-element.140), channel_id=1, source_target_pairs={{0,96},{32,0},{64,32},{96,64},{1,97},{33,1},{65,33},{97,65},{2,98}... | collective-permute-start | bytes 1572872 | tf_op jit(solution)/shard_map/one_x/ppermute | solution.py:402
  337.8 27.9 %collective-permute-start.41 = (bf16[4,64,1152]{2,1,0:T(8,128)(2,1)}, bf16[4,64,1152]{2,1,0:T(8,128)(2,1)}, u32[]{:S(2)}, u32[]{:S(2)}) collective-permute-start(bf16[4,64,1152]{2,1,0:T(8,128)(2,1)} %get-tuple-element.136), channel_id=1, source_target_pairs={{0,8},{4,12},{8,0},{12,4},{1,9},{5,13},{9,1},{13,5},{2,10},{6,14},... | collective-permute-start | bytes 1769480 | tf_op jit(solution)/shard_map/two_z/ppermute | solution.py:402
  339.6 27.6 %collective-permute-start.42 = (bf16[4,64,1152]{2,1,0:T(8,128)(2,1)}, bf16[4,64,1152]{2,1,0:T(8,128)(2,1)}, u32[]{:S(2)}, u32[]{:S(2)}) collective-permute-start(bf16[4,64,1152]{2,1,0:T(8,128)(2,1)} %get-tuple-element.138), channel_id=1, source_target_pairs={{0,4},{4,8},{8,12},{12,0},{1,5},{5,9},{9,13},{13,1},{2,6},{6,10},{... | collective-permute-start | bytes 1769480 | tf_op jit(solution)/shard_map/two_z/ppermute | solution.py:402
  350.0 19.0 %collective-permute-start.43 = (bf16[4,64,1152]{2,1,0:T(8,128)(2,1)S(1)}, bf16[4,64,1152]{2,1,0:T(8,128)(2,1)}, u32[]{:S(2)}, u32[]{:S(2)}) collective-permute-start(bf16[4,64,1152]{2,1,0:T(8,128)(2,1)S(1)} %get-tuple-element.137), channel_id=1, source_target_pairs={{0,12},{4,0},{8,4},{12,8},{1,13},{5,1},{9,5},{13,9},{2,14},{6,2},{... | collective-permute-start | bytes 1769480 | tf_op jit(solution)/shard_map/two_z/ppermute | solution.py:402
  360.1 11.8 %collective-permute-start.32 = (bf16[128,2048]{1,0:T(8,128)(2,1)S(1)}, bf16[128,2048]{1,0:T(8,128)(2,1)S(1)}, u32[]{:S(2)}, u32[]{:S(2)}) collective-permute-start(bf16[128,2048]{1,0:T(8,128)(2,1)S(1)} %copy-done.20), channel_id=1, source_target_pairs={{0,0},{1,16},{16,1},{17,17},{2,2},{3,18},{18,3},{19,19},{4,4},{5,2... | collective-permute-start | bytes 1572872 | tf_op jit(solution)/shard_map/ppermute | solution.py:21
  363.4 13.6 %collective-permute-start.51 = (bf16[64,1024]{1,0:T(8,128)(2,1)}, bf16[64,1024]{1,0:T(8,128)(2,1)}, u32[]{:S(2)}, u32[]{:S(2)}) collective-permute-start(bf16[64,1024]{1,0:T(8,128)(2,1)} %get-tuple-element.145), channel_id=1, source_target_pairs={{0,8},{4,12},{8,0},{12,4},{1,9},{5,13},{9,1},{13,5},{2,10},{6,14},... | collective-permute-start | bytes 393224 | tf_op jit(solution)/shard_map/one_z/ppermute | solution.py:402
  365.8 13.8 %collective-permute-start.52 = (bf16[64,1024]{1,0:T(8,128)(2,1)}, bf16[64,1024]{1,0:T(8,128)(2,1)}, u32[]{:S(2)}, u32[]{:S(2)}) collective-permute-start(bf16[64,1024]{1,0:T(8,128)(2,1)} %get-tuple-element.147), channel_id=1, source_target_pairs={{0,4},{4,8},{8,12},{12,0},{1,5},{5,9},{9,13},{13,1},{2,6},{6,10},{... | collective-permute-start | bytes 393224 | tf_op jit(solution)/shard_map/one_z/ppermute | solution.py:402
  367.1 12.4 %collective-permute-start.53 = (bf16[64,1024]{1,0:T(8,128)(2,1)}, bf16[64,1024]{1,0:T(8,128)(2,1)}, u32[]{:S(2)}, u32[]{:S(2)}) collective-permute-start(bf16[64,1024]{1,0:T(8,128)(2,1)} %get-tuple-element.146), channel_id=1, source_target_pairs={{0,12},{4,0},{8,4},{12,8},{1,13},{5,1},{9,5},{13,9},{2,14},{6,2},{... | collective-permute-start | bytes 393224 | tf_op jit(solution)/shard_map/one_z/ppermute | solution.py:402
  370.8 9.9 %collective-permute-start.44 = (bf16[64,1152]{1,0:T(8,128)(2,1)S(1)}, bf16[64,1152]{1,0:T(8,128)(2,1)S(1)}, u32[]{:S(2)}, u32[]{:S(2)}) collective-permute-start(bf16[64,1152]{1,0:T(8,128)(2,1)S(1)} %get-tuple-element.142), channel_id=1, source_target_pairs={{0,64},{32,96},{64,0},{96,32},{1,65},{33,97},{65,1},{97,33},{2,66}... | collective-permute-start | bytes 442376 | tf_op jit(solution)/shard_map/two_x/ppermute | solution.py:402
  385.0 18.4 %collective-permute-start.54 = (bf16[64,2048]{1,0:T(8,128)(2,1)}, bf16[64,2048]{1,0:T(8,128)(2,1)S(1)}, u32[]{:S(2)}, u32[]{:S(2)}) collective-permute-start(bf16[64,2048]{1,0:T(8,128)(2,1)} %hold.12), channel_id=1, source_target_pairs={{0,0},{1,16},{16,1},{17,17},{2,2},{3,18},{18,3},{19,19},{4,4},{5,2... | collective-permute-start | bytes 786440 | tf_op jit(solution)/shard_map/ppermute | solution.py:21
  386.8 18.5 %collective-permute-start.55 = (bf16[64,4224]{1,0:T(8,128)(2,1)}, bf16[64,4224]{1,0:T(8,128)(2,1)S(1)}, u32[]{:S(2)}, u32[]{:S(2)}) collective-permute-start(bf16[64,4224]{1,0:T(8,128)(2,1)} %reduce-scatter.2.cloned.1.call-done), channel_id=1, source_target_pairs={{0,0},{1,16},{16,1},{17,17},{2,2},{3,18},{18,3},{19,19},{4,4},{5,2... | collective-permute-start | bytes 1622024 | tf_op jit(solution)/shard_map/ppermute | solution.py:21
  389.2 11.4 %collective-permute-start.48 = (f32[4,16]{1,0:T(4,128)S(1)}, f32[4,16]{1,0:T(4,128)S(1)}, u32[]{:S(2)}, u32[]{:S(2)}) collective-permute-start(f32[4,16]{1,0:T(4,128)S(1)} %bitcast.129), channel_id=1, source_target_pairs={{16,0},{2,1},{18,2},{0,3},{17,16},{3,17},{19,18},{1,19},{20,4},{6,... | collective-permute-start | bytes 776 | tf_op jit(solution)/shard_map/norm_sum/ppermute | solution.py:47
  (51 other events, 248.2 us)
Sparse Core Ops, SparseCore 0:
  21.1 63.2 all-gather.2
  87.2 73.3 all-gather.4
  222.2 129.2 reduce-scatter.1

commit v2 on v1

--- a/solution.py
+++ b/solution.py
@@ -67,8 +67,9 @@
         return [collect(blocks[k], k) for k in (2, 1, 3, 0)]
 
 
-def call(kernel, args, outs, deps=(), limit=60, grid=None, specs=None, out_specs=None, scratch=()):
+def call(kernel, args, outs, deps=(), limit=None, grid=None, specs=None, out_specs=None, scratch=()):
     n, m = len(args), len(deps)
+    limit = limit or (60 if grid or scratch else 16)
     whole = pl.BlockSpec(memory_space=pltpu.VMEM)
     return pl.pallas_call(
         lambda *refs: kernel(*refs[:n], *refs[n + m :]),
@@ -110,6 +111,22 @@
     return value
 
 
+def pack_kernel(me, w, p0, p1, p2, p3, out):
+    out[:, :2048] = w[...]
+    norms = jnp.zeros((4, 64), F32)
+    for k, piece in enumerate((p0, p1, p2, p3)):
+        place = lax.rem(me[0] - k + 4, 4)
+        for q in range(4):
+            parts = [jnp.zeros((4, 16 * q), F32)] * (q > 0) + [piece[:4]] + [jnp.zeros((4, 48 - 16 * q), F32)] * (q < 3)
+            norms = norms + jnp.where(place == q, jnp.concatenate(parts, axis=1), 0.0)
+    high = norms.astype(BF).astype(F32)
+    middle = (norms - high).astype(BF).astype(F32)
+    biases = jnp.concatenate([p0[4:5], p0[5:6], p0[6:7], jnp.zeros((1, 16), F32)], axis=1)
+    rows = [high, middle, norms - high - middle, biases, jnp.zeros((51, 64), F32)]
+    rows = jnp.concatenate([jnp.concatenate(rows, axis=0), jnp.zeros((64, 64), F32)], axis=1)
+    out[:, 2048:] = rows.astype(BF)
+
+
 def normal_kernel(tokens, n):
     n[...] = normal(tokens[...].astype(F32))[0].astype(BF)
 
@@ -117,7 +134,6 @@
 def middle_kernel(tokens, norms, *refs):
     middle = tokens[...].astype(F32) + total(refs[:4])
     refs[4][...] = middle
-    refs[6][...] = middle.astype(BF)
     refs[5][...] = (normal(middle)[0] * norms[2:3] + norms[3:4]).astype(BF)
 
 
@@ -132,11 +148,16 @@
 
 def tokens_kernel(tokens, norms, grad, *refs):
     n, r = normal(tokens[...].astype(F32))
-    refs[4][...] = (grad[...].astype(F32) + normal_back(n, r, total(refs[:4]) * norms[0:1])).astype(BF)
+    refs[2][...] = (grad[...].astype(F32) + normal_back(n, r, total(refs[:2]) * norms[0:1])).astype(BF)
 
 
 def last_kernel(middle, *refs):
-    refs[4][...] = (middle[...].astype(F32) + total(refs[:4])).astype(BF)
+    refs[2][...] = (middle[...] + total(refs[:2])).astype(BF)
+
+
+def fold_kernel(own, pair, got, mine, theirs):
+    mine[...] = own[...].astype(F32) + got[:ROWS].astype(F32)
+    theirs[...] = (pair[...].astype(F32) + got[ROWS:].astype(F32)).astype(BF)
 
 
 def block_shapes(own=F32):
@@ -309,18 +330,47 @@
         out[:, begin : begin + width] = value.astype(BF)
 
 
-def own_half_kernel(place, a, b, c0, c1, c2, c3, d, extra, theirs, one, two):
-    split = one.shape[-1]
+def pieces_of(width):
+    cut = -(-width // 256) * 128
+    return ((0, 0, width), (1, 0, width), (2, 0, cut), (2, cut, width), (3, 0, width))
+
+
+def own_half_kernel(place, a, b, c0, c1, c2, c3, d, extra, theirs, *outs):
+    one, two = outs[:5], outs[5:10]
+    wide = theirs.shape[1]
+    split = one[0].shape[-1]
+    step = pl.program_id(0)
     for begin, width, value in half_columns(a, b, (c0, c1, c2, c3), d, extra):
         value = (value + theirs[:, begin : begin + width].astype(F32)).astype(BF)
         for z in range(4):
             at = lax.rem(z - place[2] + 4, 4)
             rows = value[z * 64 : (z + 1) * 64]
-            if begin < split:
-                one[0, at] = rows[:, :split]
-                two[at, 0, :, : width - split] = rows[:, split:]
-            else:
-                two[at, 0, :, begin - split : begin - split + width] = rows
+            for ref, (k, first, last) in zip(one, pieces_of(split)):
+                low, high = max(first, begin), min(last, begin + width)
+                if low < high:
+
+                    @pl.when(step == k)
+                    def _():
+                        ref[at, :, low - first : high - first] = rows[:, low - begin : high - begin]
+
+            for ref, (k, first, last) in zip(two, pieces_of(wide - split)):
+                low, high = max(first + split, begin), min(last + split, begin + width)
+                if low < high:
+
+                    @pl.when(at == k)
+                    def _():
+                        ref[0, :, low - split - first : high - split - first] = rows[:, low - begin : high - begin]
+
+
+def relay_kernel(*refs):
+    outs = refs[8:]
+    for c in range(2):
+        ahead, behind, first, rest = refs[4 * c : 4 * c + 4]
+        cut = first.shape[-1]
+        outs[2 * c][..., :cut] = (ahead[..., :cut].astype(F32) + first[...].astype(F32)).astype(BF)
+        outs[2 * c][..., cut:] = ahead[..., cut:]
+        outs[2 * c + 1][..., :cut] = behind[..., :cut]
+        outs[2 * c + 1][..., cut:] = (behind[..., cut:].astype(F32) + rest[...].astype(F32)).astype(BF)
 
 
 def outer_half(place, a, b, c, d, extra, split, deps, theirs=None):
@@ -337,11 +387,9 @@
         kernel, args, outs, shapes = their_half_kernel, [], [flat], [(1024, wide)]
     else:
         kernel, args, specs = own_half_kernel, [theirs], specs + [flat]
-        outs = [
-            pl.BlockSpec((1, 4, 64, split), lambda i, p: (i, 0, 0, 0)),
-            pl.BlockSpec((4, 1, 64, wide - split), lambda i, p: (0, i, 0, 0)),
-        ]
-        shapes = [(4, 4, 64, split), (4, 4, 64, wide - split)]
+        shapes = [(4, 64, last - first) for width in (split, wide - split) for _, first, last in pieces_of(width)]
+        outs = [pl.BlockSpec(shape, lambda i, p: (0, 0, 0)) for shape in shapes[:5]]
+        outs += [pl.BlockSpec((1,) + shape[1:], lambda i, p: (i, 0, 0)) for shape in shapes[5:]]
     count = 1 + len(specs)
     return pl.pallas_call(
         lambda *refs: kernel(*refs[:count], *refs[count + len(deps) :]),
@@ -357,55 +405,93 @@
     )(place, a, b, *c, d, extra, *args, *deps)
 
 
-def term_kernel(a, w, *refs):
+def term_kernel(a, w, place, *refs):
     value = mul(a[...], w[...], MT)
-    if len(refs) > 4:
-        *n, norm_two, grad_bias, t0, t1, t2, t3, tail = refs
-        refs = (t0, t1, t2, t3)
+    if len(refs) > 3:
+        *n, norm_two, grad_bias, own, pair, far, tail = refs
         gain = jnp.zeros((1, value.shape[1]), F32)
         for j in range(4):
             gain = gain + jnp.sum(value[j * ROWS : (j + 1) * ROWS] * n[j][...].astype(F32), axis=0, keepdims=True)
-        rows = jnp.concatenate([gain, jnp.sum(value, axis=0, keepdims=True), norm_two[...], jnp.zeros_like(norm_two), jnp.zeros_like(norm_two)], axis=0)
+        none = jnp.zeros((2, value.shape[1]), F32)
+        rows = jnp.concatenate([gain, jnp.sum(value, axis=0, keepdims=True), norm_two[...], none, none], axis=0)
         step = pl.program_id(0)
-        bias = jnp.zeros((24, 128), F32)
         lane = lane_of(HD)
         for f in range(8):
-            ones = [jnp.sum(jnp.where(lane == 2 * (step * 8 + f) + j, grad_bias[...], 0.0), axis=1, keepdims=True) for j in (0, 1)]
-            bias = jnp.concatenate(ones + [jnp.zeros((24, 126), F32)], axis=1)
+            two = [jnp.sum(jnp.where(lane == 2 * (step * 8 + f) + j, grad_bias[...], 0.0), axis=1, keepdims=True) for j in (0, 1)]
             tail[f * 64 : (f + 1) * 64] = jnp.concatenate(
                 [
                     jnp.concatenate([rows[:, f * 64 : (f + 1) * 64], jnp.zeros((8, 64), F32)], axis=1),
-                    bias,
+                    jnp.concatenate(two + [jnp.zeros((24, 126), F32)], axis=1),
                     jnp.zeros((32, 128), F32),
                 ],
                 axis=0,
             ).astype(BF)
-    for j in range(4):
-        refs[j][...] = value[j * ROWS : (j + 1) * ROWS].astype(refs[j].dtype)
-
-
-def row_term(a, w, at, n=None, norm_two=None, grad_bias=None, deps=(), own=BF, tile=512):
+        refs = (own, pair, far)
+    blocks = [value[j * ROWS : (j + 1) * ROWS].astype(BF) for j in range(4)]
+    refs[0][...] = blocks[0]
+    refs[2][:ROWS] = blocks[2]
+
+    @pl.when(place[3] == 0)
+    def _():
+        refs[1][...] = blocks[3]
+        refs[2][ROWS:] = blocks[1]
+
+    @pl.when(place[3] == 1)
+    def _():
+        refs[1][...] = blocks[1]
+        refs[2][ROWS:] = blocks[3]
+
+
+def row_term(a, w, at, place, n=None, norm_two=None, grad_bias=None, deps=(), tile=512):
     rows, depth = a.shape
-    block = pl.BlockSpec((ROWS, tile), lambda i: (0, i))
-    args = [a, w]
+    block = lambda height: pl.BlockSpec((height, tile), lambda i: (0, i))
+    args = [a, w, place]
     specs = [pl.BlockSpec((rows, depth), lambda i: (0, 0)), pl.BlockSpec((tile, depth), lambda i: (i, at))]
-    shapes, outs = block_shapes(own), [block] * 4
+    specs += [pl.BlockSpec(memory_space=pltpu.SMEM)]
+    shapes = [((ROWS, 2048), BF)] * 2 + [((2 * ROWS, 2048), BF)]
+    outs = [block(ROWS)] * 2 + [block(2 * ROWS)]
     if n is not None:
         args += [*n, norm_two, grad_bias]
-        specs += [block] * 4 + [pl.BlockSpec((2, tile), lambda i: (0, i)), pl.BlockSpec((24, HD), lambda i: (0, 0))]
+        specs += [block(ROWS)] * 4 + [block(2), pl.BlockSpec((24, HD), lambda i: (0, 0))]
         shapes = shapes + [((2048, 128), BF)]
         outs = outs + [pl.BlockSpec((tile, 128), lambda i: (i, 0))]
     return call(term_kernel, args, shapes, deps, grid=(2048 // tile,), specs=specs, out_specs=outs)
 
 
+def fold_rows(own, pair, far, name, deps=()):
+    with jax.named_scope(name):
+        return call(fold_kernel, (own, pair, shift(far, 2)), [((ROWS, 2048), F32), ((ROWS, 2048), BF)], deps)
+
+
+def fold_pair(mine, theirs, name):
+    with jax.named_scope(name):
+        return mine, lax.ppermute(theirs, "yl", [(0, 1), (1, 0)])
+
+
 def along(v, axis, k):
     return lax.ppermute(v, axis, [(i, (i + k) % 4) for i in range(4)])
 
 
-def sum_along(blocks, axis, name):
+def sum_pieces(one, two, axes, name):
+    got = [[], []]
     with jax.named_scope(name):
-        got = [along(blocks[k], axis, k) for k in (2, 1, 3)]
-    return blocks[0].astype(F32) + got[0].astype(F32) + got[1].astype(F32) + got[2].astype(F32)
+        for k in (2, 1, 3):
+            for c, blocks in enumerate((one, two)):
+                got[c].append(along(blocks[k], axes[c], k))
+    return got, [one[0], two[0]]
+
+
+def sum_large(one, two, axes):
+    blocks = (one, two)
+    with jax.named_scope("large_sum"):
+        got = [along(blocks[c][i], axes[c], k) for i, k in ((2, 1), (3, 3)) for c in range(2)]
+        sent = call(
+            relay_kernel,
+            (one[1], one[4], got[0], got[2], two[1], two[4], got[1], got[3]),
+            [(v.shape, BF) for v in (one[1], one[4], two[1], two[4])],
+        )
+        got = [along(sent[2 * c + i], axes[c], k) for i, k in ((0, 1), (1, 3)) for c in range(2)]
+        return [blocks[c][0].astype(F32) + got[c].astype(F32) + got[2 + c].astype(F32) for c in range(2)], sent
 
 
 def normal(v):
@@ -424,6 +510,7 @@
 
 def body(tokens, seq_lengths, norms, w_qkv, qkv_bias, w_out, w_gate_up, w_down, out_grad):
     me = 2 * lax.axis_index("yh") + lax.axis_index("yl")
+    place = jnp.stack([lax.axis_index(name) for name in ("core", "x", "z", "yl")]).astype(jnp.int32)
     small = jnp.concatenate(
         [
             norms,
@@ -433,22 +520,16 @@
         axis=0,
     )
     row_shape = [((ROWS, 2048), BF)]
-    w_attn = swap(jnp.concatenate([w_qkv[0], w_qkv[1], w_qkv[2], w_out.T], axis=1))
+    w_attn = jnp.concatenate([w_qkv[0], w_qkv[1], w_qkv[2], w_out.T], axis=1)
+    (small,) = hold([small], (w_attn,))
+    w_attn = swap(w_attn)
     n_own = call(normal_kernel, (tokens,), row_shape)[0]
     pieces = [spread(small, k) for k in range(4)]
     lengths = pieces[0][7, :4].astype(jnp.int32)
-    bias_row = pieces[0][4:7].reshape(1, 48)
-    turned = jnp.stack([p[:4] for p in pieces[::-1]] * 2)
-    ordered = lax.dynamic_slice_in_dim(turned, 3 - me, 4, axis=0)
-    norm_part = ordered.transpose(1, 0, 2).reshape(4, 64)
-    high = norm_part.astype(BF)
-    rest = norm_part - high.astype(F32)
-    middle_part = rest.astype(BF)
-    low = (rest - middle_part.astype(F32)).astype(BF)
-    extra = jnp.concatenate([high, middle_part, low, jnp.pad(bias_row.astype(BF), ((0, 0), (0, 16)))], axis=0)
-    extra = jnp.pad(extra, ((0, 64 - 13), (0, 64)))
-    (extra,) = hold([extra], (n_own,))
-    attn_full = lax.all_gather(jnp.concatenate([w_attn, extra], axis=1), FSDP, axis=0, tiled=True)
+    smem = pl.BlockSpec(memory_space=pltpu.SMEM)
+    vmem = pl.BlockSpec(memory_space=pltpu.VMEM)
+    packed = call(pack_kernel, (me.reshape(1), w_attn, *pieces), [((64, 2176), BF)], (n_own,), specs=[smem] + [vmem] * 5)[0]
+    attn_full = lax.all_gather(packed, FSDP, axis=0, tiled=True)
 
     n_rows = spread_rows(n_own, "n_rows")
     w_ffn = swap(
@@ -502,11 +583,8 @@
         scratch=[pltpu.VMEM((512, 512), F32)],
     )
     term = hold(term, mlp_rows)
-    middle, second, middle_low = call(
-        middle_kernel, (inputs, norm_all, *scatter_rows(term, "attn_sum")), [((ROWS, 2048), F32)] + row_shape * 2
-    )
+    middle, second = call(middle_kernel, (inputs, norm_all, *scatter_rows(term, "attn_sum")), [((ROWS, 2048), F32)] + row_shape)
     second = gather_rows(second, "second_rows")
-    middle_low = swap(hold([middle_low], second)[0])
     hidden, grad_pair, *term = call(
         feed_kernel,
         (*second, *mlp_rows, ffn_full),
@@ -516,7 +594,7 @@
     )
     term = scatter_rows(term, "second_sum")
     grad_ffn = outer(second, grad_pair, mlp_rows, hidden)
-    last_term = row_term(hidden, ffn_full, 2, deps=(grad_ffn,))
+    last_term = row_term(hidden, ffn_full, 2, place, deps=(grad_ffn,))
     grad_rows, norm_two = call(
         back_kernel,
         (middle, norm_all, mlp_rows[0], *term),
@@ -524,11 +602,10 @@
         (last_term[0],),
     )
     (grad_ffn,) = hold([grad_ffn], (grad_rows,))
-    ffn_sum = swap(lax.psum_scatter(grad_ffn, FSDP, scatter_dimension=0, tiled=True)).astype(F32)
+    ffn_low = swap(lax.psum_scatter(grad_ffn, FSDP, scatter_dimension=0, tiled=True))
+    ffn_sum = ffn_low.astype(F32)
     attn_rows = gather_rows(grad_rows, "middle_rows")
-    *last_term, grad_middle = hold([*last_term, grad_rows], attn_rows[1:])
-    last_term = collect_rows(last_term, "out_sum")
-    grad_middle = swap(grad_middle)
+    last_term = fold_rows(*hold(last_term, attn_rows[1:]), "out_sum")
     column = pl.BlockSpec((512, 128), lambda i: (0, i))
     grad_proj, grad_bias = call(
         attend_back_kernel,
@@ -542,21 +619,22 @@
         scratch=[pltpu.VMEM((512, 512), F32), pltpu.VMEM((512, 512), BF)],
     )
 
-    place = jnp.stack([lax.axis_index("core"), lax.axis_index("x"), lax.axis_index("z")]).astype(jnp.int32)
-    *term, tail = row_term(grad_proj, attn_full, 0, n_rows, norm_two, grad_bias)
-    first_term = collect_rows(hold(term, last_term), "first_sum")
-    place_other = place * jnp.array([-1, 1, 1]) + jnp.array([1, 0, 0])
-    theirs = across(outer_half(place_other, first, grad_proj, attn_rows, mixed, tail, 1024, last_term)[0])
-    one, two = outer_half(place, first, grad_proj, attn_rows, mixed, tail, 1024, first_term, theirs)
-    layer_out = call(last_kernel, (middle_low, *last_term), row_shape)[0]
-    one = sum_along(one, "x", "one_x").astype(BF)
-    two = sum_along(two, "z", "two_z").astype(BF)
-    grad_tokens = call(tokens_kernel, (tokens, norm_all, grad_middle, *first_term), row_shape, (one, two))[0]
-    one = sum_along(one, "z", "one_z").astype(BF)
-    two = sum_along(two, "x", "two_x")
+    *term, tail = row_term(grad_proj, attn_full, 0, place, n_rows, norm_two, grad_bias)
+    place_other = place * jnp.array([-1, 1, 1, 1]) + jnp.array([1, 0, 0, 0])
+    theirs = across(outer_half(place_other, first, grad_proj, attn_rows, mixed, tail, 1024, last_term[:1])[0])
+    parts = outer_half(place, first, grad_proj, attn_rows, mixed, tail, 1024, (), theirs)
+    (one, two), sent = sum_large(parts[:5], parts[5:], "xz")
+    first_term = fold_rows(*term, "first_sum", (parts[0],))
+    first_term = fold_pair(*first_term, "first_sum_too")
+    grad_tokens = swap(call(tokens_kernel, (inputs, norm_all, grad_rows, *first_term), row_shape)[0])
+    last_term = fold_pair(*hold(last_term, sent[:1]), "out_sum_too")
+    layer_out = swap(call(last_kernel, (middle, *last_term), row_shape)[0])
+    got, owns = sum_pieces(one.astype(BF), two.astype(BF), "zx", "small_sum")
+    owns = hold(owns, (ffn_low, grad_tokens, layer_out))
+    one, two = (sum((v.astype(F32) for v in more), own.astype(F32)) for own, more in zip(owns, got))
+    one = one.astype(BF)
     small = two[:32, 1024:].astype(F32)
-    (attn_grads,) = hold([jnp.concatenate([one, two[:, :1024].astype(BF)], axis=1)], (layer_out, grad_tokens))
-    attn_grads = swap(attn_grads).astype(F32)
+    attn_grads = swap(jnp.concatenate([one, two[:, :1024].astype(BF)], axis=1)).astype(F32)
 
     norm_parts = small[:4, :64].reshape(4, 4, 16).transpose(1, 0, 2)
     pick = lambda k: lax.dynamic_index_in_dim(norm_parts, (me - k) % 4, 0, keepdims=False)

time: 423 us -> 406 us (0.960)
  starting transfers between devices: 110 us -> 93.4 us
  local copies, waits for them, and re-layouts: 33.1 us -> 37.9 us
    ppermute x12 -> x4, waiting for transfers between devices: 23 us -> 4.03 us  [collect(): lax.ppermute(v, ('yl', 'yh', 'core'), [(b, a) for a, b in spread_pairs(k)])]
    ppermute x12 -> x4, starting transfers between devices: 20.1 us -> 9.2 us  [collect(): lax.ppermute(v, ('yl', 'yh', 'core'), [(b, a) for a, b in spread_pairs(k)])]
    ppermute x12, waiting for transfers between devices: 13.3 us -> 22.3 us  [spread(): return lax.ppermute(v, ('yl', 'yh', 'core'), spread_pairs(k))]
    ppermute x12 -> x14, waiting for transfers between devices: 65.3 us -> 72.6 us  [shift(): lax.ppermute(v, ('yl', 'yh'), [(ring_index(y), ring_index((y + k) % 4)) f...]
    ppermute x12, starting transfers between devices: 35.9 us -> 29.1 us  [spread(): return lax.ppermute(v, ('yl', 'yh', 'core'), spread_pairs(k))]
    unnamed x92 -> x118, local copies, waits for them, and re-layouts: 13.6 us -> 20.1 us
    pallas_call x11 -> x15, Pallas kernels: 105 us -> 98.4 us  [call(): pl.pallas_call(lambda *refs: kernel(*refs[:n], *refs[n + m:]), name=kerne...]
    ppermute x7, starting transfers between devices: 12.4 us -> 6.94 us  [swap(): return lax.ppermute(v, ('yl', 'core'), [(0, 0), (1, 2), (2, 1), (3, 3)])]
  transfers between devices with their start and end apart: 59 -> 57, of which waited for: 19 -> 22; matrix products, arithmetic and copies ran while one was open for 7% -> 7% of each run, Pallas kernels for 23% -> 23%
where the time goes in v2:
time: 406 us; the launch traced here: 400 us
  waiting for transfers between devices  125 us (31%)
  Pallas kernels  117 us (29%)
  starting transfers between devices  93.4 us (23%)
  local copies, waits for them, and re-layouts  37.9 us (9%)
  between operations  14.8 us (4%)
  other arithmetic  11.4 us (3%)
    pallas_call x15, Pallas kernels, call(): pl.pallas_call(lambda *refs: kernel(*refs[:n], *refs[n + m:]), name=kerne...  98.4 us
    ppermute x14, waiting for transfers between devices, shift(): lax.ppermute(v, ('yl', 'yh'), [(ring_index(y), ring_index((y + k) % 4)) f...  72.6 us
    ppermute x12, starting transfers between devices, spread(): return lax.ppermute(v, ('yl', 'yh', 'core'), spread_pairs(k))  29.1 us
    ppermute x14, starting transfers between devices, along(): return lax.ppermute(v, axis, [(i, (i + k) % 4) for i in range(4)])  23.3 us
    ppermute x14, starting transfers between devices, shift(): lax.ppermute(v, ('yl', 'yh'), [(ring_index(y), ring_index((y + k) % 4)) f...  22.8 us
    ppermute x12, waiting for transfers between devices, spread(): return lax.ppermute(v, ('yl', 'yh', 'core'), spread_pairs(k))  22.3 us
    unnamed x118, local copies, waits for them, and re-layouts  20.1 us
    pallas_call x2, Pallas kernels, outer_half(): pl.pallas_call(lambda *refs: kernel(*refs[:count], *refs[count + len(deps...  18.2 us
  transfers between devices with their start and end apart: 57, of which 22 were waited for; matrix products, arithmetic and copies ran while one was open for 7% of the time, Pallas kernels for 23%

profile of v2, /device:TPU:0, one launch (start us, length us, event | category | flops | bytes accessed | tf_op | source)
XLA Modules:
  0.0 399.5 jit_solution(2156553862693383323)
XLA Ops:
  14.0 5.3 %collective-permute-start.3 = (f32[8,16]{1,0:T(8,128)}, f32[8,16]{1,0:T(8,128)S(1)}, u32[]{:S(2)}, u32[]{:S(2)}) collective-permute-start(f32[8,16]{1,0:T(8,128)} %hold.6), channel_id=1, source_target_pairs={{0,16},{1,2},{2,18},{3,0},{16,17},{17,3},{18,19},{19,1},{4,20},{5,... | collective-permute-start | bytes 1544 | tf_op jit(solution)/shard_map/ppermute | solution.py:43
  19.3 2.9 collective-permute-start.4
  22.6 2.0 collective-permute-done.4.refs_4_
  28.7 12.2 %collective-permute-start.7 = (bf16[128,2048]{1,0:T(8,128)(2,1)S(1)}, bf16[128,2048]{1,0:T(8,128)(2,1)}, u32[]{:S(2)}, u32[]{:S(2)}) collective-permute-start(bf16[128,2048]{1,0:T(8,128)(2,1)S(1)} %normal_kernel.1.refs_6_), channel_id=1, source_target_pairs={{0,16},{1,2},{2,18},{3,0},{16,17},{17,3},{18,19},{19,1},{4,20},{5,... | collective-permute-start | bytes 1572872 | tf_op jit(solution)/shard_map/n_rows/ppermute | solution.py:43
  40.9 3.2 collective-permute-start.8
  47.9 19.1 %collective-permute-done.7.refs_1_.refs_4_ = bf16[128,2048]{1,0:T(8,128)(2,1)} collective-permute-done((bf16[128,2048]{1,0:T(8,128)(2,1)S(1)}, bf16[128,2048]{1,0:T(8,128)(2,1)}, u32[]{:S(2)}, u32[]{:S(2)}) %collective-permute-start.7) | collective-permute-done | bytes 524320 | tf_op jit(solution)/shard_map/n_rows/ppermute | solution.py:43
  69.9 1.8 multiply_sine_fusion
  71.8 2.2 concatenate.27.refs_11_.refs_10_
  73.9 2.2 concatenate.28.refs_12_.refs_11_
  78.1 3.9 all-gather.3.cloned.1.call-done.refs_5_.refs_6_.refs_7_.refs_8_.refs_4_.refs_1_
  86.0 17.8 %attend_kernel.1 = (bf16[512,2048]{1,0:T(8,128)(2,1)}, bf16[512,512]{1,0:T(8,128)(2,1)}, bf16[512,512]{1,0:T(8,128)(2,1)}, bf16[512,512]{1,0:T(8,128)(2,1)}, f32...) custom-call(bf16[128,2048]{1,0:T(8,128)(2,1)} %copy-done.39, ...), custom_call_target="tpu_custom_call" | custom-call | tf_op jit(solution)/shard_map/attend_kernel/pallas_call | solution.py:74
  104.9 3.0 collective-permute-start.15
  109.9 11.5 %collective-permute-done.15.refs_3_ = bf16[128,2048]{1,0:T(8,128)(2,1)S(1)} collective-permute-done((bf16[128,2048]{1,0:T(8,128)(2,1)}, bf16[128,2048]{1,0:T(8,128)(2,1)S(1)}, u32[]{:S(2)}, u32[]{:S(2)}) %collective-permute-start.15) | collective-permute-done | bytes 524320 | tf_op jit(solution)/shard_map/attn_sum/ppermute | solution.py:29
  121.4 10.7 %collective-permute-done.16.refs_4_ = bf16[128,2048]{1,0:T(8,128)(2,1)S(1)} collective-permute-done((bf16[128,2048]{1,0:T(8,128)(2,1)}, bf16[128,2048]{1,0:T(8,128)(2,1)S(1)}, u32[]{:S(2)}, u32[]{:S(2)}) %collective-permute-start.16) | collective-permute-done | bytes 524320 | tf_op jit(solution)/shard_map/attn_sum/ppermute | solution.py:29
  135.5 2.7 collective-permute-start.19
  139.8 9.3 %collective-permute-done.18.refs_1_ = bf16[128,2048]{1,0:T(8,128)(2,1)S(1)} collective-permute-done((bf16[128,2048]{1,0:T(8,128)(2,1)S(1)}, bf16[128,2048]{1,0:T(8,128)(2,1)S(1)}, u32[]{:S(2)}, u32[]{:S(2)}) %collective-permute-start.18) | collective-permute-done | bytes 524320 | tf_op jit(solution)/shard_map/second_rows/ppermute | solution.py:29
  149.1 12.2 %collective-permute-done.19.refs_2_ = bf16[128,2048]{1,0:T(8,128)(2,1)S(1)} collective-permute-done((bf16[128,2048]{1,0:T(8,128)(2,1)S(1)}, bf16[128,2048]{1,0:T(8,128)(2,1)S(1)}, u32[]{:S(2)}, u32[]{:S(2)}) %collective-permute-start.19) | collective-permute-done | bytes 524320 | tf_op jit(solution)/shard_map/second_rows/ppermute | solution.py:29
  162.1 22.6 %feed_kernel.1 = (bf16[512,1408]{1,0:T(8,128)(2,1)}, bf16[512,2816]{1,0:T(8,128)(2,1)}, f32[128,2048]{1,0:T(8,128)}, bf16[128,2048]{1,0:T(8,128)(2,1)}, bf16[128...) custom-call(bf16[128,2048]{1,0:T(8,128)(2,1)} %copy-done.15, bf16[128,2048]{1,0:T(8,128)(2,1)} %copy-done.44, ...), custom_call_target="tpu_custom_call" | custom-call | tf_op jit(solution)/shard_map/feed_kernel/pallas_call | solution.py:74
  184.7 2.1 collective-permute-start.21
  189.4 15.9 %outer_kernel.1.refs_3_.refs_0_ = bf16[2048,4224]{1,0:T(8,128)(2,1)} custom-call(bf16[128,2048]{1,0:T(8,128)(2,1)} %copy-done.15, bf16[128,2048]{1,0:T(8,128)(2,1)} %copy-done.44, bf16[128,2048]{1,0:T(8,128)(2,1)} %copy-done.45, bf16[128,2048]{1,0:T(8,128)(2,1)} %collective-permute-done.20.refs_3_, bf16[512,2816]{1,0:T(8,128)(2,1)} %get-tuple-element.77.refs_4_, ...), custom_call_target="tpu_custom_call" | custom-call | tf_op jit(solution)/shard_map/outer_kernel/pallas_call | solution.py:74
  205.3 7.6 %term_kernel.2 = (bf16[128,2048]{1,0:T(8,128)(2,1)}, bf16[128,2048]{1,0:T(8,128)(2,1)}, bf16[256,2048]{1,0:T(8,128)(2,1)}) custom-call(bf16[512,1408]{1,0:T(8,128)(2,1)} %get-tuple-element.76.refs_9_.refs_0_, bf16[2048,4224]{1,0:T(8,128)(2,1)} %all-gather.5.cloned.1.call-done.refs_8_.refs_1_, s32[4]{0:T(128)} %get-tuple-element.157.refs_2_.refs_0_, ...), custom_call_target="tpu_custom_call" | custom-call | tf_op jit(solution)/shard_map/term_kernel/pallas_call | solution.py:74
  214.0 2.3 back_kernel.1
  219.2 3.7 collective-permute-start.25
  222.9 10.5 %collective-permute-done.24.refs_3_.refs_1_.refs_4_ = bf16[128,2048]{1,0:T(8,128)(2,1)S(1)} collective-permute-done((bf16[128,2048]{1,0:T(8,128)(2,1)S(1)}, bf16[128,2048]{1,0:T(8,128)(2,1)S(1)}, u32[]{:S(2)}, u32[]{:S(2)}) %collective-permute-start.24) | collective-permute-done | bytes 524320 | tf_op jit(solution)/shard_map/middle_rows/ppermute | solution.py:29
  233.4 11.1 %collective-permute-done.25.refs_4_.refs_2_.refs_5_ = bf16[128,2048]{1,0:T(8,128)(2,1)S(1)} collective-permute-done((bf16[128,2048]{1,0:T(8,128)(2,1)S(1)}, bf16[128,2048]{1,0:T(8,128)(2,1)S(1)}, u32[]{:S(2)}, u32[]{:S(2)}) %collective-permute-start.25) | collective-permute-done | bytes 524320 | tf_op jit(solution)/shard_map/middle_rows/ppermute | solution.py:29
  246.4 16.4 %attend_back_kernel.1 = (bf16[512,1536]{1,0:T(8,128)(2,1)}, f32[24,64]{1,0:T(8,128)}) custom-call(bf16[128,2048]{1,0:T(8,128)(2,1)} %copy-done, bf16[128,2048]{1,0:T(8,128)(2,1)} %copy-done.31, bf16[128,2048]{1,0:T(8,128)(2,1)} %copy-done.32, bf16[128,2048]{1,0:T(8,128)(2,1)} %copy-done.33, ...), custom_call_target="tpu_custom_call" | custom-call | tf_op jit(solution)/shard_map/attend_back_kernel/pallas_call | solution.py:74
  262.8 8.7 %term_kernel.3 = (bf16[128,2048]{1,0:T(8,128)(2,1)}, bf16[128,2048]{1,0:T(8,128)(2,1)}, bf16[256,2048]{1,0:T(8,128)(2,1)}, bf16[2048,128]{1,0:T(8,128)(2,1)}) custom-call(bf16[512,1536]{1,0:T(8,128)(2,1)} %get-tuple-element.96.refs_0_.refs_2_, bf16[2048,2176]{1,0:T(8,128)(2,1)} %all-gather.3.cloned.1.call-done.refs_5_.refs_6_.refs_7_.refs_8_.refs_4_.refs_1_, ...), custom_call_target="tpu_custom_call" | custom-call | tf_op jit(solution)/shard_map/term_kernel/pallas_call | solution.py:74
  273.5 7.4 %their_half_kernel.1 = bf16[1024,2176]{1,0:T(8,128)(2,1)} custom-call(s32[4]{0:T(128)} %get-tuple-element.156.refs_0_, bf16[512,2048]{1,0:T(8,128)(2,1)} %get-tuple-element.91.refs_1_, bf16[512,1536]{1,0:T(8,128)(2,1)} %get-tuple-element.96.refs_0_.refs_2_, bf16[128,2048]{1,0:T(8,128)(2,1)} %copy-done, bf16[128,2048]{1,0:T(8,128)(2,1)} %copy-done.31, ...), custom_call_target="tpu_custom_call" | custom-call | tf_op jit(solution)/shard_map/their_half_kernel/pallas_call | solution.py:394
  281.0 2.9 collective-permute-start.35
  283.9 5.0 %collective-permute-done.28.refs_9_ = bf16[1024,2176]{1,0:T(8,128)(2,1)} collective-permute-done((bf16[1024,2176]{1,0:T(8,128)(2,1)}, bf16[1024,2176]{1,0:T(8,128)(2,1)}, u32[]{:S(2)}, u32[]{:S(2)}) %collective-permute-start.28) | collective-permute-done | bytes 4456480 | tf_op jit(solution)/shard_map/ppermute | solution.py:508
  288.8 10.8 %own_half_kernel.1 = (bf16[4,64,1024]{2,1,0:T(8,128)(2,1)}, bf16[4,64,1024]{2,1,0:T(8,128)(2,1)}, bf16[4,64,512]{2,1,0:T(8,128)(2,1)}, bf16[4,64,512]{2,1,0:T(8,...) custom-call(s32[4]{0:T(128)} %get-tuple-element.157.refs_2_.refs_0_,, ...), custom_call_target="tpu_custom_call" | custom-call | tf_op jit(solution)/shard_map/own_half_kernel/pallas_call | solution.py:394
  300.9 7.3 %collective-permute-done.35.refs_2_ = bf16[256,2048]{1,0:T(8,128)(2,1)S(1)} collective-permute-done((bf16[256,2048]{1,0:T(8,128)(2,1)S(1)}, bf16[256,2048]{1,0:T(8,128)(2,1)S(1)}, u32[]{:S(2)}, u32[]{:S(2)}) %collective-permute-start.35) | collective-permute-done | bytes 1048608 | tf_op jit(solution)/shard_map/first_sum/ppermute | solution.py:29
  312.4 2.0 collective-permute-start.36
  315.8 1.8 collective-permute-start.30
  317.6 2.6 collective-permute-start.32
  320.1 3.3 collective-permute-done.29.refs_2_
  323.4 1.9 collective-permute-done.32.refs_7_
  328.3 3.2 collective-permute-start.39
  332.4 2.8 collective-permute-start.41
  335.2 2.7 tokens_kernel.1
  338.0 1.9 collective-permute-done.33.refs_2_
  342.8 5.0 %collective-permute-done.38 = bf16[4,64,1024]{2,1,0:T(8,128)(2,1)} collective-permute-done((bf16[4,64,1024]{2,1,0:T(8,128)(2,1)}, bf16[4,64,1024]{2,1,0:T(8,128)(2,1)}, u32[]{:S(2)}, u32[]{:S(2)}) %collective-permute-start.38) | collective-permute-done | bytes 524320 | tf_op jit(solution)/shard_map/large_sum/ppermute | solution.py:472
  352.9 1.7 collective-permute-start.42
  357.0 2.7 collective-permute-start.45
  363.4 2.1 collective-permute-start.52
  368.7 1.7 collective-permute-done.51
  375.3 7.5 %collective-permute-start.47 = (f32[4,16]{1,0:T(4,128)S(1)}, f32[4,16]{1,0:T(4,128)S(1)}, u32[]{:S(2)}, u32[]{:S(2)}) collective-permute-start(f32[4,16]{1,0:T(4,128)S(1)} %bitcast.93), channel_id=1, source_target_pairs={{16,0},{2,1},{18,2},{0,3},{17,16},{3,17},{19,18},{1,19},{20,4},{6,... | collective-permute-start | bytes 776 | tf_op jit(solution)/shard_map/norm_sum/ppermute | solution.py:47
  384.7 3.3 collective-permute-done.48
  (274 shorter events, 82.5 us)
Async XLA Ops:
  7.2 74.9 %all-gather.3.cloned.1.call-start = ((), (), s32[]{:S(2)}) async-start(), calls=%async_computation.1 | async-start | bytes 9191424 | tf_op jit(solution)/shard_map/all_gather | solution.py:532
  9.1 15.6 %collective-permute-start.1 = (bf16[64,2048]{1,0:T(8,128)(2,1)S(1)}, bf16[64,2048]{1,0:T(8,128)(2,1)S(1)}, u32[]{:S(2)}, u32[]{:S(2)}) collective-permute-start(bf16[64,2048]{1,0:T(8,128)(2,1)S(1)} %pad_maximum_fusion.1.refs_1_), channel_id=1, source_target_pairs={{0,0},{1,16},{16,1},{17,17},{2,2},{3,18},{18,3},{19,19},{4,4},{5,2... | collective-permute-start | bytes 786440 | tf_op jit(solution)/shard_map/ppermute | solution.py:21
  12.7 9.9 %collective-permute-start.2 = (f32[8,16]{1,0:T(8,128)}, f32[8,16]{1,0:T(8,128)S(1)}, u32[]{:S(2)}, u32[]{:S(2)}) collective-permute-start(f32[8,16]{1,0:T(8,128)} %hold.6), channel_id=1, source_target_pairs={{0,0},{1,16},{2,2},{3,18},{16,1},{17,17},{18,3},{19,19},{4,4},{5,2... | collective-permute-start | bytes 1544 | tf_op jit(solution)/shard_map/ppermute | solution.py:43
  14.0 8.6 %collective-permute-start.3 = (f32[8,16]{1,0:T(8,128)}, f32[8,16]{1,0:T(8,128)S(1)}, u32[]{:S(2)}, u32[]{:S(2)}) collective-permute-start(f32[8,16]{1,0:T(8,128)} %hold.6), channel_id=1, source_target_pairs={{0,16},{1,2},{2,18},{3,0},{16,17},{17,3},{18,19},{19,1},{4,20},{5,... | collective-permute-start | bytes 1544 | tf_op jit(solution)/shard_map/ppermute | solution.py:43
  25.5 135.9 %all-gather.5.cloned.1.call-start = ((), (), s32[]{:S(2)}) async-start(), calls=%async_computation.2 | async-start | bytes 17842176 | tf_op jit(solution)/shard_map/all_gather | solution.py:540
  28.0 324.9 %reduce-scatter.2.cloned.1.call-start = ((), (), s32[]{:S(2)}) async-start(), calls=%async_computation.3 | async-start | bytes 17842176 | tf_op jit(solution)/shard_map/reduce_scatter | solution.py:605
  28.0 18.2 %collective-permute-start.6 = (bf16[128,2048]{1,0:T(8,128)(2,1)S(1)}, bf16[128,2048]{1,0:T(8,128)(2,1)S(1)}, u32[]{:S(2)}, u32[]{:S(2)}) collective-permute-start(bf16[128,2048]{1,0:T(8,128)(2,1)S(1)} %normal_kernel.1.refs_6_), channel_id=1, source_target_pairs={{0,0},{1,16},{2,2},{3,18},{16,1},{17,17},{18,3},{19,19},{4,4},{5,2... | collective-permute-start | bytes 1572872 | tf_op jit(solution)/shard_map/n_rows/ppermute | solution.py:43
  28.7 38.2 %collective-permute-start.7 = (bf16[128,2048]{1,0:T(8,128)(2,1)S(1)}, bf16[128,2048]{1,0:T(8,128)(2,1)}, u32[]{:S(2)}, u32[]{:S(2)}) collective-permute-start(bf16[128,2048]{1,0:T(8,128)(2,1)S(1)} %normal_kernel.1.refs_6_), channel_id=1, source_target_pairs={{0,16},{1,2},{2,18},{3,0},{16,17},{17,3},{18,19},{19,1},{4,20},{5,... | collective-permute-start | bytes 1572872 | tf_op jit(solution)/shard_map/n_rows/ppermute | solution.py:43
  40.9 27.3 %collective-permute-start.8 = (bf16[128,2048]{1,0:T(8,128)(2,1)S(1)}, bf16[128,2048]{1,0:T(8,128)(2,1)}, u32[]{:S(2)}, u32[]{:S(2)}) collective-permute-start(bf16[128,2048]{1,0:T(8,128)(2,1)S(1)} %normal_kernel.1.refs_6_), channel_id=1, source_target_pairs={{0,2},{1,18},{2,0},{3,16},{16,3},{17,19},{18,1},{19,17},{4,6},{5,2... | collective-permute-start | bytes 1572872 | tf_op jit(solution)/shard_map/n_rows/ppermute | solution.py:43
  44.1 24.5 %collective-permute-start.9 = (bf16[128,2048]{1,0:T(8,128)(2,1)S(1)}, bf16[128,2048]{1,0:T(8,128)(2,1)}, u32[]{:S(2)}, u32[]{:S(2)}) collective-permute-start(bf16[128,2048]{1,0:T(8,128)(2,1)S(1)} %normal_kernel.1.refs_6_), channel_id=1, source_target_pairs={{0,18},{1,0},{2,16},{3,2},{16,19},{17,1},{18,17},{19,3},{4,22},{5,... | collective-permute-start | bytes 1572872 | tf_op jit(solution)/shard_map/n_rows/ppermute | solution.py:43
  44.1 41.1 %collective-permute-start = (bf16[128,2048]{1,0:T(8,128)(2,1)S(1)}, bf16[128,2048]{1,0:T(8,128)(2,1)S(1)}, u32[]{:S(2)}, u32[]{:S(2)}) collective-permute-start(bf16[128,2048]{1,0:T(8,128)(2,1)S(1)} %copy-done.24), channel_id=1, source_target_pairs={{0,0},{1,16},{16,1},{17,17},{2,2},{3,18},{18,3},{19,19},{4,4},{5,2... | collective-permute-start | bytes 1572872 | tf_op jit(solution)/shard_map/ppermute | solution.py:21
  46.2 57.6 %collective-permute-start.11 = (bf16[128,2048]{1,0:T(8,128)(2,1)}, bf16[128,2048]{1,0:T(8,128)(2,1)S(1)}, u32[]{:S(2)}, u32[]{:S(2)}) collective-permute-start(bf16[128,2048]{1,0:T(8,128)(2,1)} %param.19), channel_id=1, source_target_pairs={{0,0},{1,16},{2,2},{3,18},{16,1},{17,17},{18,3},{19,19},{4,4},{5,2... | collective-permute-start | bytes 1572872 | tf_op jit(solution)/shard_map/grad_rows/ppermute | solution.py:43
  67.0 36.8 %collective-permute-start.12 = (bf16[128,2048]{1,0:T(8,128)(2,1)}, bf16[128,2048]{1,0:T(8,128)(2,1)S(1)}, u32[]{:S(2)}, u32[]{:S(2)}) collective-permute-start(bf16[128,2048]{1,0:T(8,128)(2,1)} %param.19), channel_id=1, source_target_pairs={{0,16},{1,2},{2,18},{3,0},{16,17},{17,3},{18,19},{19,1},{4,20},{5,... | collective-permute-start | bytes 1572872 | tf_op jit(solution)/shard_map/grad_rows/ppermute | solution.py:43
  68.1 35.7 %collective-permute-start.13 = (bf16[128,2048]{1,0:T(8,128)(2,1)}, bf16[128,2048]{1,0:T(8,128)(2,1)S(1)}, u32[]{:S(2)}, u32[]{:S(2)}) collective-permute-start(bf16[128,2048]{1,0:T(8,128)(2,1)} %param.19), channel_id=1, source_target_pairs={{0,2},{1,18},{2,0},{3,16},{16,3},{17,19},{18,1},{19,17},{4,6},{5,2... | collective-permute-start | bytes 1572872 | tf_op jit(solution)/shard_map/grad_rows/ppermute | solution.py:43
  68.6 35.2 %collective-permute-start.14 = (bf16[128,2048]{1,0:T(8,128)(2,1)}, bf16[128,2048]{1,0:T(8,128)(2,1)}, u32[]{:S(2)}, u32[]{:S(2)}) collective-permute-start(bf16[128,2048]{1,0:T(8,128)(2,1)} %param.19), channel_id=1, source_target_pairs={{0,18},{1,0},{2,16},{3,2},{16,19},{17,1},{18,17},{19,3},{4,22},{5,... | collective-permute-start | bytes 1572872 | tf_op jit(solution)/shard_map/grad_rows/ppermute | solution.py:43
  104.9 16.5 %collective-permute-start.15 = (bf16[128,2048]{1,0:T(8,128)(2,1)}, bf16[128,2048]{1,0:T(8,128)(2,1)S(1)}, u32[]{:S(2)}, u32[]{:S(2)}) collective-permute-start(bf16[128,2048]{1,0:T(8,128)(2,1)} %get-tuple-element.71), channel_id=1, source_target_pairs={{0,2},{16,18},{2,0},{18,16},{1,3},{17,19},{3,1},{19,17},{4,6},{20,... | collective-permute-start | bytes 1572872 | tf_op jit(solution)/shard_map/attn_sum/ppermute | solution.py:29
  107.9 24.2 %collective-permute-start.16 = (bf16[128,2048]{1,0:T(8,128)(2,1)}, bf16[128,2048]{1,0:T(8,128)(2,1)S(1)}, u32[]{:S(2)}, u32[]{:S(2)}) collective-permute-start(bf16[128,2048]{1,0:T(8,128)(2,1)} %get-tuple-element.72), channel_id=1, source_target_pairs={{0,18},{16,0},{2,16},{18,2},{1,19},{17,1},{3,17},{19,3},{4,22},{20... | collective-permute-start | bytes 1572872 | tf_op jit(solution)/shard_map/attn_sum/ppermute | solution.py:29
  109.0 23.0 %collective-permute-start.17 = (bf16[128,2048]{1,0:T(8,128)(2,1)}, bf16[128,2048]{1,0:T(8,128)(2,1)S(1)}, u32[]{:S(2)}, u32[]{:S(2)}) collective-permute-start(bf16[128,2048]{1,0:T(8,128)(2,1)} %get-tuple-element.73), channel_id=1, source_target_pairs={{0,16},{16,2},{2,18},{18,0},{1,17},{17,3},{3,19},{19,1},{4,20},{20... | collective-permute-start | bytes 1572872 | tf_op jit(solution)/shard_map/attn_sum/ppermute | solution.py:29
  134.0 15.1 %collective-permute-start.18 = (bf16[128,2048]{1,0:T(8,128)(2,1)S(1)}, bf16[128,2048]{1,0:T(8,128)(2,1)S(1)}, u32[]{:S(2)}, u32[]{:S(2)}) collective-permute-start(bf16[128,2048]{1,0:T(8,128)(2,1)S(1)} %get-tuple-element.75.refs_0_), channel_id=1, source_target_pairs={{0,16},{16,2},{2,18},{18,0},{1,17},{17,3},{3,19},{19,1},{4,20},{20... | collective-permute-start | bytes 1572872 | tf_op jit(solution)/shard_map/second_rows/ppermute | solution.py:29
  135.5 25.8 %collective-permute-start.19 = (bf16[128,2048]{1,0:T(8,128)(2,1)S(1)}, bf16[128,2048]{1,0:T(8,128)(2,1)S(1)}, u32[]{:S(2)}, u32[]{:S(2)}) collective-permute-start(bf16[128,2048]{1,0:T(8,128)(2,1)S(1)} %get-tuple-element.75.refs_0_), channel_id=1, source_target_pairs={{0,2},{16,18},{2,0},{18,16},{1,3},{17,19},{3,1},{19,17},{4,6},{20,... | collective-permute-start | bytes 1572872 | tf_op jit(solution)/shard_map/second_rows/ppermute | solution.py:29
  138.2 23.1 %collective-permute-start.20 = (bf16[128,2048]{1,0:T(8,128)(2,1)S(1)}, bf16[128,2048]{1,0:T(8,128)(2,1)}, u32[]{:S(2)}, u32[]{:S(2)}) collective-permute-start(bf16[128,2048]{1,0:T(8,128)(2,1)S(1)} %get-tuple-element.75.refs_0_), channel_id=1, source_target_pairs={{0,18},{16,0},{2,16},{18,2},{1,19},{17,1},{3,17},{19,3},{4,22},{20... | collective-permute-start | bytes 1572872 | tf_op jit(solution)/shard_map/second_rows/ppermute | solution.py:29
  184.7 28.2 %collective-permute-start.21 = (bf16[128,2048]{1,0:T(8,128)(2,1)}, bf16[128,2048]{1,0:T(8,128)(2,1)S(1)}, u32[]{:S(2)}, u32[]{:S(2)}) collective-permute-start(bf16[128,2048]{1,0:T(8,128)(2,1)} %get-tuple-element.82), channel_id=1, source_target_pairs={{0,2},{16,18},{2,0},{18,16},{1,3},{17,19},{3,1},{19,17},{4,6},{20,... | collective-permute-start | bytes 1572872 | tf_op jit(solution)/shard_map/second_sum/ppermute | solution.py:29
  186.8 26.2 %collective-permute-start.22 = (bf16[128,2048]{1,0:T(8,128)(2,1)}, bf16[128,2048]{1,0:T(8,128)(2,1)}, u32[]{:S(2)}, u32[]{:S(2)}) collective-permute-start(bf16[128,2048]{1,0:T(8,128)(2,1)} %get-tuple-element.83), channel_id=1, source_target_pairs={{0,18},{16,0},{2,16},{18,2},{1,19},{17,1},{3,17},{19,3},{4,22},{20... | collective-permute-start | bytes 1572872 | tf_op jit(solution)/shard_map/second_sum/ppermute | solution.py:29
  188.3 24.7 %collective-permute-start.23 = (bf16[128,2048]{1,0:T(8,128)(2,1)}, bf16[128,2048]{1,0:T(8,128)(2,1)}, u32[]{:S(2)}, u32[]{:S(2)}) collective-permute-start(bf16[128,2048]{1,0:T(8,128)(2,1)} %get-tuple-element.84), channel_id=1, source_target_pairs={{0,16},{16,2},{2,18},{18,0},{1,17},{17,3},{3,19},{19,1},{4,20},{20... | collective-permute-start | bytes 1572872 | tf_op jit(solution)/shard_map/second_sum/ppermute | solution.py:29
  218.7 14.7 %collective-permute-start.24 = (bf16[128,2048]{1,0:T(8,128)(2,1)S(1)}, bf16[128,2048]{1,0:T(8,128)(2,1)S(1)}, u32[]{:S(2)}, u32[]{:S(2)}) collective-permute-start(bf16[128,2048]{1,0:T(8,128)(2,1)S(1)} %copy-done.1), channel_id=1, source_target_pairs={{0,16},{16,2},{2,18},{18,0},{1,17},{17,3},{3,19},{19,1},{4,20},{20... | collective-permute-start | bytes 1572872 | tf_op jit(solution)/shard_map/middle_rows/ppermute | solution.py:29
  219.2 25.4 %collective-permute-start.25 = (bf16[128,2048]{1,0:T(8,128)(2,1)S(1)}, bf16[128,2048]{1,0:T(8,128)(2,1)S(1)}, u32[]{:S(2)}, u32[]{:S(2)}) collective-permute-start(bf16[128,2048]{1,0:T(8,128)(2,1)S(1)} %copy-done.1), channel_id=1, source_target_pairs={{0,2},{16,18},{2,0},{18,16},{1,3},{17,19},{3,1},{19,17},{4,6},{20,... | collective-permute-start | bytes 1572872 | tf_op jit(solution)/shard_map/middle_rows/ppermute | solution.py:29
  222.9 21.6 %collective-permute-start.26 = (bf16[128,2048]{1,0:T(8,128)(2,1)S(1)}, bf16[128,2048]{1,0:T(8,128)(2,1)S(1)}, u32[]{:S(2)}, u32[]{:S(2)}) collective-permute-start(bf16[128,2048]{1,0:T(8,128)(2,1)S(1)} %copy-done.1), channel_id=1, source_target_pairs={{0,18},{16,0},{2,16},{18,2},{1,19},{17,1},{3,17},{19,3},{4,22},{20... | collective-permute-start | bytes 1572872 | tf_op jit(solution)/shard_map/middle_rows/ppermute | solution.py:29
  245.5 25.9 %collective-permute-start.27 = (bf16[256,2048]{1,0:T(8,128)(2,1)}, bf16[256,2048]{1,0:T(8,128)(2,1)S(1)}, u32[]{:S(2)}, u32[]{:S(2)}) collective-permute-start(bf16[256,2048]{1,0:T(8,128)(2,1)} %get-tuple-element.88), channel_id=1, source_target_pairs={{0,2},{16,18},{2,0},{18,16},{1,3},{17,19},{3,1},{19,17},{4,6},{20,... | collective-permute-start | bytes 3145736 | tf_op jit(solution)/shard_map/out_sum/ppermute | solution.py:29
  281.0 27.2 %collective-permute-start.35 = (bf16[256,2048]{1,0:T(8,128)(2,1)S(1)}, bf16[256,2048]{1,0:T(8,128)(2,1)S(1)}, u32[]{:S(2)}, u32[]{:S(2)}) collective-permute-start(bf16[256,2048]{1,0:T(8,128)(2,1)S(1)} %copy-done.54), channel_id=1, source_target_pairs={{0,2},{16,18},{2,0},{18,16},{1,3},{17,19},{3,1},{19,17},{4,6},{20,... | collective-permute-start | bytes 3145736 | tf_op jit(solution)/shard_map/first_sum/ppermute | solution.py:29
  299.6 25.7 %collective-permute-start.31 = (bf16[4,64,640]{2,1,0:T(8,128)(2,1)}, bf16[4,64,640]{2,1,0:T(8,128)(2,1)S(1)}, u32[]{:S(2)}, u32[]{:S(2)}) collective-permute-start(bf16[4,64,640]{2,1,0:T(8,128)(2,1)} %get-tuple-element.107), channel_id=1, source_target_pairs={{0,4},{4,8},{8,12},{12,0},{1,5},{5,9},{9,13},{13,1},{2,6},{6,10},{... | collective-permute-start | bytes 983048 | tf_op jit(solution)/shard_map/large_sum/ppermute | solution.py:472
  312.4 20.0 %collective-permute-start.36 = (bf16[128,2048]{1,0:T(8,128)(2,1)}, bf16[128,2048]{1,0:T(8,128)(2,1)}, u32[]{:S(2)}, u32[]{:S(2)}) collective-permute-start(bf16[128,2048]{1,0:T(8,128)(2,1)} %get-tuple-element.117), channel_id=1, source_target_pairs={{0,16},{16,0},{1,17},{17,1},{2,18},{18,2},{3,19},{19,3},{4,20},{20... | collective-permute-start | bytes 1572872 | tf_op jit(solution)/shard_map/first_sum_too/ppermute | solution.py:468
  314.3 9.1 %collective-permute-start.29 = (bf16[4,64,512]{2,1,0:T(8,128)(2,1)}, bf16[4,64,512]{2,1,0:T(8,128)(2,1)S(1)}, u32[]{:S(2)}, u32[]{:S(2)}) collective-permute-start(bf16[4,64,512]{2,1,0:T(8,128)(2,1)} %get-tuple-element.103), channel_id=1, source_target_pairs={{0,32},{32,64},{64,96},{96,0},{1,33},{33,65},{65,97},{97,1},{2,34}... | collective-permute-start | bytes 786440 | tf_op jit(solution)/shard_map/large_sum/ppermute | solution.py:472
  328.3 11.6 %collective-permute-start.33 = (bf16[128,2048]{1,0:T(8,128)(2,1)}, bf16[128,2048]{1,0:T(8,128)(2,1)}, u32[]{:S(2)}, u32[]{:S(2)}) collective-permute-start(bf16[128,2048]{1,0:T(8,128)(2,1)} %get-tuple-element.111), channel_id=1, source_target_pairs={{0,16},{16,0},{1,17},{17,1},{2,18},{18,2},{3,19},{19,3},{4,20},{20... | collective-permute-start | bytes 1572872 | tf_op jit(solution)/shard_map/out_sum_too/ppermute | solution.py:468
  328.3 19.5 %collective-permute-start.38 = (bf16[4,64,1024]{2,1,0:T(8,128)(2,1)}, bf16[4,64,1024]{2,1,0:T(8,128)(2,1)}, u32[]{:S(2)}, u32[]{:S(2)}) collective-permute-start(bf16[4,64,1024]{2,1,0:T(8,128)(2,1)} %copy-done.25), channel_id=1, source_target_pairs={{0,32},{32,64},{64,96},{96,0},{1,33},{33,65},{65,97},{97,1},{2,34}... | collective-permute-start | bytes 1572872 | tf_op jit(solution)/shard_map/large_sum/ppermute | solution.py:472
  328.3 20.2 %collective-permute-start.39 = (bf16[4,64,1024]{2,1,0:T(8,128)(2,1)}, bf16[4,64,1024]{2,1,0:T(8,128)(2,1)}, u32[]{:S(2)}, u32[]{:S(2)}) collective-permute-start(bf16[4,64,1024]{2,1,0:T(8,128)(2,1)} %copy-done.30), channel_id=1, source_target_pairs={{0,96},{32,0},{64,32},{96,64},{1,97},{33,1},{65,33},{97,65},{2,98}... | collective-permute-start | bytes 1572872 | tf_op jit(solution)/shard_map/large_sum/ppermute | solution.py:472
  331.5 19.8 %collective-permute-start.40 = (bf16[4,64,1152]{2,1,0:T(8,128)(2,1)}, bf16[4,64,1152]{2,1,0:T(8,128)(2,1)}, u32[]{:S(2)}, u32[]{:S(2)}) collective-permute-start(bf16[4,64,1152]{2,1,0:T(8,128)(2,1)} %copy-done.29), channel_id=1, source_target_pairs={{0,4},{4,8},{8,12},{12,0},{1,5},{5,9},{9,13},{13,1},{2,6},{6,10},{... | collective-permute-start | bytes 1769480 | tf_op jit(solution)/shard_map/large_sum/ppermute | solution.py:472
  332.4 19.0 %collective-permute-start.41 = (bf16[4,64,1152]{2,1,0:T(8,128)(2,1)}, bf16[4,64,1152]{2,1,0:T(8,128)(2,1)}, u32[]{:S(2)}, u32[]{:S(2)}) collective-permute-start(bf16[4,64,1152]{2,1,0:T(8,128)(2,1)} %copy-done.28), channel_id=1, source_target_pairs={{0,12},{4,0},{8,4},{12,8},{1,13},{5,1},{9,5},{13,9},{2,14},{6,2},{... | collective-permute-start | bytes 1769480 | tf_op jit(solution)/shard_map/large_sum/ppermute | solution.py:472
  339.9 17.1 %collective-permute-start.37 = (bf16[128,2048]{1,0:T(8,128)(2,1)}, bf16[128,2048]{1,0:T(8,128)(2,1)S(1)}, u32[]{:S(2)}, u32[]{:S(2)}) collective-permute-start(bf16[128,2048]{1,0:T(8,128)(2,1)} %tokens_kernel.1), channel_id=1, source_target_pairs={{0,0},{1,16},{16,1},{17,17},{2,2},{3,18},{18,3},{19,19},{4,4},{5,2... | collective-permute-start | bytes 1572872 | tf_op jit(solution)/shard_map/ppermute | solution.py:21
  347.8 12.6 %collective-permute-start.34 = (bf16[128,2048]{1,0:T(8,128)(2,1)S(1)}, bf16[128,2048]{1,0:T(8,128)(2,1)S(1)}, u32[]{:S(2)}, u32[]{:S(2)}) collective-permute-start(bf16[128,2048]{1,0:T(8,128)(2,1)S(1)} %last_kernel.1), channel_id=1, source_target_pairs={{0,0},{1,16},{16,1},{17,17},{2,2},{3,18},{18,3},{19,19},{4,4},{5,2... | collective-permute-start | bytes 1572872 | tf_op jit(solution)/shard_map/ppermute | solution.py:21
  352.9 9.2 %collective-permute-start.42 = (bf16[64,4224]{1,0:T(8,128)(2,1)}, bf16[64,4224]{1,0:T(8,128)(2,1)S(1)}, u32[]{:S(2)}, u32[]{:S(2)}) collective-permute-start(bf16[64,4224]{1,0:T(8,128)(2,1)} %reduce-scatter.2.cloned.1.call-done), channel_id=1, source_target_pairs={{0,0},{1,16},{16,1},{17,17},{2,2},{3,18},{18,3},{19,19},{4,4},{5,2... | collective-permute-start | bytes 1622024 | tf_op jit(solution)/shard_map/ppermute | solution.py:21
  355.3 8.0 %collective-permute-start.43 = (bf16[64,1152]{1,0:T(8,128)(2,1)}, bf16[64,1152]{1,0:T(8,128)(2,1)S(1)}, u32[]{:S(2)}, u32[]{:S(2)}) collective-permute-start(bf16[64,1152]{1,0:T(8,128)(2,1)} %get-tuple-element.161), channel_id=1, source_target_pairs={{0,64},{32,96},{64,0},{96,32},{1,65},{33,97},{65,1},{97,33},{2,66}... | collective-permute-start | bytes 442376 | tf_op jit(solution)/shard_map/small_sum/ppermute | solution.py:472
  356.4 10.5 %collective-permute-start.44 = (bf16[64,1152]{1,0:T(8,128)(2,1)S(1)}, bf16[64,1152]{1,0:T(8,128)(2,1)S(1)}, u32[]{:S(2)}, u32[]{:S(2)}) collective-permute-start(bf16[64,1152]{1,0:T(8,128)(2,1)S(1)} %get-tuple-element.160), channel_id=1, source_target_pairs={{0,32},{32,64},{64,96},{96,0},{1,33},{33,65},{65,97},{97,1},{2,34}... | collective-permute-start | bytes 442376 | tf_op jit(solution)/shard_map/small_sum/ppermute | solution.py:472
  357.0 9.9 %collective-permute-start.45 = (bf16[64,1152]{1,0:T(8,128)(2,1)S(1)}, bf16[64,1152]{1,0:T(8,128)(2,1)S(1)}, u32[]{:S(2)}, u32[]{:S(2)}) collective-permute-start(bf16[64,1152]{1,0:T(8,128)(2,1)S(1)} %get-tuple-element.159), channel_id=1, source_target_pairs={{0,96},{32,0},{64,32},{96,64},{1,97},{33,1},{65,33},{97,65},{2,98}... | collective-permute-start | bytes 442376 | tf_op jit(solution)/shard_map/small_sum/ppermute | solution.py:472
  360.4 8.3 %collective-permute-start.50 = (bf16[64,1024]{1,0:T(8,128)(2,1)}, bf16[64,1024]{1,0:T(8,128)(2,1)S(1)}, u32[]{:S(2)}, u32[]{:S(2)}) collective-permute-start(bf16[64,1024]{1,0:T(8,128)(2,1)} %get-tuple-element.162), channel_id=1, source_target_pairs={{0,8},{4,12},{8,0},{12,4},{1,9},{5,13},{9,1},{13,5},{2,10},{6,14},... | collective-permute-start | bytes 393224 | tf_op jit(solution)/shard_map/small_sum/ppermute | solution.py:472
  362.1 8.3 %collective-permute-start.51 = (bf16[64,1024]{1,0:T(8,128)(2,1)}, bf16[64,1024]{1,0:T(8,128)(2,1)S(1)}, u32[]{:S(2)}, u32[]{:S(2)}) collective-permute-start(bf16[64,1024]{1,0:T(8,128)(2,1)} %get-tuple-element.164), channel_id=1, source_target_pairs={{0,4},{4,8},{8,12},{12,0},{1,5},{5,9},{9,13},{13,1},{2,6},{6,10},{... | collective-permute-start | bytes 393224 | tf_op jit(solution)/shard_map/small_sum/ppermute | solution.py:472
  371.4 17.8 %collective-permute-start.53 = (bf16[64,2048]{1,0:T(8,128)(2,1)S(1)}, bf16[64,2048]{1,0:T(8,128)(2,1)S(1)}, u32[]{:S(2)}, u32[]{:S(2)}) collective-permute-start(bf16[64,2048]{1,0:T(8,128)(2,1)S(1)} %pad_maximum_fusion.2), channel_id=1, source_target_pairs={{0,0},{1,16},{16,1},{17,17},{2,2},{3,18},{18,3},{19,19},{4,4},{5,2... | collective-permute-start | bytes 786440 | tf_op jit(solution)/shard_map/ppermute | solution.py:21
  374.7 9.2 %collective-permute-start.46 = (f32[7,16]{1,0:T(8,128)S(1)}, f32[7,16]{1,0:T(8,128)S(1)}, u32[]{:S(2)}, u32[]{:S(2)}) collective-permute-start(f32[7,16]{1,0:T(8,128)S(1)} %pad_maximum_fusion.3), channel_id=1, source_target_pairs={{0,0},{16,1},{2,2},{18,3},{1,16},{17,17},{3,18},{19,19},{4,4},{20,... | collective-permute-start | bytes 1352 | tf_op jit(solution)/shard_map/norm_sum/ppermute | solution.py:47
  375.3 9.3 %collective-permute-start.47 = (f32[4,16]{1,0:T(4,128)S(1)}, f32[4,16]{1,0:T(4,128)S(1)}, u32[]{:S(2)}, u32[]{:S(2)}) collective-permute-start(f32[4,16]{1,0:T(4,128)S(1)} %bitcast.93), channel_id=1, source_target_pairs={{16,0},{2,1},{18,2},{0,3},{17,16},{3,17},{19,18},{1,19},{20,4},{6,... | collective-permute-start | bytes 776 | tf_op jit(solution)/shard_map/norm_sum/ppermute | solution.py:47
  (65 other events, 509.7 us)
Sparse Core Ops, SparseCore 0:
  25.6 56.4 all-gather.2
  84.9 73.3 all-gather.4
  217.8 127.7 reduce-scatter.1

commit v3 on v2

--- a/solution.py
+++ b/solution.py
@@ -304,7 +304,7 @@
     out[:, n : n + m] = mul(c, d[...], TM).astype(BF)
 
 
-def outer(a, b, c, d, deps=(), tile=256):
+def outer(a, b, c, d, deps=(), tile=512):
     n, m = b.shape[1], d.shape[1]
     left = [pl.BlockSpec((ROWS, tile), lambda i: (0, i))] * 4
     whole = lambda w: pl.BlockSpec((512, w), lambda i: (0, 0))
@@ -340,26 +340,31 @@
     wide = theirs.shape[1]
     split = one[0].shape[-1]
     step = pl.program_id(0)
-    for begin, width, value in half_columns(a, b, (c0, c1, c2, c3), d, extra):
-        value = (value + theirs[:, begin : begin + width].astype(F32)).astype(BF)
-        for z in range(4):
-            at = lax.rem(z - place[2] + 4, 4)
-            rows = value[z * 64 : (z + 1) * 64]
-            for ref, (k, first, last) in zip(one, pieces_of(split)):
-                low, high = max(first, begin), min(last, begin + width)
-                if low < high:
-
-                    @pl.when(step == k)
-                    def _():
-                        ref[at, :, low - first : high - first] = rows[:, low - begin : high - begin]
-
-            for ref, (k, first, last) in zip(two, pieces_of(wide - split)):
-                low, high = max(first + split, begin), min(last + split, begin + width)
-                if low < high:
-
-                    @pl.when(at == k)
-                    def _():
-                        ref[0, :, low - split - first : high - split - first] = rows[:, low - begin : high - begin]
+    values = [
+        (begin, width, (value + theirs[:, begin : begin + width].astype(F32)).astype(BF))
+        for begin, width, value in half_columns(a, b, (c0, c1, c2, c3), d, extra)
+    ]
+
+    def store(refs, k, at, z, first_column, columns):
+        for ref, (block, first, last) in zip(refs, pieces_of(columns)):
+            for begin, width, value in values:
+                low, high = max(first + first_column, begin), min(last + first_column, begin + width)
+                if block == k and low < high:
+                    rows = value[z * 64 : (z + 1) * 64, low - begin : high - begin]
+                    ref[at, :, low - first_column - first : high - first_column - first] = rows
+
+    for here in range(4):
+
+        @pl.when(place[2] == here)
+        def _():
+            for z in range(4):
+                store(two, (z - here) % 4, 0, z, split, wide - split)
+            for k in range(4):
+
+                @pl.when(step == k)
+                def _():
+                    for z in range(4):
+                        store(one, k, (z - here) % 4, z, 0, split)
 
 
 def relay_kernel(*refs):

time: 406 us -> 405 us (level)
  transfers between devices with their start and end apart: 57 -> 57, of which waited for: 22 -> 22; matrix products, arithmetic and copies ran while one was open for 7% -> 7% of each run, Pallas kernels for 23% -> 22%
where the time goes in v3:
time: 405 us; the launch traced here: 399 us
  waiting for transfers between devices  127 us (31%)
  Pallas kernels  114 us (28%)
  starting transfers between devices  93.7 us (23%)
  local copies, waits for them, and re-layouts  37.9 us (9%)
  between operations  14.8 us (4%)
  other arithmetic  11.4 us (3%)
    pallas_call x15, Pallas kernels, call(): pl.pallas_call(lambda *refs: kernel(*refs[:n], *refs[n + m:]), name=kerne...  97.4 us
    ppermute x14, waiting for transfers between devices, shift(): lax.ppermute(v, ('yl', 'yh'), [(ring_index(y), ring_index((y + k) % 4)) f...  73.9 us
    ppermute x12, starting transfers between devices, spread(): return lax.ppermute(v, ('yl', 'yh', 'core'), spread_pairs(k))  28.8 us
    ppermute x14, starting transfers between devices, along(): return lax.ppermute(v, axis, [(i, (i + k) % 4) for i in range(4)])  23.5 us
    ppermute x14, starting transfers between devices, shift(): lax.ppermute(v, ('yl', 'yh'), [(ring_index(y), ring_index((y + k) % 4)) f...  23.1 us
    ppermute x12, waiting for transfers between devices, spread(): return lax.ppermute(v, ('yl', 'yh', 'core'), spread_pairs(k))  22.3 us
    unnamed x118, local copies, waits for them, and re-layouts  20.1 us
    pallas_call x2, Pallas kernels, outer_half(): pl.pallas_call(lambda *refs: kernel(*refs[:count], *refs[count + len(deps...  16.9 us
  transfers between devices with their start and end apart: 57, of which 22 were waited for; matrix products, arithmetic and copies ran while one was open for 7% of the time, Pallas kernels for 22%

profile of v3, /device:TPU:0, one launch (start us, length us, event | category | flops | bytes accessed | tf_op | source)
XLA Modules:
  0.0 398.9 jit_solution(9101578026527087210)
XLA Ops:
  14.0 5.3 %collective-permute-start.3 = (f32[8,16]{1,0:T(8,128)}, f32[8,16]{1,0:T(8,128)S(1)}, u32[]{:S(2)}, u32[]{:S(2)}) collective-permute-start(f32[8,16]{1,0:T(8,128)} %hold.6), channel_id=1, source_target_pairs={{0,16},{1,2},{2,18},{3,0},{16,17},{17,3},{18,19},{19,1},{4,20},{5,... | collective-permute-start | bytes 1544 | tf_op jit(solution)/shard_map/ppermute | solution.py:43
  19.3 2.9 collective-permute-start.4
  22.6 2.0 collective-permute-done.4.refs_4_
  28.7 12.2 %collective-permute-start.7 = (bf16[128,2048]{1,0:T(8,128)(2,1)S(1)}, bf16[128,2048]{1,0:T(8,128)(2,1)}, u32[]{:S(2)}, u32[]{:S(2)}) collective-permute-start(bf16[128,2048]{1,0:T(8,128)(2,1)S(1)} %normal_kernel.1.refs_6_), channel_id=1, source_target_pairs={{0,16},{1,2},{2,18},{3,0},{16,17},{17,3},{18,19},{19,1},{4,20},{5,... | collective-permute-start | bytes 1572872 | tf_op jit(solution)/shard_map/n_rows/ppermute | solution.py:43
  40.9 3.2 collective-permute-start.8
  47.9 19.1 %collective-permute-done.7.refs_1_.refs_4_ = bf16[128,2048]{1,0:T(8,128)(2,1)} collective-permute-done((bf16[128,2048]{1,0:T(8,128)(2,1)S(1)}, bf16[128,2048]{1,0:T(8,128)(2,1)}, u32[]{:S(2)}, u32[]{:S(2)}) %collective-permute-start.7) | collective-permute-done | bytes 524320 | tf_op jit(solution)/shard_map/n_rows/ppermute | solution.py:43
  69.6 1.8 multiply_sine_fusion
  71.5 2.1 concatenate.27.refs_11_.refs_10_
  73.6 2.2 concatenate.28.refs_12_.refs_11_
  77.8 4.3 %all-gather.3.cloned.1.call-done.refs_5_.refs_6_.refs_7_.refs_8_.refs_4_.refs_1_ = bf16[2048,2176]{1,0:T(8,128)(2,1)} async-done(((bf16[64,2176]{1,0:T(8,128)(2,1)}), bf16[2048,2176]{1,0:T(8,128)(2,1)}) %all-gather.3.cloned.1.call-update) | async-done | bytes 8912912 | tf_op jit(solution)/shard_map/all_gather | solution.py:537
  86.0 17.8 %attend_kernel.1 = (bf16[512,2048]{1,0:T(8,128)(2,1)}, bf16[512,512]{1,0:T(8,128)(2,1)}, bf16[512,512]{1,0:T(8,128)(2,1)}, bf16[512,512]{1,0:T(8,128)(2,1)}, f32...) custom-call(bf16[128,2048]{1,0:T(8,128)(2,1)} %copy-done.39, ...), custom_call_target="tpu_custom_call" | custom-call | tf_op jit(solution)/shard_map/attend_kernel/pallas_call | solution.py:74
  104.9 3.0 collective-permute-start.15
  109.9 11.5 %collective-permute-done.15.refs_3_ = bf16[128,2048]{1,0:T(8,128)(2,1)S(1)} collective-permute-done((bf16[128,2048]{1,0:T(8,128)(2,1)}, bf16[128,2048]{1,0:T(8,128)(2,1)S(1)}, u32[]{:S(2)}, u32[]{:S(2)}) %collective-permute-start.15) | collective-permute-done | bytes 524320 | tf_op jit(solution)/shard_map/attn_sum/ppermute | solution.py:29
  121.4 10.7 %collective-permute-done.16.refs_4_ = bf16[128,2048]{1,0:T(8,128)(2,1)S(1)} collective-permute-done((bf16[128,2048]{1,0:T(8,128)(2,1)}, bf16[128,2048]{1,0:T(8,128)(2,1)S(1)}, u32[]{:S(2)}, u32[]{:S(2)}) %collective-permute-start.16) | collective-permute-done | bytes 524320 | tf_op jit(solution)/shard_map/attn_sum/ppermute | solution.py:29
  135.5 2.7 collective-permute-start.19
  138.2 1.8 collective-permute-start.20
  140.0 9.1 %collective-permute-done.18.refs_1_ = bf16[128,2048]{1,0:T(8,128)(2,1)S(1)} collective-permute-done((bf16[128,2048]{1,0:T(8,128)(2,1)S(1)}, bf16[128,2048]{1,0:T(8,128)(2,1)S(1)}, u32[]{:S(2)}, u32[]{:S(2)}) %collective-permute-start.18) | collective-permute-done | bytes 524320 | tf_op jit(solution)/shard_map/second_rows/ppermute | solution.py:29
  149.1 12.2 %collective-permute-done.19.refs_2_ = bf16[128,2048]{1,0:T(8,128)(2,1)S(1)} collective-permute-done((bf16[128,2048]{1,0:T(8,128)(2,1)S(1)}, bf16[128,2048]{1,0:T(8,128)(2,1)S(1)}, u32[]{:S(2)}, u32[]{:S(2)}) %collective-permute-start.19) | collective-permute-done | bytes 524320 | tf_op jit(solution)/shard_map/second_rows/ppermute | solution.py:29
  162.1 22.3 %feed_kernel.1 = (bf16[512,1408]{1,0:T(8,128)(2,1)}, bf16[512,2816]{1,0:T(8,128)(2,1)}, f32[128,2048]{1,0:T(8,128)}, bf16[128,2048]{1,0:T(8,128)(2,1)}, bf16[128...) custom-call(bf16[128,2048]{1,0:T(8,128)(2,1)} %copy-done.15, bf16[128,2048]{1,0:T(8,128)(2,1)} %copy-done.44, ...), custom_call_target="tpu_custom_call" | custom-call | tf_op jit(solution)/shard_map/feed_kernel/pallas_call | solution.py:74
  184.5 2.1 collective-permute-start.21
  186.5 1.7 collective-permute-start.22
  189.2 15.1 %outer_kernel.1.refs_3_.refs_0_ = bf16[2048,4224]{1,0:T(8,128)(2,1)} custom-call(bf16[128,2048]{1,0:T(8,128)(2,1)} %copy-done.15, bf16[128,2048]{1,0:T(8,128)(2,1)} %copy-done.44, bf16[128,2048]{1,0:T(8,128)(2,1)} %copy-done.45, bf16[128,2048]{1,0:T(8,128)(2,1)} %collective-permute-done.20.refs_3_, bf16[512,2816]{1,0:T(8,128)(2,1)} %get-tuple-element.77.refs_4_, ...), custom_call_target="tpu_custom_call" | custom-call | tf_op jit(solution)/shard_map/outer_kernel/pallas_call | solution.py:74
  204.3 7.6 %term_kernel.2 = (bf16[128,2048]{1,0:T(8,128)(2,1)}, bf16[128,2048]{1,0:T(8,128)(2,1)}, bf16[256,2048]{1,0:T(8,128)(2,1)}) custom-call(bf16[512,1408]{1,0:T(8,128)(2,1)} %get-tuple-element.76.refs_9_.refs_0_, bf16[2048,4224]{1,0:T(8,128)(2,1)} %all-gather.5.cloned.1.call-done.refs_8_.refs_1_, s32[4]{0:T(128)} %get-tuple-element.157.refs_2_.refs_0_, ...), custom_call_target="tpu_custom_call" | custom-call | tf_op jit(solution)/shard_map/term_kernel/pallas_call | solution.py:74
  212.9 2.3 back_kernel.1
  218.1 3.9 collective-permute-start.25
  222.1 10.5 %collective-permute-done.24.refs_3_.refs_1_.refs_4_ = bf16[128,2048]{1,0:T(8,128)(2,1)S(1)} collective-permute-done((bf16[128,2048]{1,0:T(8,128)(2,1)S(1)}, bf16[128,2048]{1,0:T(8,128)(2,1)S(1)}, u32[]{:S(2)}, u32[]{:S(2)}) %collective-permute-start.24) | collective-permute-done | bytes 524320 | tf_op jit(solution)/shard_map/middle_rows/ppermute | solution.py:29
  232.6 11.3 %collective-permute-done.25.refs_4_.refs_2_.refs_5_ = bf16[128,2048]{1,0:T(8,128)(2,1)S(1)} collective-permute-done((bf16[128,2048]{1,0:T(8,128)(2,1)S(1)}, bf16[128,2048]{1,0:T(8,128)(2,1)S(1)}, u32[]{:S(2)}, u32[]{:S(2)}) %collective-permute-start.25) | collective-permute-done | bytes 524320 | tf_op jit(solution)/shard_map/middle_rows/ppermute | solution.py:29
  245.9 16.4 %attend_back_kernel.1 = (bf16[512,1536]{1,0:T(8,128)(2,1)}, f32[24,64]{1,0:T(8,128)}) custom-call(bf16[128,2048]{1,0:T(8,128)(2,1)} %copy-done, bf16[128,2048]{1,0:T(8,128)(2,1)} %copy-done.31, bf16[128,2048]{1,0:T(8,128)(2,1)} %copy-done.32, bf16[128,2048]{1,0:T(8,128)(2,1)} %copy-done.33, ...), custom_call_target="tpu_custom_call" | custom-call | tf_op jit(solution)/shard_map/attend_back_kernel/pallas_call | solution.py:74
  262.3 8.7 %term_kernel.3 = (bf16[128,2048]{1,0:T(8,128)(2,1)}, bf16[128,2048]{1,0:T(8,128)(2,1)}, bf16[256,2048]{1,0:T(8,128)(2,1)}, bf16[2048,128]{1,0:T(8,128)(2,1)}) custom-call(bf16[512,1536]{1,0:T(8,128)(2,1)} %get-tuple-element.96.refs_0_.refs_2_, bf16[2048,2176]{1,0:T(8,128)(2,1)} %all-gather.3.cloned.1.call-done.refs_5_.refs_6_.refs_7_.refs_8_.refs_4_.refs_1_, ...), custom_call_target="tpu_custom_call" | custom-call | tf_op jit(solution)/shard_map/term_kernel/pallas_call | solution.py:74
  273.0 7.4 %their_half_kernel.1 = bf16[1024,2176]{1,0:T(8,128)(2,1)} custom-call(s32[4]{0:T(128)} %get-tuple-element.156.refs_0_, bf16[512,2048]{1,0:T(8,128)(2,1)} %get-tuple-element.91.refs_1_, bf16[512,1536]{1,0:T(8,128)(2,1)} %get-tuple-element.96.refs_0_.refs_2_, bf16[128,2048]{1,0:T(8,128)(2,1)} %copy-done, bf16[128,2048]{1,0:T(8,128)(2,1)} %copy-done.31, ...), custom_call_target="tpu_custom_call" | custom-call | tf_op jit(solution)/shard_map/their_half_kernel/pallas_call | solution.py:399
  280.5 2.6 collective-permute-start.35
  283.1 5.2 %collective-permute-done.28.refs_9_ = bf16[1024,2176]{1,0:T(8,128)(2,1)} collective-permute-done((bf16[1024,2176]{1,0:T(8,128)(2,1)}, bf16[1024,2176]{1,0:T(8,128)(2,1)}, u32[]{:S(2)}, u32[]{:S(2)}) %collective-permute-start.28) | collective-permute-done | bytes 4456480 | tf_op jit(solution)/shard_map/ppermute | solution.py:513
  288.4 9.5 %own_half_kernel.1 = (bf16[4,64,1024]{2,1,0:T(8,128)(2,1)}, bf16[4,64,1024]{2,1,0:T(8,128)(2,1)}, bf16[4,64,512]{2,1,0:T(8,128)(2,1)}, bf16[4,64,512]{2,1,0:T(8,...) custom-call(s32[4]{0:T(128)} %get-tuple-element.157.refs_2_.refs_0_,, ...), custom_call_target="tpu_custom_call" | custom-call | tf_op jit(solution)/shard_map/own_half_kernel/pallas_call | solution.py:399
  299.0 8.5 %collective-permute-done.35.refs_2_ = bf16[256,2048]{1,0:T(8,128)(2,1)S(1)} collective-permute-done((bf16[256,2048]{1,0:T(8,128)(2,1)S(1)}, bf16[256,2048]{1,0:T(8,128)(2,1)S(1)}, u32[]{:S(2)}, u32[]{:S(2)}) %collective-permute-start.35) | collective-permute-done | bytes 1048608 | tf_op jit(solution)/shard_map/first_sum/ppermute | solution.py:29
  311.7 1.8 collective-permute-start.36
  315.0 1.7 collective-permute-start.30
  316.8 2.5 collective-permute-start.32
  319.3 3.3 collective-permute-done.29.refs_2_
  327.5 3.0 collective-permute-start.39
  331.6 2.7 collective-permute-start.41
  334.4 2.7 tokens_kernel.1
  337.1 2.1 collective-permute-done.33.refs_2_
  342.1 5.1 %collective-permute-done.38 = bf16[4,64,1024]{2,1,0:T(8,128)(2,1)} collective-permute-done((bf16[4,64,1024]{2,1,0:T(8,128)(2,1)}, bf16[4,64,1024]{2,1,0:T(8,128)(2,1)}, u32[]{:S(2)}, u32[]{:S(2)}) %collective-permute-start.38) | collective-permute-done | bytes 524320 | tf_op jit(solution)/shard_map/large_sum/ppermute | solution.py:477
  356.4 2.7 collective-permute-start.45
  362.8 2.1 collective-permute-start.52
  368.1 1.7 collective-permute-done.51
  374.7 7.4 %collective-permute-start.47 = (f32[4,16]{1,0:T(4,128)S(1)}, f32[4,16]{1,0:T(4,128)S(1)}, u32[]{:S(2)}, u32[]{:S(2)}) collective-permute-start(f32[4,16]{1,0:T(4,128)S(1)} %bitcast.93), channel_id=1, source_target_pairs={{16,0},{2,1},{18,2},{0,3},{17,16},{3,17},{19,18},{1,19},{20,4},{6,... | collective-permute-start | bytes 776 | tf_op jit(solution)/shard_map/norm_sum/ppermute | solution.py:47
  384.1 3.2 collective-permute-done.48
  (274 shorter events, 82.9 us)
Async XLA Ops:
  7.2 74.9 %all-gather.3.cloned.1.call-start = ((), (), s32[]{:S(2)}) async-start(), calls=%async_computation.1 | async-start | bytes 9191424 | tf_op jit(solution)/shard_map/all_gather | solution.py:537
  9.1 15.6 %collective-permute-start.1 = (bf16[64,2048]{1,0:T(8,128)(2,1)S(1)}, bf16[64,2048]{1,0:T(8,128)(2,1)S(1)}, u32[]{:S(2)}, u32[]{:S(2)}) collective-permute-start(bf16[64,2048]{1,0:T(8,128)(2,1)S(1)} %pad_maximum_fusion.1.refs_1_), channel_id=1, source_target_pairs={{0,0},{1,16},{16,1},{17,17},{2,2},{3,18},{18,3},{19,19},{4,4},{5,2... | collective-permute-start | bytes 786440 | tf_op jit(solution)/shard_map/ppermute | solution.py:21
  12.7 9.9 %collective-permute-start.2 = (f32[8,16]{1,0:T(8,128)}, f32[8,16]{1,0:T(8,128)S(1)}, u32[]{:S(2)}, u32[]{:S(2)}) collective-permute-start(f32[8,16]{1,0:T(8,128)} %hold.6), channel_id=1, source_target_pairs={{0,0},{1,16},{2,2},{3,18},{16,1},{17,17},{18,3},{19,19},{4,4},{5,2... | collective-permute-start | bytes 1544 | tf_op jit(solution)/shard_map/ppermute | solution.py:43
  14.0 8.6 %collective-permute-start.3 = (f32[8,16]{1,0:T(8,128)}, f32[8,16]{1,0:T(8,128)S(1)}, u32[]{:S(2)}, u32[]{:S(2)}) collective-permute-start(f32[8,16]{1,0:T(8,128)} %hold.6), channel_id=1, source_target_pairs={{0,16},{1,2},{2,18},{3,0},{16,17},{17,3},{18,19},{19,1},{4,20},{5,... | collective-permute-start | bytes 1544 | tf_op jit(solution)/shard_map/ppermute | solution.py:43
  25.5 135.9 %all-gather.5.cloned.1.call-start = ((), (), s32[]{:S(2)}) async-start(), calls=%async_computation.2 | async-start | bytes 17842176 | tf_op jit(solution)/shard_map/all_gather | solution.py:545
  28.0 324.1 %reduce-scatter.2.cloned.1.call-start = ((), (), s32[]{:S(2)}) async-start(), calls=%async_computation.3 | async-start | bytes 17842176 | tf_op jit(solution)/shard_map/reduce_scatter | solution.py:610
  28.0 18.2 %collective-permute-start.6 = (bf16[128,2048]{1,0:T(8,128)(2,1)S(1)}, bf16[128,2048]{1,0:T(8,128)(2,1)S(1)}, u32[]{:S(2)}, u32[]{:S(2)}) collective-permute-start(bf16[128,2048]{1,0:T(8,128)(2,1)S(1)} %normal_kernel.1.refs_6_), channel_id=1, source_target_pairs={{0,0},{1,16},{2,2},{3,18},{16,1},{17,17},{18,3},{19,19},{4,4},{5,2... | collective-permute-start | bytes 1572872 | tf_op jit(solution)/shard_map/n_rows/ppermute | solution.py:43
  28.7 38.2 %collective-permute-start.7 = (bf16[128,2048]{1,0:T(8,128)(2,1)S(1)}, bf16[128,2048]{1,0:T(8,128)(2,1)}, u32[]{:S(2)}, u32[]{:S(2)}) collective-permute-start(bf16[128,2048]{1,0:T(8,128)(2,1)S(1)} %normal_kernel.1.refs_6_), channel_id=1, source_target_pairs={{0,16},{1,2},{2,18},{3,0},{16,17},{17,3},{18,19},{19,1},{4,20},{5,... | collective-permute-start | bytes 1572872 | tf_op jit(solution)/shard_map/n_rows/ppermute | solution.py:43
  40.9 27.3 %collective-permute-start.8 = (bf16[128,2048]{1,0:T(8,128)(2,1)S(1)}, bf16[128,2048]{1,0:T(8,128)(2,1)}, u32[]{:S(2)}, u32[]{:S(2)}) collective-permute-start(bf16[128,2048]{1,0:T(8,128)(2,1)S(1)} %normal_kernel.1.refs_6_), channel_id=1, source_target_pairs={{0,2},{1,18},{2,0},{3,16},{16,3},{17,19},{18,1},{19,17},{4,6},{5,2... | collective-permute-start | bytes 1572872 | tf_op jit(solution)/shard_map/n_rows/ppermute | solution.py:43
  44.1 24.5 %collective-permute-start.9 = (bf16[128,2048]{1,0:T(8,128)(2,1)S(1)}, bf16[128,2048]{1,0:T(8,128)(2,1)}, u32[]{:S(2)}, u32[]{:S(2)}) collective-permute-start(bf16[128,2048]{1,0:T(8,128)(2,1)S(1)} %normal_kernel.1.refs_6_), channel_id=1, source_target_pairs={{0,18},{1,0},{2,16},{3,2},{16,19},{17,1},{18,17},{19,3},{4,22},{5,... | collective-permute-start | bytes 1572872 | tf_op jit(solution)/shard_map/n_rows/ppermute | solution.py:43
  44.1 41.1 %collective-permute-start = (bf16[128,2048]{1,0:T(8,128)(2,1)S(1)}, bf16[128,2048]{1,0:T(8,128)(2,1)S(1)}, u32[]{:S(2)}, u32[]{:S(2)}) collective-permute-start(bf16[128,2048]{1,0:T(8,128)(2,1)S(1)} %copy-done.24), channel_id=1, source_target_pairs={{0,0},{1,16},{16,1},{17,17},{2,2},{3,18},{18,3},{19,19},{4,4},{5,2... | collective-permute-start | bytes 1572872 | tf_op jit(solution)/shard_map/ppermute | solution.py:21
  46.2 57.6 %collective-permute-start.11 = (bf16[128,2048]{1,0:T(8,128)(2,1)}, bf16[128,2048]{1,0:T(8,128)(2,1)S(1)}, u32[]{:S(2)}, u32[]{:S(2)}) collective-permute-start(bf16[128,2048]{1,0:T(8,128)(2,1)} %param.19), channel_id=1, source_target_pairs={{0,0},{1,16},{2,2},{3,18},{16,1},{17,17},{18,3},{19,19},{4,4},{5,2... | collective-permute-start | bytes 1572872 | tf_op jit(solution)/shard_map/grad_rows/ppermute | solution.py:43
  67.0 36.8 %collective-permute-start.12 = (bf16[128,2048]{1,0:T(8,128)(2,1)}, bf16[128,2048]{1,0:T(8,128)(2,1)S(1)}, u32[]{:S(2)}, u32[]{:S(2)}) collective-permute-start(bf16[128,2048]{1,0:T(8,128)(2,1)} %param.19), channel_id=1, source_target_pairs={{0,16},{1,2},{2,18},{3,0},{16,17},{17,3},{18,19},{19,1},{4,20},{5,... | collective-permute-start | bytes 1572872 | tf_op jit(solution)/shard_map/grad_rows/ppermute | solution.py:43
  68.1 35.7 %collective-permute-start.13 = (bf16[128,2048]{1,0:T(8,128)(2,1)}, bf16[128,2048]{1,0:T(8,128)(2,1)S(1)}, u32[]{:S(2)}, u32[]{:S(2)}) collective-permute-start(bf16[128,2048]{1,0:T(8,128)(2,1)} %param.19), channel_id=1, source_target_pairs={{0,2},{1,18},{2,0},{3,16},{16,3},{17,19},{18,1},{19,17},{4,6},{5,2... | collective-permute-start | bytes 1572872 | tf_op jit(solution)/shard_map/grad_rows/ppermute | solution.py:43
  68.6 35.2 %collective-permute-start.14 = (bf16[128,2048]{1,0:T(8,128)(2,1)}, bf16[128,2048]{1,0:T(8,128)(2,1)}, u32[]{:S(2)}, u32[]{:S(2)}) collective-permute-start(bf16[128,2048]{1,0:T(8,128)(2,1)} %param.19), channel_id=1, source_target_pairs={{0,18},{1,0},{2,16},{3,2},{16,19},{17,1},{18,17},{19,3},{4,22},{5,... | collective-permute-start | bytes 1572872 | tf_op jit(solution)/shard_map/grad_rows/ppermute | solution.py:43
  104.9 16.5 %collective-permute-start.15 = (bf16[128,2048]{1,0:T(8,128)(2,1)}, bf16[128,2048]{1,0:T(8,128)(2,1)S(1)}, u32[]{:S(2)}, u32[]{:S(2)}) collective-permute-start(bf16[128,2048]{1,0:T(8,128)(2,1)} %get-tuple-element.71), channel_id=1, source_target_pairs={{0,2},{16,18},{2,0},{18,16},{1,3},{17,19},{3,1},{19,17},{4,6},{20,... | collective-permute-start | bytes 1572872 | tf_op jit(solution)/shard_map/attn_sum/ppermute | solution.py:29
  107.9 24.2 %collective-permute-start.16 = (bf16[128,2048]{1,0:T(8,128)(2,1)}, bf16[128,2048]{1,0:T(8,128)(2,1)S(1)}, u32[]{:S(2)}, u32[]{:S(2)}) collective-permute-start(bf16[128,2048]{1,0:T(8,128)(2,1)} %get-tuple-element.72), channel_id=1, source_target_pairs={{0,18},{16,0},{2,16},{18,2},{1,19},{17,1},{3,17},{19,3},{4,22},{20... | collective-permute-start | bytes 1572872 | tf_op jit(solution)/shard_map/attn_sum/ppermute | solution.py:29
  109.1 23.0 %collective-permute-start.17 = (bf16[128,2048]{1,0:T(8,128)(2,1)}, bf16[128,2048]{1,0:T(8,128)(2,1)S(1)}, u32[]{:S(2)}, u32[]{:S(2)}) collective-permute-start(bf16[128,2048]{1,0:T(8,128)(2,1)} %get-tuple-element.73), channel_id=1, source_target_pairs={{0,16},{16,2},{2,18},{18,0},{1,17},{17,3},{3,19},{19,1},{4,20},{20... | collective-permute-start | bytes 1572872 | tf_op jit(solution)/shard_map/attn_sum/ppermute | solution.py:29
  134.0 15.1 %collective-permute-start.18 = (bf16[128,2048]{1,0:T(8,128)(2,1)S(1)}, bf16[128,2048]{1,0:T(8,128)(2,1)S(1)}, u32[]{:S(2)}, u32[]{:S(2)}) collective-permute-start(bf16[128,2048]{1,0:T(8,128)(2,1)S(1)} %get-tuple-element.75.refs_0_), channel_id=1, source_target_pairs={{0,16},{16,2},{2,18},{18,0},{1,17},{17,3},{3,19},{19,1},{4,20},{20... | collective-permute-start | bytes 1572872 | tf_op jit(solution)/shard_map/second_rows/ppermute | solution.py:29
  135.5 25.8 %collective-permute-start.19 = (bf16[128,2048]{1,0:T(8,128)(2,1)S(1)}, bf16[128,2048]{1,0:T(8,128)(2,1)S(1)}, u32[]{:S(2)}, u32[]{:S(2)}) collective-permute-start(bf16[128,2048]{1,0:T(8,128)(2,1)S(1)} %get-tuple-element.75.refs_0_), channel_id=1, source_target_pairs={{0,2},{16,18},{2,0},{18,16},{1,3},{17,19},{3,1},{19,17},{4,6},{20,... | collective-permute-start | bytes 1572872 | tf_op jit(solution)/shard_map/second_rows/ppermute | solution.py:29
  138.2 23.2 %collective-permute-start.20 = (bf16[128,2048]{1,0:T(8,128)(2,1)S(1)}, bf16[128,2048]{1,0:T(8,128)(2,1)}, u32[]{:S(2)}, u32[]{:S(2)}) collective-permute-start(bf16[128,2048]{1,0:T(8,128)(2,1)S(1)} %get-tuple-element.75.refs_0_), channel_id=1, source_target_pairs={{0,18},{16,0},{2,16},{18,2},{1,19},{17,1},{3,17},{19,3},{4,22},{20... | collective-permute-start | bytes 1572872 | tf_op jit(solution)/shard_map/second_rows/ppermute | solution.py:29
  184.5 27.4 %collective-permute-start.21 = (bf16[128,2048]{1,0:T(8,128)(2,1)}, bf16[128,2048]{1,0:T(8,128)(2,1)S(1)}, u32[]{:S(2)}, u32[]{:S(2)}) collective-permute-start(bf16[128,2048]{1,0:T(8,128)(2,1)} %get-tuple-element.82), channel_id=1, source_target_pairs={{0,2},{16,18},{2,0},{18,16},{1,3},{17,19},{3,1},{19,17},{4,6},{20,... | collective-permute-start | bytes 1572872 | tf_op jit(solution)/shard_map/second_sum/ppermute | solution.py:29
  186.5 25.3 %collective-permute-start.22 = (bf16[128,2048]{1,0:T(8,128)(2,1)}, bf16[128,2048]{1,0:T(8,128)(2,1)}, u32[]{:S(2)}, u32[]{:S(2)}) collective-permute-start(bf16[128,2048]{1,0:T(8,128)(2,1)} %get-tuple-element.83), channel_id=1, source_target_pairs={{0,18},{16,0},{2,16},{18,2},{1,19},{17,1},{3,17},{19,3},{4,22},{20... | collective-permute-start | bytes 1572872 | tf_op jit(solution)/shard_map/second_sum/ppermute | solution.py:29
  188.3 23.6 %collective-permute-start.23 = (bf16[128,2048]{1,0:T(8,128)(2,1)}, bf16[128,2048]{1,0:T(8,128)(2,1)}, u32[]{:S(2)}, u32[]{:S(2)}) collective-permute-start(bf16[128,2048]{1,0:T(8,128)(2,1)} %get-tuple-element.84), channel_id=1, source_target_pairs={{0,16},{16,2},{2,18},{18,0},{1,17},{17,3},{3,19},{19,1},{4,20},{20... | collective-permute-start | bytes 1572872 | tf_op jit(solution)/shard_map/second_sum/ppermute | solution.py:29
  217.7 14.9 %collective-permute-start.24 = (bf16[128,2048]{1,0:T(8,128)(2,1)S(1)}, bf16[128,2048]{1,0:T(8,128)(2,1)S(1)}, u32[]{:S(2)}, u32[]{:S(2)}) collective-permute-start(bf16[128,2048]{1,0:T(8,128)(2,1)S(1)} %copy-done.1), channel_id=1, source_target_pairs={{0,16},{16,2},{2,18},{18,0},{1,17},{17,3},{3,19},{19,1},{4,20},{20... | collective-permute-start | bytes 1572872 | tf_op jit(solution)/shard_map/middle_rows/ppermute | solution.py:29
  218.1 25.8 %collective-permute-start.25 = (bf16[128,2048]{1,0:T(8,128)(2,1)S(1)}, bf16[128,2048]{1,0:T(8,128)(2,1)S(1)}, u32[]{:S(2)}, u32[]{:S(2)}) collective-permute-start(bf16[128,2048]{1,0:T(8,128)(2,1)S(1)} %copy-done.1), channel_id=1, source_target_pairs={{0,2},{16,18},{2,0},{18,16},{1,3},{17,19},{3,1},{19,17},{4,6},{20,... | collective-permute-start | bytes 1572872 | tf_op jit(solution)/shard_map/middle_rows/ppermute | solution.py:29
  222.0 21.9 %collective-permute-start.26 = (bf16[128,2048]{1,0:T(8,128)(2,1)S(1)}, bf16[128,2048]{1,0:T(8,128)(2,1)S(1)}, u32[]{:S(2)}, u32[]{:S(2)}) collective-permute-start(bf16[128,2048]{1,0:T(8,128)(2,1)S(1)} %copy-done.1), channel_id=1, source_target_pairs={{0,18},{16,0},{2,16},{18,2},{1,19},{17,1},{3,17},{19,3},{4,22},{20... | collective-permute-start | bytes 1572872 | tf_op jit(solution)/shard_map/middle_rows/ppermute | solution.py:29
  244.9 26.0 %collective-permute-start.27 = (bf16[256,2048]{1,0:T(8,128)(2,1)}, bf16[256,2048]{1,0:T(8,128)(2,1)S(1)}, u32[]{:S(2)}, u32[]{:S(2)}) collective-permute-start(bf16[256,2048]{1,0:T(8,128)(2,1)} %get-tuple-element.88), channel_id=1, source_target_pairs={{0,2},{16,18},{2,0},{18,16},{1,3},{17,19},{3,1},{19,17},{4,6},{20,... | collective-permute-start | bytes 3145736 | tf_op jit(solution)/shard_map/out_sum/ppermute | solution.py:29
  280.5 27.1 %collective-permute-start.35 = (bf16[256,2048]{1,0:T(8,128)(2,1)S(1)}, bf16[256,2048]{1,0:T(8,128)(2,1)S(1)}, u32[]{:S(2)}, u32[]{:S(2)}) collective-permute-start(bf16[256,2048]{1,0:T(8,128)(2,1)S(1)} %copy-done.54), channel_id=1, source_target_pairs={{0,2},{16,18},{2,0},{18,16},{1,3},{17,19},{3,1},{19,17},{4,6},{20,... | collective-permute-start | bytes 3145736 | tf_op jit(solution)/shard_map/first_sum/ppermute | solution.py:29
  297.9 26.1 %collective-permute-start.31 = (bf16[4,64,640]{2,1,0:T(8,128)(2,1)}, bf16[4,64,640]{2,1,0:T(8,128)(2,1)S(1)}, u32[]{:S(2)}, u32[]{:S(2)}) collective-permute-start(bf16[4,64,640]{2,1,0:T(8,128)(2,1)} %get-tuple-element.107), channel_id=1, source_target_pairs={{0,4},{4,8},{8,12},{12,0},{1,5},{5,9},{9,13},{13,1},{2,6},{6,10},{... | collective-permute-start | bytes 983048 | tf_op jit(solution)/shard_map/large_sum/ppermute | solution.py:477
  311.7 19.9 %collective-permute-start.36 = (bf16[128,2048]{1,0:T(8,128)(2,1)}, bf16[128,2048]{1,0:T(8,128)(2,1)}, u32[]{:S(2)}, u32[]{:S(2)}) collective-permute-start(bf16[128,2048]{1,0:T(8,128)(2,1)} %get-tuple-element.117), channel_id=1, source_target_pairs={{0,16},{16,0},{1,17},{17,1},{2,18},{18,2},{3,19},{19,3},{4,20},{20... | collective-permute-start | bytes 1572872 | tf_op jit(solution)/shard_map/first_sum_too/ppermute | solution.py:473
  313.5 9.1 %collective-permute-start.29 = (bf16[4,64,512]{2,1,0:T(8,128)(2,1)}, bf16[4,64,512]{2,1,0:T(8,128)(2,1)S(1)}, u32[]{:S(2)}, u32[]{:S(2)}) collective-permute-start(bf16[4,64,512]{2,1,0:T(8,128)(2,1)} %get-tuple-element.103), channel_id=1, source_target_pairs={{0,32},{32,64},{64,96},{96,0},{1,33},{33,65},{65,97},{97,1},{2,34}... | collective-permute-start | bytes 786440 | tf_op jit(solution)/shard_map/large_sum/ppermute | solution.py:477
  327.0 12.1 %collective-permute-start.33 = (bf16[128,2048]{1,0:T(8,128)(2,1)}, bf16[128,2048]{1,0:T(8,128)(2,1)}, u32[]{:S(2)}, u32[]{:S(2)}) collective-permute-start(bf16[128,2048]{1,0:T(8,128)(2,1)} %get-tuple-element.111), channel_id=1, source_target_pairs={{0,16},{16,0},{1,17},{17,1},{2,18},{18,2},{3,19},{19,3},{4,20},{20... | collective-permute-start | bytes 1572872 | tf_op jit(solution)/shard_map/out_sum_too/ppermute | solution.py:473
  327.2 20.0 %collective-permute-start.38 = (bf16[4,64,1024]{2,1,0:T(8,128)(2,1)}, bf16[4,64,1024]{2,1,0:T(8,128)(2,1)}, u32[]{:S(2)}, u32[]{:S(2)}) collective-permute-start(bf16[4,64,1024]{2,1,0:T(8,128)(2,1)} %copy-done.25), channel_id=1, source_target_pairs={{0,32},{32,64},{64,96},{96,0},{1,33},{33,65},{65,97},{97,1},{2,34}... | collective-permute-start | bytes 1572872 | tf_op jit(solution)/shard_map/large_sum/ppermute | solution.py:477
  327.5 20.4 %collective-permute-start.39 = (bf16[4,64,1024]{2,1,0:T(8,128)(2,1)}, bf16[4,64,1024]{2,1,0:T(8,128)(2,1)}, u32[]{:S(2)}, u32[]{:S(2)}) collective-permute-start(bf16[4,64,1024]{2,1,0:T(8,128)(2,1)} %copy-done.30), channel_id=1, source_target_pairs={{0,96},{32,0},{64,32},{96,64},{1,97},{33,1},{65,33},{97,65},{2,98}... | collective-permute-start | bytes 1572872 | tf_op jit(solution)/shard_map/large_sum/ppermute | solution.py:477
  330.4 20.1 %collective-permute-start.40 = (bf16[4,64,1152]{2,1,0:T(8,128)(2,1)}, bf16[4,64,1152]{2,1,0:T(8,128)(2,1)}, u32[]{:S(2)}, u32[]{:S(2)}) collective-permute-start(bf16[4,64,1152]{2,1,0:T(8,128)(2,1)} %copy-done.29), channel_id=1, source_target_pairs={{0,4},{4,8},{8,12},{12,0},{1,5},{5,9},{9,13},{13,1},{2,6},{6,10},{... | collective-permute-start | bytes 1769480 | tf_op jit(solution)/shard_map/large_sum/ppermute | solution.py:477
  331.6 19.0 %collective-permute-start.41 = (bf16[4,64,1152]{2,1,0:T(8,128)(2,1)}, bf16[4,64,1152]{2,1,0:T(8,128)(2,1)}, u32[]{:S(2)}, u32[]{:S(2)}) collective-permute-start(bf16[4,64,1152]{2,1,0:T(8,128)(2,1)} %copy-done.28), channel_id=1, source_target_pairs={{0,12},{4,0},{8,4},{12,8},{1,13},{5,1},{9,5},{13,9},{2,14},{6,2},{... | collective-permute-start | bytes 1769480 | tf_op jit(solution)/shard_map/large_sum/ppermute | solution.py:477
  339.1 17.2 %collective-permute-start.37 = (bf16[128,2048]{1,0:T(8,128)(2,1)}, bf16[128,2048]{1,0:T(8,128)(2,1)S(1)}, u32[]{:S(2)}, u32[]{:S(2)}) collective-permute-start(bf16[128,2048]{1,0:T(8,128)(2,1)} %tokens_kernel.1), channel_id=1, source_target_pairs={{0,0},{1,16},{16,1},{17,17},{2,2},{3,18},{18,3},{19,19},{4,4},{5,2... | collective-permute-start | bytes 1572872 | tf_op jit(solution)/shard_map/ppermute | solution.py:21
  347.2 12.6 %collective-permute-start.34 = (bf16[128,2048]{1,0:T(8,128)(2,1)S(1)}, bf16[128,2048]{1,0:T(8,128)(2,1)S(1)}, u32[]{:S(2)}, u32[]{:S(2)}) collective-permute-start(bf16[128,2048]{1,0:T(8,128)(2,1)S(1)} %last_kernel.1), channel_id=1, source_target_pairs={{0,0},{1,16},{16,1},{17,17},{2,2},{3,18},{18,3},{19,19},{4,4},{5,2... | collective-permute-start | bytes 1572872 | tf_op jit(solution)/shard_map/ppermute | solution.py:21
  352.1 9.4 %collective-permute-start.42 = (bf16[64,4224]{1,0:T(8,128)(2,1)}, bf16[64,4224]{1,0:T(8,128)(2,1)S(1)}, u32[]{:S(2)}, u32[]{:S(2)}) collective-permute-start(bf16[64,4224]{1,0:T(8,128)(2,1)} %reduce-scatter.2.cloned.1.call-done), channel_id=1, source_target_pairs={{0,0},{1,16},{16,1},{17,17},{2,2},{3,18},{18,3},{19,19},{4,4},{5,2... | collective-permute-start | bytes 1622024 | tf_op jit(solution)/shard_map/ppermute | solution.py:21
  354.5 8.2 %collective-permute-start.43 = (bf16[64,1152]{1,0:T(8,128)(2,1)}, bf16[64,1152]{1,0:T(8,128)(2,1)S(1)}, u32[]{:S(2)}, u32[]{:S(2)}) collective-permute-start(bf16[64,1152]{1,0:T(8,128)(2,1)} %get-tuple-element.161), channel_id=1, source_target_pairs={{0,64},{32,96},{64,0},{96,32},{1,65},{33,97},{65,1},{97,33},{2,66}... | collective-permute-start | bytes 442376 | tf_op jit(solution)/shard_map/small_sum/ppermute | solution.py:477
  355.8 10.3 %collective-permute-start.44 = (bf16[64,1152]{1,0:T(8,128)(2,1)S(1)}, bf16[64,1152]{1,0:T(8,128)(2,1)S(1)}, u32[]{:S(2)}, u32[]{:S(2)}) collective-permute-start(bf16[64,1152]{1,0:T(8,128)(2,1)S(1)} %get-tuple-element.160), channel_id=1, source_target_pairs={{0,32},{32,64},{64,96},{96,0},{1,33},{33,65},{65,97},{97,1},{2,34}... | collective-permute-start | bytes 442376 | tf_op jit(solution)/shard_map/small_sum/ppermute | solution.py:477
  356.4 9.7 %collective-permute-start.45 = (bf16[64,1152]{1,0:T(8,128)(2,1)S(1)}, bf16[64,1152]{1,0:T(8,128)(2,1)S(1)}, u32[]{:S(2)}, u32[]{:S(2)}) collective-permute-start(bf16[64,1152]{1,0:T(8,128)(2,1)S(1)} %get-tuple-element.159), channel_id=1, source_target_pairs={{0,96},{32,0},{64,32},{96,64},{1,97},{33,1},{65,33},{97,65},{2,98}... | collective-permute-start | bytes 442376 | tf_op jit(solution)/shard_map/small_sum/ppermute | solution.py:477
  359.8 8.3 %collective-permute-start.50 = (bf16[64,1024]{1,0:T(8,128)(2,1)}, bf16[64,1024]{1,0:T(8,128)(2,1)S(1)}, u32[]{:S(2)}, u32[]{:S(2)}) collective-permute-start(bf16[64,1024]{1,0:T(8,128)(2,1)} %get-tuple-element.162), channel_id=1, source_target_pairs={{0,8},{4,12},{8,0},{12,4},{1,9},{5,13},{9,1},{13,5},{2,10},{6,14},... | collective-permute-start | bytes 393224 | tf_op jit(solution)/shard_map/small_sum/ppermute | solution.py:477
  361.5 8.3 %collective-permute-start.51 = (bf16[64,1024]{1,0:T(8,128)(2,1)}, bf16[64,1024]{1,0:T(8,128)(2,1)S(1)}, u32[]{:S(2)}, u32[]{:S(2)}) collective-permute-start(bf16[64,1024]{1,0:T(8,128)(2,1)} %get-tuple-element.164), channel_id=1, source_target_pairs={{0,4},{4,8},{8,12},{12,0},{1,5},{5,9},{9,13},{13,1},{2,6},{6,10},{... | collective-permute-start | bytes 393224 | tf_op jit(solution)/shard_map/small_sum/ppermute | solution.py:477
  370.8 17.8 %collective-permute-start.53 = (bf16[64,2048]{1,0:T(8,128)(2,1)S(1)}, bf16[64,2048]{1,0:T(8,128)(2,1)S(1)}, u32[]{:S(2)}, u32[]{:S(2)}) collective-permute-start(bf16[64,2048]{1,0:T(8,128)(2,1)S(1)} %pad_maximum_fusion.2), channel_id=1, source_target_pairs={{0,0},{1,16},{16,1},{17,17},{2,2},{3,18},{18,3},{19,19},{4,4},{5,2... | collective-permute-start | bytes 786440 | tf_op jit(solution)/shard_map/ppermute | solution.py:21
  374.1 9.2 %collective-permute-start.46 = (f32[7,16]{1,0:T(8,128)S(1)}, f32[7,16]{1,0:T(8,128)S(1)}, u32[]{:S(2)}, u32[]{:S(2)}) collective-permute-start(f32[7,16]{1,0:T(8,128)S(1)} %pad_maximum_fusion.3), channel_id=1, source_target_pairs={{0,0},{16,1},{2,2},{18,3},{1,16},{17,17},{3,18},{19,19},{4,4},{20,... | collective-permute-start | bytes 1352 | tf_op jit(solution)/shard_map/norm_sum/ppermute | solution.py:47
  374.7 9.3 %collective-permute-start.47 = (f32[4,16]{1,0:T(4,128)S(1)}, f32[4,16]{1,0:T(4,128)S(1)}, u32[]{:S(2)}, u32[]{:S(2)}) collective-permute-start(f32[4,16]{1,0:T(4,128)S(1)} %bitcast.93), channel_id=1, source_target_pairs={{16,0},{2,1},{18,2},{0,3},{17,16},{3,17},{19,18},{1,19},{20,4},{6,... | collective-permute-start | bytes 776 | tf_op jit(solution)/shard_map/norm_sum/ppermute | solution.py:47
  (65 other events, 506.5 us)
Sparse Core Ops, SparseCore 0:
  25.6 56.4 all-gather.2
  84.9 73.3 all-gather.4
  216.8 128.3 reduce-scatter.1
